TPU v7x, 256 devices: a whole 4x4x8 slice. The times are simulated.
256 devices in a mesh: dp: 32 (over y_hi, z, core), ctx: 8 (over y_lo, x).
Axes of the slice: x: 4, y: 4 (y_hi: 2, y_lo: 2; y = y_hi * 2 + y_lo), z: 8, core: 2. Of those that a mesh axis runs over, the one named last changes fastest.
Arguments:
- inputs: bfloat16 [64, 512, 1024], P('dp', 'ctx'), may hold values from -8 to 8
- frames: int32 [64], P('dp'), may hold values from 64 to 512, as said below
- gain_first: float32 [1024], replicated, may hold values from 0.25 to 1.75
- w_first: bfloat16 [1024, 2048], P('dp'), may hold values from -0.1875 to 0.1875
- depth_kernel: float32 [31, 1024], replicated, may hold values from -1 to 1
- gain_second: float32 [1024], replicated, may hold values from 0.25 to 1.75
- w_second: bfloat16 [1024, 1024], P('dp'), may hold values from -0.1875 to 0.1875
- gain_attn: float32 [1024], replicated, may hold values from 0.25 to 1.75
- w_qkv: bfloat16 [1024, 3072], P('dp'), may hold values from -2.25 to 2.25
- w_proj: bfloat16 [1024, 1024], P('dp'), may hold values from -2.5 to 2.5
- grad_out: bfloat16 [64, 512, 1024], P('dp', 'ctx'), may hold values from -6 to 6
Outputs:
- result: bfloat16 [64, 512, 1024], P('dp', 'ctx')
- grad_in: bfloat16 [64, 512, 1024], P('dp', 'ctx')
- grad_first: float32 [1024, 2048], P('dp')
- grad_kernel: float32 [31, 1024], replicated
Inputs may be any that keep to these rules, and one draw needn't show every extreme that they name: Recording b has frames[b] real frames at the start and padding after them; some recording is full.
All inputs are finite; a program needn't handle non-finite values.
Results may differ from a plain program's by a relative error of at most 0.025.
Values may be sent and summed in bfloat16 or wider, within the bound.
No kernel may reach another device: no remote copies, remote signals or barrier semaphores. Data moves between devices by JAX's collectives and lax.ppermute only.
A program may use at most 128 MiB of HBM per device.

v0:
```python
import jax
import jax.numpy as jnp
from jax import lax
from jax.sharding import PartitionSpec as P

HEADS = 16


EPSILON = 1e-05


def extended(block, sides, width):
    for axis, dim in sides:
        count = lax.axis_size(axis)
        forward = [(i, i + 1) for i in range(count - 1)]
        backward = [(target, source) for source, target in forward]
        low = lax.ppermute(
            lax.slice_in_dim(block, block.shape[dim] - width, None, axis=dim), axis, forward
        )
        high = lax.ppermute(lax.slice_in_dim(block, 0, width, axis=dim), axis, backward)
        block = jnp.concatenate([low, block, high], axis=dim)
    return block


def normalize(values, gain_vec):
    centre = values - jnp.mean(values, -1, keepdims=True)
    spread = jnp.mean(centre * centre, -1, keepdims=True)
    return centre * lax.rsqrt(spread + EPSILON) * gain_vec


def swish_norm(values, gain_vec):
    normal_part = normalize(values, gain_vec)
    return normal_part * jax.nn.sigmoid(normal_part)


def local(
    inputs,
    frames,
    gain_first,
    w_first,
    depth_kernel,
    gain_second,
    w_second,
    gain_attn,
    w_qkv,
    w_proj,
    grad_out,
):
    records, local_len, model_dim = inputs.shape
    kernel_len = depth_kernel.shape[0]
    reach = (kernel_len - 1) // 2
    head_count = HEADS
    head_dim = model_dim // head_count
    offset = lax.axis_index("ctx") * local_len
    positions = offset + jnp.arange(local_len, dtype=jnp.int32)
    present = (positions[None, :] < frames[:, None]).astype(jnp.float32)[:, :, None]
    present_rows = present.reshape(-1, 1)
    full_first = lax.all_gather(w_first, "dp", axis=0, tiled=True)
    full_second = lax.all_gather(w_second, "dp", axis=0, tiled=True)
    full_qkv = lax.all_gather(w_qkv, "dp", axis=0, tiled=True)
    full_proj = lax.all_gather(w_proj, "dp", axis=0, tiled=True)
    flat_in = inputs.reshape(-1, model_dim).astype(jnp.float32)
    normed = normalize(flat_in, gain_first).astype(jnp.bfloat16)
    hidden = jnp.dot(normed, full_first, preferred_element_type=jnp.float32)
    linear = hidden[:, :model_dim]
    gating = hidden[:, model_dim:]
    gated = (present_rows * linear * jax.nn.sigmoid(gating)).astype(jnp.bfloat16)
    gated = gated.reshape(records, local_len, model_dim)
    gated_pad = extended(gated, (("ctx", 1),), reach)
    gated_wide = gated_pad.astype(jnp.float32)
    convolved = jnp.zeros((records, local_len, model_dim), jnp.float32)
    for tap_index in range(kernel_len):
        convolved = (
            convolved + depth_kernel[tap_index] * gated_wide[:, tap_index : tap_index + local_len]
        )
    swished, pull_back = jax.vjp(
        lambda v: swish_norm(v, gain_second), convolved.reshape(-1, model_dim)
    )
    residual = (
        flat_in
        + jnp.dot(swished.astype(jnp.bfloat16), full_second, preferred_element_type=jnp.float32)
    ).astype(jnp.bfloat16)
    attn_in = normalize(residual.astype(jnp.float32), gain_attn).astype(jnp.bfloat16)
    packed = jnp.dot(attn_in, full_qkv, preferred_element_type=jnp.float32).astype(jnp.bfloat16)
    packed = packed.reshape(records, local_len, 3, model_dim)
    scaling = head_dim ** (-0.5)
    query_heads = jnp.transpose(
        packed[:, :, 0].reshape(records, local_len, head_count, head_dim), (2, 0, 1, 3)
    )
    start_state = (
        jnp.full((head_count, records, local_len), -1e30, jnp.float32),
        jnp.zeros((head_count, records, local_len), jnp.float32),
        jnp.zeros((head_count, records, local_len, head_dim), jnp.float32),
    )
    pieces = (
        lax.all_gather(packed[:, :, 1], "ctx", axis=1, tiled=True),
        lax.all_gather(packed[:, :, 2], "ctx", axis=1, tiled=True),
    )
    key_len = pieces[0].shape[1]
    key_pos = jnp.arange(key_len, dtype=jnp.int32)
    key_ok = (key_pos[None, :] < frames[:, None]).astype(jnp.float32)
    key_heads = jnp.transpose(
        pieces[0].reshape(records, key_len, head_count, head_dim), (2, 0, 1, 3)
    )
    value_heads = jnp.transpose(
        pieces[1].reshape(records, key_len, head_count, head_dim), (2, 0, 1, 3)
    )

    def per_head(items):
        query_h, key_h, value_h, run_max, run_sum, run_acc = items
        scores = (
            jnp.einsum("rqe,rke->rqk", query_h, key_h, preferred_element_type=jnp.float32) * scaling
        )
        scores = jnp.where(key_ok[:, None, :] > 0, scores, -1e30)
        new_max = jnp.maximum(run_max, jnp.max(scores, -1))
        rescale = jnp.exp(run_max - new_max)
        numerator = jnp.exp(scores - new_max[..., None]) * key_ok[:, None, :]
        new_sum = run_sum * rescale + jnp.sum(numerator, -1)
        new_acc = run_acc * rescale[..., None] + jnp.einsum(
            "rqk,rke->rqe",
            numerator.astype(jnp.bfloat16),
            value_h,
            preferred_element_type=jnp.float32,
        )
        return (new_max, new_sum, new_acc)

    final_max, final_sum, final_acc = lax.map(
        per_head, (query_heads, key_heads, value_heads) + tuple(start_state)
    )
    attended = (final_acc / final_sum[..., None]).astype(jnp.bfloat16)
    attended = jnp.transpose(attended, (1, 2, 0, 3)).reshape(records, local_len, model_dim)
    projected = jnp.dot(
        attended.reshape(-1, model_dim), full_proj, preferred_element_type=jnp.float32
    )
    result = (residual.astype(jnp.float32) + present_rows * projected).astype(jnp.bfloat16)
    result = result.reshape(records, local_len, model_dim)
    cotangent = grad_out.reshape(-1, model_dim)
    back_two = jnp.dot(cotangent, full_second.T, preferred_element_type=jnp.float32)
    grad_conv = pull_back(back_two)[0].astype(jnp.bfloat16).reshape(records, local_len, model_dim)
    conv_pad = extended(grad_conv, (("ctx", 1),), reach)
    conv_wide = conv_pad.astype(jnp.float32)
    grad_gated = jnp.zeros((records, local_len, model_dim), jnp.float32)
    for tap_index in range(kernel_len):
        lead_in = 2 * reach - tap_index
        grad_gated = (
            grad_gated + depth_kernel[tap_index] * conv_wide[:, lead_in : lead_in + local_len]
        )
    grad_gated = grad_gated.reshape(-1, model_dim) * present_rows
    opening = jax.nn.sigmoid(gating)
    grad_hidden = jnp.concatenate(
        [grad_gated * opening, grad_gated * linear * opening * (1.0 - opening)], 1
    ).astype(jnp.bfloat16)
    conv_local = grad_conv.astype(jnp.float32)
    kernel_term = jnp.stack(
        [
            jnp.sum(gated_wide[:, tap_index : tap_index + local_len] * conv_local, axis=(0, 1))
            for tap_index in range(kernel_len)
        ]
    )
    grad_kernel = lax.psum(kernel_term, ("dp", "ctx"))
    partial_share = lax.psum_scatter(
        jnp.dot(normed.T, grad_hidden, preferred_element_type=jnp.float32).astype(jnp.bfloat16),
        "dp",
        scatter_dimension=0,
        tiled=True,
    )
    grad_first = lax.psum(partial_share, "ctx").astype(jnp.float32)
    back_one = jnp.dot(grad_hidden, full_first.T, preferred_element_type=jnp.float32)
    unused_out, pull_first = jax.vjp(lambda v: normalize(v, gain_first), flat_in)
    grad_in = (cotangent.astype(jnp.float32) + pull_first(back_one)[0]).astype(jnp.bfloat16)
    grad_in = grad_in.reshape(records, local_len, model_dim)
    return (result, grad_in, grad_first, grad_kernel)


def solution(mesh):
    placed = (
        P("dp", "ctx", None),
        P("dp"),
        P(),
        P("dp", None),
        P(),
        P(),
        P("dp", None),
        P(),
        P("dp", None),
        P("dp", None),
        P("dp", "ctx", None),
    )
    return jax.shard_map(
        local,
        mesh=mesh,
        in_specs=placed,
        out_specs=(P("dp", "ctx", None), P("dp", "ctx", None), P("dp", None), P()),
        check_vma=False,
    )
```

profile of v0, /device:TPU:8, one launch (start us, length us, event | category | flops | bytes accessed | tf_op | source)
XLA Modules:
  0.0 927.8 jit_solution(2277407869119887705)
XLA Ops:
  15.2 84.4 %all-gather.9.cloned.1.call-done = bf16[1024,2048]{1,0:T(8,128)(2,1)} async-done(((bf16[32,2048]{1,0:T(8,128)(2,1)}), bf16[1024,2048]{1,0:T(8,128)(2,1)}) %all-gather.9.cloned.1.call-update) | async-done | bytes 4194320 | tf_op jit(solution)/shard_map/all_gather | solution.py:58
  99.6 2.9 fusion.105
  102.7 3.4 collective-permute-start
  106.1 4.6 collective-permute-start.1
  112.7 2.8 fusion.97
  116.0 63.1 %all-gather.11.cloned.1.call-done = bf16[1024,1024]{1,0:T(8,128)(2,1)} async-done(((bf16[32,1024]{1,0:T(8,128)(2,1)}), bf16[1024,1024]{1,0:T(8,128)(2,1)}) %all-gather.11.cloned.1.call-update) | async-done | bytes 2097168 | tf_op jit(solution)/shard_map/all_gather | solution.py:59
  184.0 3.4 collective-permute-start.2
  187.4 4.6 collective-permute-start.3
  196.3 3.4 convolution_convert_fusion
  203.0 69.9 %all-gather.13.cloned.1.call-done = bf16[1024,3072]{1,0:T(8,128)(2,1)} async-done(((bf16[32,3072]{1,0:T(8,128)(2,1)}), bf16[1024,3072]{1,0:T(8,128)(2,1)}) %all-gather.13.cloned.1.call-update) | async-done | bytes 6291472 | tf_op jit(solution)/shard_map/all_gather | solution.py:60
  272.9 4.7 convolution_convert_fusion.1
  277.7 2.7 reshape.240
  280.4 121.1 %reduce-scatter.2.cloned.1.call-done = bf16[32,2048]{1,0:T(8,128)(2,1)} async-done(((bf16[1024,2048]{1,0:T(8,128)(2,1)}), bf16[32,2048]{1,0:T(8,128)(2,1)}) %reduce-scatter.2.cloned.1.call-update) | async-done | bytes 131088 | tf_op jit(solution)/shard_map/reduce_scatter | solution.py:161
  401.7 3.0 fusion.99
  409.9 3.8 multiply_reduce_fusion
  415.5 64.7 %all-reduce.3.cloned.1.call-done = bf16[32,2048]{1,0:T(8,128)(2,1)} async-done(((bf16[32,2048]{1,0:T(8,128)(2,1)}), bf16[32,2048]{1,0:T(8,128)(2,1)}) %all-reduce.3.cloned.1.call-update) | async-done | bytes 131088 | tf_op jit(solution)/shard_map/psum | solution.py:167
  481.9 54.7 %all-gather.17.cloned.1.call-done = bf16[2,512,1,1024]{3,2,1,0:T(2,128)(2,1)} async-done(((bf16[2,64,1,1024]{3,2,1,0:T(2,128)(2,1)}), bf16[2,512,1,1024]{3,2,1,0:T(2,128)(2,1)}) %all-gather.17.cloned.1.call-update) | async-done | bytes 2097168 | tf_op jit(solution)/shard_map/all_gather | solution.py:96
  536.6 9.0 copy.15
  545.6 46.8 %all-gather.19.cloned.1.call-done = bf16[2,512,1,1024]{3,2,1,0:T(2,128)(2,1)} async-done(((bf16[2,64,1,1024]{3,2,1,0:T(2,128)(2,1)}), bf16[2,512,1,1024]{3,2,1,0:T(2,128)(2,1)}) %all-gather.19.cloned.1.call-update) | async-done | bytes 2097168 | tf_op jit(solution)/shard_map/all_gather | solution.py:97
  592.4 10.5 %copy.16 = bf16[2,512,1,1024]{1,3,0,2:T(8,128)(2,1)} copy(bf16[2,512,1,1024]{3,2,1,0:T(2,128)(2,1)} %all-gather.19.cloned.1.call-done) | data formatting | bytes 4194304 | tf_op jit(solution)/shard_map/all_gather | solution.py:97
  602.9 37.5 %while.13 = (s32[]{:T(128)}, f32[16,2,64]{2,1,0:T(2,128)S(1)}, f32[16,2,64,64]{3,2,1,0:T(8,128)}, bf16[16,2,64,64]{3,2,1,0:T(8,128)(2,1)S(1)}, bf16[16,2,512,64]...) while((s32[]{:T(128)}, f32[16,2,64]{2,1,0:T(2,128)S(1)}, ...), condition=%wide.region_9.10_spmd.clone, body=%wide.region_6.9_spmd.clone.sunk | while | flops 17378944 | bytes 1171553 | solution.py:127
  642.6 31.6 %all-gather.15.cloned.1.call-done = bf16[1024,1024]{1,0:T(8,128)(2,1)} async-done(((bf16[32,1024]{1,0:T(8,128)(2,1)}), bf16[1024,1024]{1,0:T(8,128)(2,1)}) %all-gather.15.cloned.1.call-update) | async-done | bytes 2097168 | tf_op jit(solution)/shard_map/all_gather | solution.py:61
  674.2 2.7 fusion.19
  676.9 242.7 %all-reduce.5.cloned.1.call-done = f32[31,1024]{1,0:T(8,128)} async-done(((f32[31,1024]{1,0:T(8,128)}), f32[31,1024]{1,0:T(8,128)}) %all-reduce.5.cloned.1.call-update) | async-done | bytes 126992 | tf_op jit(solution)/shard_map/psum | solution.py:160
  (186 shorter events, 72.8 us)
Async XLA Ops:
  7.2 92.5 %all-gather.9.cloned.1.call-start = ((), (), s32[]{:S(2)}) async-start(), calls=%async_computation.1 | async-start | bytes 4325376 | tf_op jit(solution)/shard_map/all_gather | solution.py:58
  7.9 171.1 %all-gather.11.cloned.1.call-start = ((), (), s32[]{:S(2)}) async-start(), calls=%async_computation.2 | async-start | bytes 2162688 | tf_op jit(solution)/shard_map/all_gather | solution.py:59
  8.6 264.3 %all-gather.13.cloned.1.call-start = ((), (), s32[]{:S(2)}) async-start(), calls=%async_computation.3 | async-start | bytes 6488064 | tf_op jit(solution)/shard_map/all_gather | solution.py:60
  9.4 392.1 %reduce-scatter.2.cloned.1.call-start = ((), (), s32[]{:S(2)}) async-start(), calls=%async_computation.5 | async-start | bytes 4325376 | tf_op jit(solution)/shard_map/reduce_scatter | solution.py:161
  102.7 9.1 collective-permute-start
  106.1 6.5 collective-permute-start.1
  112.7 66.3 %copy-start.3 = (bf16[2,64,1024]{2,1,0:T(8,128)(2,1)S(1)}, bf16[2,64,1024]{2,1,0:T(8,128)(2,1)}, u32[]{:S(2)}) copy-start(bf16[2,64,1024]{2,1,0:T(8,128)(2,1)} %param.23) | copy-start | bytes 786436
  112.7 66.3 %copy-start.8 = (f32[1024]{0:T(1024)S(1)}, f32[1024]{0:T(1024)}, u32[]{:S(2)}) copy-start(f32[1024]{0:T(1024)} %param.18) | copy-start | bytes 12292
  184.0 8.3 collective-permute-start.2
  187.4 6.5 collective-permute-start.3
  199.7 0.9 copy-start
  199.7 1.0 copy-start.2
  199.7 73.2 %copy-start.7 = (f32[1024]{0:T(1024)S(1)}, f32[1024]{0:T(1024)}, u32[]{:S(2)}) copy-start(f32[1024]{0:T(1024)} %param.20) | copy-start | bytes 12292
  199.7 280.5 %all-reduce.3.cloned.1.call-start = ((), (), s32[]{:S(2)}) async-start(), calls=%async_computation.6 | async-start | bytes 262144 | tf_op jit(solution)/shard_map/psum | solution.py:167
  401.5 135.1 %all-gather.17.cloned.1.call-start = ((), (), s32[]{:S(2)}) async-start(), calls=%async_computation.8 | async-start | bytes 4718592 | tf_op jit(solution)/shard_map/all_gather | solution.py:96
  404.8 187.6 %all-gather.19.cloned.1.call-start = ((), (), s32[]{:S(2)}) async-start(), calls=%async_computation.9 | async-start | bytes 4718592 | tf_op jit(solution)/shard_map/all_gather | solution.py:97
  405.5 268.7 %all-gather.15.cloned.1.call-start = ((), (), s32[]{:S(2)}) async-start(), calls=%async_computation.4 | async-start | bytes 2162688 | tf_op jit(solution)/shard_map/all_gather | solution.py:61
  406.3 513.4 %all-reduce.5.cloned.1.call-start = ((), (), s32[]{:S(2)}) async-start(), calls=%async_computation.7 | async-start | bytes 262144 | tf_op jit(solution)/shard_map/psum | solution.py:160
  406.3 3.5 copy-start.6
  409.9 4.1 copy-start.4
  413.7 1.3 copy-start.1
  545.6 57.3 %copy-start.5 = (s32[2]{0:T(128)S(1)}, s32[2]{0:T(128)}, u32[]{:S(2)}) copy-start(s32[2]{0:T(128)} %param.14) | copy-start | bytes 28
Sparse Core Ops, SparseCore 0:
  10.8 88.8 all-gather.8
  102.4 76.5 all-gather.10
  181.8 91.0 all-gather.12
  277.0 124.4 reduce-scatter.1
  404.1 76.0 all-reduce.2
  481.9 54.6 all-gather.16
  538.4 53.9 all-gather.18
  595.1 79.0 all-gather.14
  680.3 239.3 all-reduce.4
where the time goes:
time: 929 us; the launch traced here: 928 us
  waiting for transfers between devices  785 us (84%)
  matrix products  54.7 us (6%)
  local copies, waits for them, and re-layouts  34.5 us (4%)
  other arithmetic  22.4 us (2%)
  starting transfers between devices  16.4 us (2%)
  between operations  14.2 us (2%)
    psum x1, waiting for transfers between devices, local(): grad_kernel = lax.psum(kernel_term, ('dp', 'ctx'))  243 us
    reduce_scatter x1, waiting for transfers between devices, local(): lax.psum_scatter(jnp.dot(normed.T, grad_hidden, preferred_element_type=jn...  121 us
    all_gather x1, waiting for transfers between devices, local(): full_first = lax.all_gather(w_first, 'dp', axis=0, tiled=True)  84.4 us
    all_gather x1, waiting for transfers between devices, local(): full_qkv = lax.all_gather(w_qkv, 'dp', axis=0, tiled=True)  69.9 us
    psum x1, waiting for transfers between devices, local(): grad_first = lax.psum(partial_share, 'ctx').astype(jnp.float32)  64.7 us
    all_gather x1, waiting for transfers between devices, local(): full_second = lax.all_gather(w_second, 'dp', axis=0, tiled=True)  63.1 us
    all_gather x1, waiting for transfers between devices, local(): lax.all_gather(packed[:, :, 1], 'ctx', axis=1, tiled=True)  54.7 us
    all_gather x1, waiting for transfers between devices, local(): lax.all_gather(packed[:, :, 2], 'ctx', axis=1, tiled=True)  46.8 us
  transfers between devices with their start and end apart: 13, of which 12 were waited for; matrix products, arithmetic and copies ran while one was open for 12% of the time, Pallas kernels for 0%

commit v1 on v0

v1 whole, which is shorter than its diff:
```python
import functools

import jax
import jax.numpy as jnp
from jax import lax
from jax.experimental import pallas as pl
from jax.experimental.pallas import tpu as pltpu
from jax.sharding import Mesh
from jax.sharding import PartitionSpec as P

HEADS = 16
EPSILON = 1e-05
BF = jnp.bfloat16
F32 = jnp.float32

DP = ("yh", "z", "core")
CTX = ("yl", "x")
YZ = ("yh", "z")

VM = pl.BlockSpec(memory_space=pltpu.VMEM)
SM = pl.BlockSpec(memory_space=pltpu.SMEM)
ANY = pl.BlockSpec(memory_space=pl.ANY)


def params(mib):
    return pltpu.CompilerParams(vmem_limit_bytes=mib << 20)


def cost(flops, nbytes):
    return pl.CostEstimate(flops=flops, bytes_accessed=nbytes, transcendentals=0)


def centred(values):
    centre = values - jnp.mean(values, -1, keepdims=True)
    spread = jnp.mean(centre * centre, -1, keepdims=True)
    return centre, lax.rsqrt(spread + EPSILON)


def norm_pull(cot, centre, inv):
    xhat = centre * inv
    return inv * (
        cot - jnp.mean(cot, -1, keepdims=True) - xhat * jnp.mean(cot * xhat, -1, keepdims=True)
    )


def dot(a, b):
    return jnp.dot(a, b, preferred_element_type=F32)


def dot_t(a, b):
    return lax.dot_general(a, b, (((1,), (1,)), ((), ())), preferred_element_type=F32)


def sigmoid(v):
    return jax.nn.sigmoid(v)


def first_body(scal, x_ref, g_ref, w_ref, out_ref, wout_ref):
    count, rows, model = out_ref.shape
    centre, inv = centred(x_ref[...].astype(F32))
    normed = (centre * inv * g_ref[...]).astype(BF)
    for i in range(count):
        out_ref[i] = normed
    width = wout_ref.shape[2] // 2
    at = pl.multiple_of(scal[2] * width, width)
    cut = jnp.concatenate(
        [w_ref[:, pl.ds(at, width)], w_ref[:, pl.ds(pl.multiple_of(model + at, width), width)]], 1
    )
    for i in range(wout_ref.shape[0]):
        wout_ref[i] = cut


def gate_body(taps, scal, x_ref, wm_ref, wo_ref, k_ref, conv_ref, hid_ref, gated_ref, w_s, pad_s):
    rec = pl.program_id(0)
    core = scal[0]

    @pl.when(rec == 0)
    def _():
        w_s[:, pl.ds(core, 1)] = wm_ref[...][:, None]
        w_s[:, pl.ds(1 - core, 1)] = wo_ref[...][:, None]

    blocks, _, local, model = x_ref.shape
    length = blocks * local
    width = k_ref.shape[1]
    x = x_ref[...].reshape(length, model)
    hidden = dot(x, w_s[...].reshape(model, 2 * width))
    hid_ref[0] = hidden
    frames = scal[3 + rec]
    here = lax.broadcasted_iota(jnp.int32, (length, width), 0) < frames
    gated = jnp.where(here, hidden[:, :width] * sigmoid(hidden[:, width:]), 0.0).astype(BF)
    gated_ref[0] = gated
    pad_s[0:16] = jnp.zeros((16, width), F32)
    pad_s[16 + length : 32 + length] = jnp.zeros((16, width), F32)
    pad_s[16 : 16 + length] = gated.astype(F32)
    for b in range(blocks):
        total = jnp.zeros((local, width), F32)
        for j in range(taps):
            at = b * local + j + 1
            total = total + k_ref[j : j + 1, :] * pad_s[at : at + local, :]
        conv_ref[b, 0] = total


def fetch(pieces, slots, yh, core, sems):
    copies = []
    for dst, lo, width in slots:
        group = []
        for src, owner in pieces:
            for slot in range(2):
                side = yh if slot == 0 else 1 - yh
                group.append(
                    pltpu.make_async_copy(
                        src.at[:, slot, :, lo : lo + width],
                        dst.at[side, :, owner],
                        sems.at[len(copies) * 4 + len(group)],
                    )
                )
        copies.append(group)
    for group in copies:
        for one in group:
            one.start()
    return copies


def finish(group):
    for one in group:
        one.wait()


def token_body(scal, c_ref, x_ref, go_ref, g2_ref, ga_ref, mine, other, out_ref, res_ref, w2_s, wq_s, sems):
    yh, core = scal[1], scal[0]
    model = x_ref.shape[1]
    blocks = out_ref.shape[0]
    width = model // blocks
    copies = fetch(
        ((mine, core), (other, 1 - core)),
        ((w2_s, 0, model), (wq_s, model, 3 * model)),
        yh,
        core,
        sems,
    )
    conv = jnp.concatenate([c_ref[i] for i in range(blocks)], 1)
    centre, inv = centred(conv)
    gain = g2_ref[...]
    normal = centre * inv * gain
    opening = sigmoid(normal)
    swished = (normal * opening).astype(BF)
    finish(copies[0])
    w2 = w2_s[...].reshape(model, model)
    residual = (x_ref[...].astype(F32) + dot(swished, w2)).astype(BF)
    res_ref[...] = residual
    back_two = dot_t(go_ref[...], w2)
    slope = opening + normal * opening * (1.0 - opening)
    grad_conv = norm_pull(back_two * slope * gain, centre, inv).astype(BF)
    for i in range(blocks):
        out_ref[i, :, 3 * width :] = grad_conv[:, i * width : (i + 1) * width]
    centre, inv = centred(residual.astype(F32))
    attn_in = (centre * inv * ga_ref[...]).astype(BF)
    finish(copies[1])
    wide = 2 * width
    for part in range(3):
        for i in range(0, blocks, 2):
            lo = part * model + i * width
            got = dot(attn_in, wq_s[:, :, :, :, lo : lo + wide].reshape(model, wide)).astype(BF)
            out_ref[i, :, part * width : (part + 1) * width] = got[:, :width]
            out_ref[i + 1, :, part * width : (part + 1) * width] = got[:, width:]


def feature_body(
    taps, head_dim, scal, p_ref, hid_ref, gated_ref, x_ref, k_ref,
    out_ref, keep_ref, send_ref, gk_ref, pad_s, gpad_s, gf_s, gk_s,
):
    rec = pl.program_id(0)
    core = scal[0]
    frames = scal[3 + rec]
    blocks, _, local, _ = p_ref.shape
    length = blocks * local
    width = k_ref.shape[1]
    model = x_ref.shape[3]

    @pl.when(rec == 0)
    def _():
        gk_s[...] = jnp.zeros_like(gk_s)

    zeros = jnp.zeros((16, width), F32)
    for ref in (pad_s, gpad_s):
        ref[0:16] = zeros
        ref[16 + length : 32 + length] = zeros
    pad_s[16 : 16 + length] = p_ref[:, 0, :, 3 * width :].reshape(length, width).astype(F32)
    gpad_s[16 : 16 + length] = gated_ref[0].astype(F32)
    for b in range(blocks):
        base = b * local
        total = jnp.zeros((local, width), F32)
        own = pad_s[16 + base : 16 + base + local, :]
        for j in range(taps):
            at = base + taps - j
            total = total + k_ref[j : j + 1, :] * pad_s[at : at + local, :]
            at = base + j + 1
            term = (gpad_s[at : at + local, :] * own).reshape(local // 8, 8, width)
            gk_s[j] += jnp.sum(term, 0)
        at = lax.broadcasted_iota(jnp.int32, (local, width), 0) + base
        grad_gated = jnp.where(at < frames, total, 0.0)
        linear = hid_ref[0, base : base + local, :width]
        opening = sigmoid(hid_ref[0, base : base + local, width:])
        first = grad_gated * opening
        out_ref[b, 0, :, :width] = first.astype(BF)
        out_ref[b, 0, :, width : 2 * width] = (first * linear * (1.0 - opening)).astype(BF)
    grad_hidden = out_ref[:, 0, :, : 2 * width].reshape(length, 2 * width)
    x = x_ref[...].reshape(length, model)
    grad_first = lax.dot_general(
        x, grad_hidden, (((0,), (0,)), ((), ())), preferred_element_type=F32
    ).reshape(gf_s.shape)

    @pl.when(rec == 0)
    def _():
        gf_s[...] = grad_first

    @pl.when(rec > 0)
    def _():
        gf_s[...] += grad_first

    q = p_ref[:, 0, :, :width].reshape(length, width)
    k = p_ref[:, 0, :, width : 2 * width].reshape(length, width)
    v = p_ref[:, 0, :, 2 * width : 3 * width].reshape(length, width)
    rows = min(256, length)
    key_ok = lax.broadcasted_iota(jnp.int32, (rows, length), 1) < frames
    lane = lax.broadcasted_iota(jnp.int32, (rows, width), 1)
    scaling = head_dim**-0.5
    for r in range(0, length, rows):
        qr = q[r : r + rows]
        attended = jnp.zeros((rows, width), F32)
        for h in range(width // head_dim):
            mine = (lane >= h * head_dim) & (lane < (h + 1) * head_dim)
            scores = dot_t(jnp.where(mine, qr, jnp.zeros_like(qr)), k) * scaling
            scores = jnp.where(key_ok, scores, -1e30)
            top = jnp.max(scores, -1, keepdims=True)
            numer = jnp.where(key_ok, jnp.exp(scores - top), 0.0)
            denom = jnp.sum(numer, -1, keepdims=True)
            attended = jnp.where(mine, dot(numer.astype(BF), v) / denom, attended)
        got = attended.astype(BF).reshape(rows // local, local, width)
        out_ref[r // local : (r + rows) // local, 0, :, 2 * width :] = got

    @pl.when(rec == pl.num_programs(0) - 1)
    def _():
        keep_ref[...] = gf_s[:, pl.ds(core, 1)][:, 0]
        send_ref[...] = gf_s[:, pl.ds(1 - core, 1)][:, 0].astype(BF)
        gk = jnp.sum(gk_s[...], 1)
        half = gk_ref.shape[0]
        gk_ref[:, :width] = gk[:half]
        gk_ref[:, width:] = gk[half:]


def pair_body(keep_ref, recv_ref, gk_ref, gkr_ref, out_ref):
    count, depth, _ = keep_ref.shape
    out_ref[:, :depth] = (keep_ref[...] + recv_ref[...].astype(F32)).astype(BF)
    gk = (gk_ref[...] + gkr_ref[...]).astype(BF)
    for i in range(count):
        out_ref[i, depth:] = gk


def sum_body(x_ref, out_ref):
    total = jnp.sum(x_ref[...].astype(F32), 0)
    for i in range(out_ref.shape[0]):
        out_ref[i] = total


def last_body(x_ref, gf_ref, gk_ref):
    blocks = x_ref.shape[0]
    depth = gf_ref.shape[0]
    width = x_ref.shape[2] // 2
    model = gk_ref.shape[1]
    half = x_ref.shape[1] - depth
    taps = gk_ref.shape[0]
    for i in range(blocks):
        lo = i * width
        gf_ref[:, lo : lo + width] = x_ref[i, :depth, :width]
        gf_ref[:, model + lo : model + lo + width] = x_ref[i, :depth, width:]
        gk_ref[:half, lo : lo + width] = x_ref[i, depth:, :width]
        gk_ref[half:, lo : lo + width] = x_ref[i, depth : depth + taps - half, width:]


def result_body(scal, a_ref, res_ref, x_ref, go_ref, g1_ref, mine, other, out_ref, gin_ref, wp_s, w1_s, sems):
    yh, core, ctx = scal[1], scal[0], scal[2]
    rows, model = x_ref.shape
    blocks = a_ref.shape[0]
    width = model // blocks
    copies = fetch(
        ((mine, core), (other, 1 - core)),
        ((wp_s, 0, model), (w1_s, model, 2 * model)),
        yh,
        core,
        sems,
    )
    centre, inv = centred(x_ref[...].astype(F32))
    attended = jnp.concatenate([a_ref[i, :, 2 * width :] for i in range(blocks)], 1)
    linear = jnp.concatenate([a_ref[i, :, :width] for i in range(blocks)], 1)
    gating = jnp.concatenate([a_ref[i, :, width : 2 * width] for i in range(blocks)], 1)
    finish(copies[0])
    projected = dot(attended, wp_s[...].reshape(model, model))
    records = 2
    local = rows // records
    at = lax.broadcasted_iota(jnp.int32, (local, model), 0) + ctx * local
    present = jnp.concatenate([(at < scal[3 + r]).astype(F32) for r in range(records)], 0)
    out_ref[...] = (res_ref[...].astype(F32) + present * projected).astype(BF)
    finish(copies[1])
    w1 = w1_s[...].reshape(model, 2 * model)
    back_one = dot_t(linear, w1[:, :model]) + dot_t(gating, w1[:, model:])
    pulled = norm_pull(back_one * g1_ref[...], centre, inv)
    gin_ref[...] = (go_ref[...].astype(F32) + pulled).astype(BF)


def swap_core(v):
    return lax.ppermute(v, "core", [(0, 1), (1, 0)])


def swap_yh(v):
    return lax.ppermute(v, ("yh", "yl"), [(0, 3), (3, 0), (1, 2), (2, 1)])


def gathered(cat):
    shard = jnp.stack([cat, swap_yh(cat)])
    return shard


def local(
    inputs,
    frames,
    gain_first,
    w_first,
    depth_kernel,
    gain_second,
    w_second,
    gain_attn,
    w_qkv,
    w_proj,
    grad_out,
):
    records, local_len, model = inputs.shape
    taps = depth_kernel.shape[0]
    blocks = lax.axis_size(CTX)
    zs = lax.axis_size("z")
    groups = 2 * zs
    depth = w_first.shape[0]
    width = model // blocks
    length = blocks * local_len
    rows = records * local_len
    head_dim = model // HEADS
    ctx = lax.axis_index(CTX)
    shape = jax.ShapeDtypeStruct

    scal = jnp.concatenate(
        [
            jnp.stack([lax.axis_index("core"), lax.axis_index("yh"), ctx]).astype(jnp.int32),
            frames,
        ]
    )
    x = inputs.reshape(rows, model)
    cot = grad_out.reshape(rows, model)
    taps_own = lax.dynamic_slice_in_dim(
        jnp.pad(depth_kernel, ((0, 32 - taps), (0, 0))), ctx * width, width, 1
    )

    shard_a = gathered(jnp.concatenate([w_second, w_qkv], 1))
    sent, w1_sent = pl.pallas_call(
        first_body,
        out_shape=(
            shape((blocks, rows, model), BF),
            shape((groups, depth, 2 * width), BF),
        ),
        in_specs=[SM, VM, VM, VM],
        out_specs=(VM, VM),
        compiler_params=params(32),
        name="first_norm",
    )(scal, x, gain_first.reshape(1, model), w_first)
    shard_a, w1_sent = lax.optimization_barrier((shard_a, w1_sent))
    all_a = lax.all_gather(shard_a, "z", axis=0, tiled=False)
    w1_mine = lax.all_to_all(w1_sent, YZ, 0, 0, tiled=True)
    w1_other = swap_core(w1_mine)
    normed = lax.all_to_all(sent, CTX, 0, 0, tiled=True).reshape(blocks, records, local_len, model)

    conv, hidden, gated = pl.pallas_call(
        functools.partial(gate_body, taps),
        grid=(records,),
        out_shape=(
            shape((blocks, records, local_len, width), F32),
            shape((records, length, 2 * width), F32),
            shape((records, length, width), BF),
        ),
        in_specs=[
            SM,
            pl.BlockSpec((blocks, 1, local_len, model), lambda r: (0, r, 0, 0)),
            pl.BlockSpec((groups, depth, 2 * width), lambda r: (0, 0, 0)),
            pl.BlockSpec((groups, depth, 2 * width), lambda r: (0, 0, 0)),
            pl.BlockSpec((32, width), lambda r: (0, 0)),
        ],
        out_specs=(
            pl.BlockSpec((blocks, 1, local_len, width), lambda r: (0, r, 0, 0)),
            pl.BlockSpec((1, length, 2 * width), lambda r: (r, 0, 0)),
            pl.BlockSpec((1, length, width), lambda r: (r, 0, 0)),
        ),
        scratch_shapes=[
            pltpu.VMEM((groups, 2, depth, 2 * width), BF),
            pltpu.VMEM((length + 32, width), F32),
        ],
        compiler_params=params(32),
        name="gate_conv",
    )(scal, normed, w1_mine, w1_other, taps_own)

    all_a, conv = lax.optimization_barrier((all_a, conv))
    other_a = swap_core(all_a)
    shard_b = gathered(jnp.concatenate([w_proj, w_first], 1))
    shard_b, all_a = lax.optimization_barrier((shard_b, all_a))
    all_b = lax.all_gather(shard_b, "z", axis=0, tiled=False)
    conv_rows = lax.all_to_all(conv, CTX, 0, 0, tiled=True).reshape(blocks, rows, width)

    packed, residual = pl.pallas_call(
        token_body,
        out_shape=(shape((blocks, rows, 4 * width), BF), shape((rows, model), BF)),
        in_specs=[SM, VM, VM, VM, VM, VM, ANY, ANY],
        out_specs=(VM, VM),
        scratch_shapes=[
            pltpu.VMEM((2, zs, 2, depth, model), BF),
            pltpu.VMEM((2, zs, 2, depth, 3 * model), BF),
            pltpu.SemaphoreType.DMA((8,)),
        ],
        compiler_params=params(40),
        name="token_rows",
    )(
        scal, conv_rows, x, cot, gain_second.reshape(1, model), gain_attn.reshape(1, model),
        all_a, other_a,
    )

    packed = lax.all_to_all(packed, CTX, 0, 0, tiled=True)
    packed = packed.reshape(blocks, records, local_len, 4 * width)
    back, keep, send, gk = pl.pallas_call(
        functools.partial(feature_body, taps, head_dim),
        grid=(records,),
        out_shape=(
            shape((blocks, records, local_len, 3 * width), BF),
            shape((groups, depth, 2 * width), F32),
            shape((groups, depth, 2 * width), BF),
            shape((16, 2 * width), F32),
        ),
        in_specs=[
            SM,
            pl.BlockSpec((blocks, 1, local_len, 4 * width), lambda r: (0, r, 0, 0)),
            pl.BlockSpec((1, length, 2 * width), lambda r: (r, 0, 0)),
            pl.BlockSpec((1, length, width), lambda r: (r, 0, 0)),
            pl.BlockSpec((blocks, 1, local_len, model), lambda r: (0, r, 0, 0)),
            pl.BlockSpec((32, width), lambda r: (0, 0)),
        ],
        out_specs=(
            pl.BlockSpec((blocks, 1, local_len, 3 * width), lambda r: (0, r, 0, 0)),
            pl.BlockSpec((groups, depth, 2 * width), lambda r: (0, 0, 0)),
            pl.BlockSpec((groups, depth, 2 * width), lambda r: (0, 0, 0)),
            pl.BlockSpec((16, 2 * width), lambda r: (0, 0)),
        ),
        scratch_shapes=[
            pltpu.VMEM((length + 32, width), F32),
            pltpu.VMEM((length + 32, width), F32),
            pltpu.VMEM((groups, 2, depth, 2 * width), F32),
            pltpu.VMEM((32, 8, width), F32),
        ],
        compiler_params=params(40),
        name="features",
    )(scal, packed, hidden, gated, normed, taps_own)

    other_b = swap_core(all_b)
    recv, gk_recv = swap_core(send), swap_core(gk)
    back = lax.all_to_all(back, CTX, 0, 0, tiled=True).reshape(blocks, rows, 3 * width)
    shares = pl.pallas_call(
        pair_body,
        out_shape=shape((groups, depth + 16, 2 * width), BF),
        in_specs=[VM] * 4,
        out_specs=VM,
        compiler_params=params(16),
        name="pair_sum",
    )(keep, recv, gk, gk_recv)
    shares = lax.all_to_all(shares, YZ, 0, 0, tiled=True)
    total = pl.pallas_call(
        sum_body,
        out_shape=shape((blocks, depth + 16, 2 * width), F32),
        in_specs=[VM],
        out_specs=VM,
        compiler_params=params(16),
        name="share_sum",
    )(shares)
    total = lax.all_to_all(total, CTX, 0, 0, tiled=True)
    grad_first, grad_kernel = pl.pallas_call(
        last_body,
        out_shape=(shape((depth, 2 * model), F32), shape((taps, model), F32)),
        in_specs=[VM],
        out_specs=(VM, VM),
        compiler_params=params(16),
        name="lay_out",
    )(total)

    result, grad_in = pl.pallas_call(
        result_body,
        out_shape=(shape((rows, model), BF), shape((rows, model), BF)),
        in_specs=[SM, VM, VM, VM, VM, VM, ANY, ANY],
        out_specs=(VM, VM),
        scratch_shapes=[
            pltpu.VMEM((2, zs, 2, depth, model), BF),
            pltpu.VMEM((2, zs, 2, depth, 2 * model), BF),
            pltpu.SemaphoreType.DMA((8,)),
        ],
        compiler_params=params(40),
        name="result_rows",
    )(scal, back, residual, x, cot, gain_first.reshape(1, model), all_b, other_b)
    return (
        result.reshape(records, local_len, model),
        grad_in.reshape(records, local_len, model),
        grad_first,
        grad_kernel,
    )


def solution(mesh):
    dp, ctx = mesh.devices.shape
    split = Mesh(
        mesh.devices.reshape(2, dp // 4, 2, 2, ctx // 2), ("yh", "z", "core", "yl", "x")
    )
    tokens = P(DP, CTX, None)
    placed = (
        tokens,
        P(DP),
        P(),
        P(DP, None),
        P(),
        P(),
        P(DP, None),
        P(),
        P(DP, None),
        P(DP, None),
        tokens,
    )
    return jax.shard_map(
        local,
        mesh=split,
        in_specs=placed,
        out_specs=(tokens, tokens, P(DP, None), P()),
        check_vma=False,
    )
```

time: 929 us -> 224 us (0.24)
  waiting for transfers between devices: 785 us -> 73 us
  blocking collectives: 0 us -> 75.9 us
  matrix products: 54.7 us -> 0 us
  Pallas kernels: 0 us -> 21.9 us
  local copies, waits for them, and re-layouts: 34.5 us -> 13.3 us
  other arithmetic: 22.4 us -> 3.31 us
    psum x2 -> x0, waiting for transfers between devices: 307 us -> none  [the longest x1 243 us: local(): grad_kernel = lax.psum(kernel_term, ('dp', 'ctx'))]
    all_gather x6 -> x2, waiting for transfers between devices: 350 us -> 44.6 us  [the longest x1 40 us: local(): all_b = lax.all_gather(shard_b, 'z', axis=0, tiled=False)]
    reduce_scatter x1 -> x0, waiting for transfers between devices: 121 us -> none  [local(): lax.psum_scatter(jnp.dot(normed.T, grad_hidden, preferred_element_type=jn...]
    all_to_all x0 -> x4, blocking collectives: none -> 75.9 us  [the longest x1 23.4 us: local(): w1_mine = lax.all_to_all(w1_sent, YZ, 0, 0, tiled=True)]
    dot_general x39 -> x0, matrix products: 54.7 us -> none  [the longest x16 28.5 us: per_head(): jnp.einsum('rqk,rke->rqe', numerator.astype(jnp.bfloat16), value_h, prefe...]
    pallas_call x0 -> x8, Pallas kernels: none -> 21.9 us  [the longest x1 7.64 us: local(): pl.pallas_call(functools.partial(feature_body, taps, head_dim), grid=(rec...]
    all_to_all x0 -> x3, waiting for transfers between devices: none -> 20.7 us  [the longest x1 13.7 us: local(): lax.all_to_all(sent, CTX, 0, 0, tiled=True)]
    all_gather x2 -> x0, local copies, waits for them, and re-layouts: 19.5 us -> none  [the longest x1 10.5 us: local(): lax.all_gather(packed[:, :, 2], 'ctx', axis=1, tiled=True)]
  transfers between devices with their start and end apart: 13 -> 12, of which waited for: 12 -> 7; matrix products, arithmetic and copies ran while one was open for 12% -> 1% of each run, Pallas kernels for 0% -> 7%
where the time goes in v1:
time: 224 us; the launch traced here: 222 us
  blocking collectives  75.9 us (34%)
  waiting for transfers between devices  73 us (33%)
  Pallas kernels  21.9 us (10%)
  starting transfers between devices  19.9 us (9%)
  between operations  14.3 us (6%)
  local copies, waits for them, and re-layouts  13.3 us (6%)
  other arithmetic  3.31 us (1%)
    all_gather x1, waiting for transfers between devices, local(): all_b = lax.all_gather(shard_b, 'z', axis=0, tiled=False)  40 us
    all_to_all x1, blocking collectives, local(): w1_mine = lax.all_to_all(w1_sent, YZ, 0, 0, tiled=True)  23.4 us
    all_to_all x1, blocking collectives, local(): packed = lax.all_to_all(packed, CTX, 0, 0, tiled=True)  20.4 us
    all_to_all x1, blocking collectives, local(): shares = lax.all_to_all(shares, YZ, 0, 0, tiled=True)  20.4 us
    all_to_all x1, waiting for transfers between devices, local(): lax.all_to_all(sent, CTX, 0, 0, tiled=True)  13.7 us
    unnamed x46, local copies, waits for them, and re-layouts  12.4 us
    all_to_all x1, blocking collectives, local(): total = lax.all_to_all(total, CTX, 0, 0, tiled=True)  11.7 us
    pallas_call x1, Pallas kernels, local(): pl.pallas_call(functools.partial(feature_body, taps, head_dim), grid=(rec...  7.64 us
  transfers between devices with their start and end apart: 12, of which 7 were waited for; matrix products, arithmetic and copies ran while one was open for 1% of the time, Pallas kernels for 7%

profile of v1, /device:TPU:8, one launch (start us, length us, event | category | flops | bytes accessed | tf_op | source)
XLA Modules:
  0.0 221.7 jit_solution(13002807327574087182)
XLA Ops:
  9.0 1.7 collective-permute-start
  14.8 1.4 copy-done.4
  16.2 1.0 collective-permute-done
  18.0 23.4 %all_to_all.35.wm_ref = bf16[16,32,256]{2,1,0:T(8,128)(2,1)S(1)} all-to-all(bf16[16,32,256]{2,1,0:T(8,128)(2,1)S(1)} %get-tuple-element.28), channel_id=1, replica_groups=mesh['yh'=2,'z'=8,'core'=2,'yl'=2,'x'=4] {'yh','z'}, dimensions={0} | all-to-all | bytes 524288 | tf_op jit(solution)/shard_map/all_to_all | solution.py:376
  41.4 5.9 %all-to-all-start = ((bf16[8,128,1024]{2,1,0:T(8,128)(2,1)}), bf16[8,128,1024]{2,1,0:T(8,128)(2,1)S(1)}, u32[]{:S(2)}, u32[]{:S(2)}) async-start(bf16[8,128,1024]{2,1,0:T(8,128)(2,1)} %copy-done.4), calls=%async_computation | async-start | bytes 4194304 | tf_op jit(solution)/shard_map/all_to_all | solution.py:378
  47.7 5.6 %collective-permute-done.2 = bf16[32,3072]{1,0:T(8,128)(2,1)} collective-permute-done((bf16[32,3072]{1,0:T(8,128)(2,1)S(1)}, bf16[32,3072]{1,0:T(8,128)(2,1)}, u32[]{:S(2)}, u32[]{:S(2)}) %collective-permute-start.2) | collective-permute-done | bytes 196640 | tf_op jit(solution)/shard_map/ppermute | solution.py:316
  53.3 1.7 pad_maximum_fusion.1
  55.1 13.7 %all-to-all-done = bf16[8,128,1024]{2,1,0:T(8,128)(2,1)S(1)} async-done(((bf16[8,128,1024]{2,1,0:T(8,128)(2,1)}), bf16[8,128,1024]{2,1,0:T(8,128)(2,1)S(1)}, u32[]{:S(2)}, u32[]{:S(2)}) %all-to-all-start) | async-done | bytes 2097184 | tf_op jit(solution)/shard_map/all_to_all | solution.py:378
  68.8 2.7 %gate_conv.1 = (f32[8,2,64,128]{3,2,1,0:T(8,128)S(1)}, f32[2,512,256]{2,1,0:T(8,128)S(1)}, bf16[2,512,128]{2,1,0:T(8,128)(2,1)S(1)}) custom-call(s32[5]{0:T(128)S(1)} %pad_add_fusion.scal, bf16[8,2,64,1024]{3,2,1,0:T(8,128)(2,1)S(1)} %bitcast.20, bf16[16,32,256]{2,1,0:T(8,128)(2,1)S(1)} %all_to_all.35.wm_ref, ...), custom_call_target="tpu_custom_call" | custom-call | tf_op jit(solution)/shard_map/gate_conv/pallas_call | solution.py:380
  71.5 1.0 copy-done.6
  73.3 4.7 %all-gather.5.cloned.1.call-done = bf16[16,32,4096]{2,1,0:T(8,128)(2,1)} async-done(((bf16[2,32,4096]{2,1,0:T(8,128)(2,1)}), bf16[16,32,4096]{2,1,0:T(8,128)(2,1)}) %all-gather.5.cloned.1.call-update) | async-done | bytes 4194320 | tf_op jit(solution)/shard_map/all_gather | solution.py:375
  78.2 5.8 %all-to-all-start.2 = ((f32[8,2,64,128]{3,2,1,0:T(8,128)}), f32[8,2,64,128]{3,2,1,0:T(8,128)S(1)}, u32[]{:S(2)}, u32[]{:S(2)}) async-start(f32[8,2,64,128]{3,2,1,0:T(8,128)} %copy-done.11), calls=%async_computation.2 | async-start | bytes 1048576 | tf_op jit(solution)/shard_map/all_to_all | solution.py:413
  83.9 40.0 %all-gather.7.cloned.1.call-done = bf16[16,32,3072]{2,1,0:T(8,128)(2,1)} async-done(((bf16[2,32,3072]{2,1,0:T(8,128)(2,1)}), bf16[16,32,3072]{2,1,0:T(8,128)(2,1)}) %all-gather.7.cloned.1.call-update) | async-done | bytes 3145744 | tf_op jit(solution)/shard_map/all_gather | solution.py:412
  123.9 2.2 copy-done
  126.1 4.3 %token_rows.1 = (bf16[8,128,512]{2,1,0:T(8,128)(2,1)S(1)}, bf16[128,1024]{1,0:T(8,128)(2,1)S(1)}) custom-call(s32[5]{0:T(128)S(1)} %pad_add_fusion.scal, f32[8,128,128]{2,1,0:T(8,128)S(1)} %bitcast.30, bf16[128,1024]{1,0:T(8,128)(2,1)S(1)} %bitcast.28, bf16[128,1024]{1,0:T(8,128)(2,1)S(1)} %bitcast.31, f32[1,1024]{1,0:T(1,128)S(1)} %bitcast.35, ...), custom_call_target="tpu_custom_call" | custom-call | tf_op jit(solution)/shard_map/token_rows/pallas_call | solution.py:415
  131.1 20.4 %all_to_all.36 = bf16[8,128,512]{2,1,0:T(8,128)(2,1)S(1)} all-to-all(bf16[8,128,512]{2,1,0:T(8,128)(2,1)S(1)} %get-tuple-element.33), channel_id=1, replica_groups=mesh['yh'=2,'z'=8,'core'=2,'yl'=2,'x'=4] {'yl','x'}, dimensions={0} | all-to-all | bytes 2097152 | tf_op jit(solution)/shard_map/all_to_all | solution.py:432
  151.5 7.6 %features.1 = (bf16[8,2,64,384]{3,2,1,0:T(8,128)(2,1)S(1)}, f32[16,32,256]{2,1,0:T(8,128)S(1)}, bf16[16,32,256]{2,1,0:T(8,128)(2,1)S(1)}, f32[16,256]{1,0:T(8,128)S(1)}) custom-call(s32[5]{0:T(128)S(1)} %pad_add_fusion.scal, bf16[8,2,64,512]{3,2,1,0:T(8,128)(2,1)S(1)} %bitcast.22, f32[2,512,256]{2,1,0:T(8,128)S(1)} %copy-done.7, ...), custom_call_target="tpu_custom_call" | custom-call | tf_op jit(solution)/shard_map/features/pallas_call | solution.py:434
  159.8 1.0 collective-permute-done.6.gkr_ref
  160.9 20.4 %all_to_all.37.x_ref = bf16[16,48,256]{2,1,0:T(8,128)(2,1)S(1)} all-to-all(bf16[16,48,256]{2,1,0:T(8,128)(2,1)S(1)} %pair_sum.1), channel_id=1, replica_groups=mesh['yh'=2,'z'=8,'core'=2,'yl'=2,'x'=4] {'yh','z'}, dimensions={0} | all-to-all | bytes 786432 | tf_op jit(solution)/shard_map/all_to_all | solution.py:478
  181.3 11.7 %all_to_all.38.x_ref = f32[8,48,256]{2,1,0:T(8,128)} all-to-all(f32[8,48,256]{2,1,0:T(8,128)S(1)} %share_sum.1), channel_id=1, replica_groups=mesh['yh'=2,'z'=8,'core'=2,'yl'=2,'x'=4] {'yl','x'}, dimensions={0} | all-to-all | bytes 786432 | tf_op jit(solution)/shard_map/all_to_all | solution.py:487
  193.0 5.6 %all-to-all-start.4 = ((bf16[8,2,64,384]{3,2,1,0:T(8,128)(2,1)}), bf16[8,2,64,384]{3,2,1,0:T(8,128)(2,1)}, u32[]{:S(2)}, u32[]{:S(2)}) async-start(bf16[8,2,64,384]{3,2,1,0:T(8,128)(2,1)} %copy-done.10), calls=%async_computation.4 | async-start | bytes 1572864 | tf_op jit(solution)/shard_map/all_to_all | solution.py:469
  198.6 1.0 copy-done.5
  200.4 7.0 %all-to-all-done.4 = bf16[8,2,64,384]{3,2,1,0:T(8,128)(2,1)} async-done(((bf16[8,2,64,384]{3,2,1,0:T(8,128)(2,1)}), bf16[8,2,64,384]{3,2,1,0:T(8,128)(2,1)}, u32[]{:S(2)}, u32[]{:S(2)}) %all-to-all-start.4) | async-done | bytes 786464 | tf_op jit(solution)/shard_map/all_to_all | solution.py:469
  209.2 5.6 %result_rows.1 = (bf16[128,1024]{1,0:T(8,128)(2,1)}, bf16[128,1024]{1,0:T(8,128)(2,1)}) custom-call(s32[5]{0:T(128)S(1)} %pad_add_fusion.scal, bf16[8,128,384]{2,1,0:T(8,128)(2,1)} %bitcast.16.a_ref, bf16[128,1024]{1,0:T(8,128)(2,1)S(1)} %copy-done.15, bf16[128,1024]{1,0:T(8,128)(2,1)S(1)} %bitcast.29, bf16[128,1024]{1,0:T(8,128)(2,1)S(1)} %bitcast.32, ...), custom_call_target="tpu_custom_call" | custom-call | tf_op jit(solution)/shard_map/result_rows/pallas_call | solution.py:497
  (66 shorter events, 12.2 us)
Async XLA Ops:
  7.2 70.8 %all-gather.5.cloned.1.call-start = ((), (), s32[]{:S(2)}) async-start(), calls=%async_computation.7 | async-start | bytes 4718592 | tf_op jit(solution)/shard_map/all_gather | solution.py:375
  9.0 8.1 %collective-permute-start = (bf16[32,4096]{1,0:T(8,128)(2,1)S(1)}, bf16[32,4096]{1,0:T(8,128)(2,1)S(1)}, u32[]{:S(2)}, u32[]{:S(2)}) collective-permute-start(bf16[32,4096]{1,0:T(8,128)(2,1)S(1)} %constant_dynamic-update-slice_fusion), channel_id=1, source_target_pairs={{0,132},{132,0},{4,128},{128,4},{1,133},{133,1},{5,129},{129,5},{2... | collective-permute-start | bytes 786440 | tf_op jit(solution)/shard_map/ppermute | solution.py:316
  17.1 30.3 %copy-start.21 = (bf16[32,1024]{1,0:T(8,128)(2,1)S(1)}, bf16[32,1024]{1,0:T(8,128)(2,1)}, u32[]{:S(2)}) copy-start(bf16[32,1024]{1,0:T(8,128)(2,1)} %param.20) | copy-start | bytes 196612
  17.1 30.3 %copy-start.13 = (bf16[32,2048]{1,0:T(8,128)(2,1)S(1)}, bf16[32,2048]{1,0:T(8,128)(2,1)}, u32[]{:S(2)}) copy-start(bf16[32,2048]{1,0:T(8,128)(2,1)} %w_ref.1) | copy-start | bytes 393220
  18.0 29.6 %copy-start.20 = (f32[31,1024]{1,0:T(8,128)S(1)}, f32[31,1024]{1,0:T(8,128)}, u32[]{:S(2)}) copy-start(f32[31,1024]{1,0:T(8,128)} %param.15) | copy-start | bytes 380932
  41.4 27.4 %all-to-all-start = ((bf16[8,128,1024]{2,1,0:T(8,128)(2,1)}), bf16[8,128,1024]{2,1,0:T(8,128)(2,1)S(1)}, u32[]{:S(2)}, u32[]{:S(2)}) async-start(bf16[8,128,1024]{2,1,0:T(8,128)(2,1)} %copy-done.4), calls=%async_computation | async-start | bytes 4194304 | tf_op jit(solution)/shard_map/all_to_all | solution.py:378
  47.3 76.6 %copy-start.3 = (bf16[2,64,1024]{2,1,0:T(8,128)(2,1)S(1)}, bf16[2,64,1024]{2,1,0:T(8,128)(2,1)}, u32[]{:S(2)}) copy-start(bf16[2,64,1024]{2,1,0:T(8,128)(2,1)} %param.11) | copy-start | bytes 786436
  47.3 76.6 %copy-start.8 = (bf16[2,64,1024]{2,1,0:T(8,128)(2,1)S(1)}, bf16[2,64,1024]{2,1,0:T(8,128)(2,1)}, u32[]{:S(2)}) copy-start(bf16[2,64,1024]{2,1,0:T(8,128)(2,1)} %param.21) | copy-start | bytes 786436
  47.3 76.6 %copy-start.18 = (f32[1024]{0:T(1024)S(1)}, f32[1024]{0:T(1024)}, u32[]{:S(2)}) copy-start(f32[1024]{0:T(1024)} %param.16) | copy-start | bytes 12292
  47.3 76.6 %copy-start.19 = (f32[1024]{0:T(1024)S(1)}, f32[1024]{0:T(1024)}, u32[]{:S(2)}) copy-start(f32[1024]{0:T(1024)} %param.18) | copy-start | bytes 12292
  47.4 76.5 %all-gather.7.cloned.1.call-start = ((), (), s32[]{:S(2)}) async-start(), calls=%async_computation.8 | async-start | bytes 3538944 | tf_op jit(solution)/shard_map/all_gather | solution.py:412
  47.5 5.9 %collective-permute-start.2 = (bf16[32,3072]{1,0:T(8,128)(2,1)S(1)}, bf16[32,3072]{1,0:T(8,128)(2,1)}, u32[]{:S(2)}, u32[]{:S(2)}) collective-permute-start(bf16[32,3072]{1,0:T(8,128)(2,1)S(1)} %constant_dynamic-update-slice_fusion.2), channel_id=1, source_target_pairs={{0,132},{132,0},{4,128},{128,4},{1,133},{133,1},{5,129},{129,5},{2... | collective-permute-start | bytes 589832 | tf_op jit(solution)/shard_map/ppermute | solution.py:316
  47.6 7.5 %collective-permute-start.1 = (bf16[16,32,256]{2,1,0:T(8,128)(2,1)S(1)}, bf16[16,32,256]{2,1,0:T(8,128)(2,1)S(1)}, u32[]{:S(2)}, u32[]{:S(2)}) collective-permute-start(bf16[16,32,256]{2,1,0:T(8,128)(2,1)S(1)} %all_to_all.35.wm_ref), channel_id=1, source_target_pairs={{0,8},{8,0},{1,9},{9,1},{2,10},{10,2},{3,11},{11,3},{4,12},{12,4},... | collective-permute-start | bytes 786440 | tf_op jit(solution)/shard_map/ppermute | solution.py:312
  78.0 45.9 %collective-permute-start.3 = (bf16[8,2,32,4096]{3,2,1,0:T(8,128)(2,1)}, bf16[8,2,32,4096]{3,2,1,0:T(8,128)(2,1)}, u32[]{:S(2)}, u32[]{:S(2)}) collective-permute-start(bf16[8,2,32,4096]{3,2,1,0:T(8,128)(2,1)} %bitcast.23), channel_id=1, source_target_pairs={{0,8},{8,0},{1,9},{9,1},{2,10},{10,2},{3,11},{11,3},{4,12},{12,4},... | collective-permute-start | bytes 12582920 | tf_op jit(solution)/shard_map/ppermute | solution.py:312
  78.2 45.7 %all-to-all-start.2 = ((f32[8,2,64,128]{3,2,1,0:T(8,128)}), f32[8,2,64,128]{3,2,1,0:T(8,128)S(1)}, u32[]{:S(2)}, u32[]{:S(2)}) async-start(f32[8,2,64,128]{3,2,1,0:T(8,128)} %copy-done.11), calls=%async_computation.2 | async-start | bytes 1048576 | tf_op jit(solution)/shard_map/all_to_all | solution.py:413
  123.9 83.5 %collective-permute-start.4 = (bf16[8,2,32,3072]{3,2,1,0:T(8,128)(2,1)}, bf16[8,2,32,3072]{3,2,1,0:T(8,128)(2,1)}, u32[]{:S(2)}, u32[]{:S(2)}) collective-permute-start(bf16[8,2,32,3072]{3,2,1,0:T(8,128)(2,1)} %bitcast.25), channel_id=1, source_target_pairs={{0,8},{8,0},{1,9},{9,1},{2,10},{10,2},{3,11},{11,3},{4,12},{12,4},... | collective-permute-start | bytes 9437192 | tf_op jit(solution)/shard_map/ppermute | solution.py:312
  123.9 2.2 copy-start
  126.1 25.4 %copy-start.7 = (f32[2,512,256]{2,1,0:T(8,128)S(1)}, f32[2,512,256]{2,1,0:T(8,128)}, u32[]{:S(2)}) copy-start(f32[2,512,256]{2,1,0:T(8,128)} %copy-done.6) | copy-start | bytes 3145732
  159.2 33.8 %copy-start.10 = (bf16[8,2,64,384]{3,2,1,0:T(8,128)(2,1)}, bf16[8,2,64,384]{3,2,1,0:T(8,128)(2,1)S(1)}, u32[]{:S(2)}) copy-start(bf16[8,2,64,384]{3,2,1,0:T(8,128)(2,1)S(1)} %get-tuple-element.36) | copy-start | bytes 2359300
  159.2 48.2 %copy-start.1 = (bf16[16,32,3072]{2,1,0:T(8,128)(2,1)S(1)}, bf16[16,32,3072]{2,1,0:T(8,128)(2,1)}, u32[]{:S(2)}) copy-start(bf16[16,32,3072]{2,1,0:T(8,128)(2,1)} %all-gather.7.cloned.1.call-done) | copy-start | bytes 9437188
  159.2 48.2 %copy-start.17 = (f32[1024]{0:T(1024)S(1)}, f32[1024]{0:T(1024)}, u32[]{:S(2)}) copy-start(f32[1024]{0:T(1024)} %param.13) | copy-start | bytes 12292
  159.2 1.6 collective-permute-start.5
  159.3 1.5 collective-permute-start.6
  193.0 14.3 %all-to-all-start.4 = ((bf16[8,2,64,384]{3,2,1,0:T(8,128)(2,1)}), bf16[8,2,64,384]{3,2,1,0:T(8,128)(2,1)}, u32[]{:S(2)}, u32[]{:S(2)}) async-start(bf16[8,2,64,384]{3,2,1,0:T(8,128)(2,1)} %copy-done.10), calls=%async_computation.4 | async-start | bytes 1572864 | tf_op jit(solution)/shard_map/all_to_all | solution.py:469
  (10 other events, 9.3 us)
Sparse Core Ops, SparseCore 0:
  18.1 59.8 all-gather.4
  79.8 44.0 all-gather.6

commit v2 on v0

v2 whole, which is shorter than its diff:
```python
import functools

import jax
import jax.numpy as jnp
from jax import lax
from jax.experimental import pallas as pl
from jax.experimental.pallas import tpu as pltpu
from jax.sharding import Mesh
from jax.sharding import PartitionSpec as P

HEADS = 16
EPSILON = 1e-05
BF = jnp.bfloat16
F32 = jnp.float32

DP = ("yh", "z", "core")
CTX = ("yl", "x")

HBM, VMEM, SMEM, ANY = pltpu.HBM, pltpu.VMEM, pltpu.SMEM, pl.ANY


def run(body, outs, ins, name, scratch=(), sems=0, alias=None, mib=36):
    scratch = [pltpu.VMEM(*one) for one in scratch]
    if sems:
        scratch.append(pltpu.SemaphoreType.DMA((sems,)))
    return pl.pallas_call(
        body,
        out_shape=tuple(o[2](o[0], o[1]) for o in outs),
        in_specs=[pl.BlockSpec(memory_space=space) for _, space in ins],
        out_specs=tuple(pl.BlockSpec(memory_space=o[2]) for o in outs),
        scratch_shapes=scratch,
        input_output_aliases=alias or {},
        compiler_params=pltpu.CompilerParams(vmem_limit_bytes=mib << 20),
        name=name,
    )(
        *[
            v if space in (SMEM, ANY) else pltpu.with_memory_space_constraint(v, space)
            for v, space in ins
        ]
    )


class Copies:
    def __init__(self, sems):
        self.sems, self.used = sems, 0

    def start(self, src, dst):
        one = pltpu.make_async_copy(src, dst, self.sems.at[self.used])
        self.used += 1
        one.start()
        return one


def wait(*copies):
    for one in copies:
        one.wait()


def centred(values):
    centre = values - jnp.mean(values, -1, keepdims=True)
    spread = jnp.mean(centre * centre, -1, keepdims=True)
    return centre, lax.rsqrt(spread + EPSILON)


def norm_pull(cot, centre, inv):
    xhat = centre * inv
    return inv * (
        cot - jnp.mean(cot, -1, keepdims=True) - xhat * jnp.mean(cot * xhat, -1, keepdims=True)
    )


def dot(a, b):
    return jnp.dot(a, b, preferred_element_type=F32)


def dot_t(a, b):
    return lax.dot_general(a, b, (((1,), (1,)), ((), ())), preferred_element_type=F32)


def sigmoid(v):
    return jax.nn.sigmoid(v)


def ctx_index():
    return lax.axis_index("yl") * lax.axis_size("x") + lax.axis_index("x")


def lanes(block, width):
    return pl.ds(pl.multiple_of(block * width, width), width)


def cut_body(blocks, w2, wq, w1, own, w1_own, beside, sems):
    model = w2.shape[1]
    width = model // blocks
    ctx = ctx_index()
    copies = Copies(sems)
    going = []
    for dst, block in ((beside, lax.rem(ctx + blocks // 2, blocks)), (own, ctx)):
        going.append(copies.start(w2, dst.at[:, :model]))
        for part in range(3):
            lo = model + part * width
            going.append(
                copies.start(
                    wq.at[:, lanes(part * blocks + block, width)], dst.at[:, lo : lo + width]
                )
            )
        to, lo = (beside, model + 3 * width) if dst is beside else (w1_own, 0)
        for part in range(2):
            at = lo + part * width
            going.append(
                copies.start(
                    w1.at[:, lanes(part * blocks + block, width)], to.at[:, at : at + width]
                )
            )
    wait(*going)


def pack_body(wp, w1, out, sems):
    model = wp.shape[1]
    copies = Copies(sems)
    wait(copies.start(wp, out.at[:, :model]), copies.start(w1, out.at[:, model:]))


def lay_rows(copies, lo, wide, mine, other, out):
    core, yh = lax.axis_index("core"), lax.axis_index("yh")
    return [
        copies.start(src.at[:, slot, :, lo : lo + wide], out.at[side, :, owner])
        for src, owner in ((mine, core), (other, 1 - core))
        for slot, side in ((0, yh), (1, 1 - yh))
    ]


def first_body(x, gain, out, x_s, g_s, n_s, sems):
    copies = Copies(sems)
    wait(copies.start(x, x_s), copies.start(gain, g_s))
    centre, inv = centred(x_s[...].astype(F32))
    n_s[...] = (centre * inv * g_s[...]).astype(BF)
    wait(*[copies.start(n_s, out.at[i]) for i in range(out.shape[0])])


def gate_body(
    taps, frames, x, wm, wo, k, conv, hid, gated, w_s, k_s, pad_s, conv_s, hid_s, gated_s, sems
):
    blocks, records, local, model = x.shape
    length = blocks * local
    width = k_s.shape[1]
    core, yh, z = lax.axis_index("core"), lax.axis_index("yh"), lax.axis_index("z")
    copies = Copies(sems)
    get_k = copies.start(k.at[:, lanes(ctx_index(), width)], k_s)
    for s in range(wm.shape[0]):
        for slot, side in ((0, yh), (1, 1 - yh)):
            w_s[side, z ^ s, core] = wm[s, slot]
            w_s[side, z ^ s, 1 - core] = wo[s, slot]
    zeros = jnp.zeros((16, width), F32)
    pad_s[0:16] = zeros
    pad_s[16 + length : 32 + length] = zeros
    wait(get_k)
    going = []
    for rec in range(records):
        hidden = dot(x[:, rec].reshape(length, model), w_s[...].reshape(model, 2 * width))
        hid_s[rec] = hidden
        here = lax.broadcasted_iota(jnp.int32, (length, width), 0) < frames[rec]
        value = jnp.where(here, hidden[:, :width] * sigmoid(hidden[:, width:]), 0.0).astype(BF)
        gated_s[rec] = value
        pad_s[16 : 16 + length] = value.astype(F32)
        for b in range(blocks):
            total = jnp.zeros((local, width), F32)
            for j in range(taps):
                at = b * local + j + 1
                total = total + k_s[j : j + 1, :] * pad_s[at : at + local, :]
            conv_s[b, rec] = total.astype(BF)
        going.append(copies.start(conv_s.at[:, rec], conv.at[:, rec]))
        going.append(copies.start(hid_s.at[rec], hid.at[rec]))
        going.append(copies.start(gated_s.at[rec], gated.at[rec]))
    wait(*going)


def token_body(
    c, mine, other, x, go, g2, ga, sent, res, gc, w2_s, x_s, go_s, g2_s, ga_s, n_s, res_s, gc_s, sems
):
    rows, model = x_s.shape
    blocks = c.shape[0]
    width = model // blocks
    copies = Copies(sems)
    get_w2 = lay_rows(copies, 0, model, mine, other, w2_s)
    get_gain = copies.start(g2, g2_s)
    get_go = copies.start(go, go_s)
    get_x = copies.start(x, x_s)
    get_ga = copies.start(ga, ga_s)
    conv = jnp.concatenate([c[i] for i in range(blocks)], 1).astype(F32)
    centre, inv = centred(conv)
    wait(get_gain)
    gain = g2_s[...]
    normal = centre * inv * gain
    opening = sigmoid(normal)
    swished = (normal * opening).astype(BF)
    wait(get_go, *get_w2)
    w2 = w2_s[...].reshape(model, model)
    back_two = dot_t(go_s[...], w2)
    slope = opening + normal * opening * (1.0 - opening)
    grad_conv = norm_pull(back_two * slope * gain, centre, inv).astype(BF)
    for i in range(blocks):
        gc_s[i] = grad_conv[:, i * width : (i + 1) * width]
    going = [copies.start(gc_s, gc)]
    wait(get_x, get_ga)
    residual = (x_s[...].astype(F32) + dot(swished, w2)).astype(BF)
    res_s[...] = residual
    going.append(copies.start(res_s, res))
    centre, inv = centred(residual.astype(F32))
    n_s[...] = (centre * inv * ga_s[...]).astype(BF)
    wait(*going, *[copies.start(n_s, sent.at[i]) for i in range(blocks)])


def back_body(
    taps, frames, gc, x, hid, gated, k, back, keep, send, gk_out,
    k_s, hid_s, gated_s, pad_s, gpad_s, gh_s, both_s, gf_s, gk_s, out_s, gko_s, sems,
):
    blocks, records, local, model = x.shape
    length = blocks * local
    rows = records * local
    width = k_s.shape[1]
    core = lax.axis_index("core")
    copies = Copies(sems)
    get_k = copies.start(k.at[:, lanes(ctx_index(), width)], k_s)
    get_gated = copies.start(gated, gated_s)
    get_hid = copies.start(hid, hid_s)
    gk_s[...] = jnp.zeros_like(gk_s)
    zeros = jnp.zeros((16, width), F32)
    for ref in (pad_s, gpad_s):
        ref[0:16] = zeros
        ref[16 + length : 32 + length] = zeros
    wait(get_k, get_gated, get_hid)
    for rec in range(records):
        pad_s[16 : 16 + length] = gc[:, rec].reshape(length, width).astype(F32)
        gpad_s[16 : 16 + length] = gated_s[rec].astype(F32)
        for b in range(blocks):
            base = b * local
            total = jnp.zeros((local, width), F32)
            own = pad_s[16 + base : 16 + base + local, :]
            for j in range(taps):
                at = base + taps - j
                total = total + k_s[j : j + 1, :] * pad_s[at : at + local, :]
                at = base + j + 1
                term = (gpad_s[at : at + local, :] * own).reshape(local // 8, 8, width)
                gk_s[j] += jnp.sum(term, 0)
            at = lax.broadcasted_iota(jnp.int32, (local, width), 0) + base
            grad_gated = jnp.where(at < frames[rec], total, 0.0)
            linear = hid_s[rec, base : base + local, :width]
            opening = sigmoid(hid_s[rec, base : base + local, width:])
            first = grad_gated * opening
            second = (first * linear * (1.0 - opening)).astype(BF)
            first = first.astype(BF)
            gh_s[base : base + local, :width] = first
            gh_s[base : base + local, width:] = second
            out_s[b, rec * local : (rec + 1) * local] = first
            out_s[b, rows + rec * local : rows + (rec + 1) * local] = second
        grad_first = lax.dot_general(
            x[:, rec].reshape(length, model),
            gh_s[...],
            (((0,), (0,)), ((), ())),
            preferred_element_type=F32,
        ).reshape(gf_s.shape)
        if rec == 0:
            gf_s[...] = grad_first
        else:
            both_s[...] = (gf_s[...] + grad_first).astype(BF)
    gk = jnp.sum(gk_s[...], 1)
    half = gko_s.shape[0]
    gko_s[:, :width] = gk[:half]
    gko_s[:, width:] = gk[half:]
    wait(
        copies.start(both_s.at[:, :, 1 - core], send),
        copies.start(gko_s, gk_out),
        copies.start(both_s.at[:, :, core], keep),
        copies.start(out_s, back.at[:, : 2 * rows]),
    )


def pair_body(keep, recv, gk, gkr, *refs):
    zs = len(refs) - 5
    outs, (keep_s, gk_s, both_s, out_s, sems) = refs[:zs], refs[zs:]
    depth, wide = keep_s.shape[2:]
    half = wide // 2
    copies = Copies(sems)
    wait(copies.start(keep, keep_s), copies.start(gk, gk_s))
    both_s[...] = (keep_s[...].astype(F32) + recv[...].astype(F32)).astype(BF)
    gk_sum = (gk_s[...] + gkr[...]).astype(BF)
    tall = out_s.shape[2] // 2
    z = lax.axis_index("z")
    going = []
    for s in range(zs):
        for side in range(2):
            part = both_s[side, z ^ s]
            for h in range(2):
                at = h * tall
                out_s[s, side, at : at + depth] = part[:, h * half : (h + 1) * half]
                out_s[s, side, at + depth : at + tall] = gk_sum[:, h * half : (h + 1) * half]
        going.append(copies.start(out_s.at[s], outs[s]))
    wait(*going)


def sum_body(*refs):
    keep, send, own_s, total_s, sems = refs[-5:]
    copies = Copies(sems)
    get_own = copies.start(refs[0], own_s)
    total = refs[1][...].astype(F32)
    for ref in refs[2:-5]:
        total = total + ref[...].astype(F32)
    wait(get_own)
    total_s[...] = (total + own_s[...].astype(F32)).astype(BF)
    yh = lax.axis_index("yh")
    wait(copies.start(total_s.at[1 - yh], send), copies.start(total_s.at[yh], keep))


def heads_body(head_dim, frames, x, mine, other, held, back, w, att_s, sems):
    del held
    copies = Copies(sems)
    get_w = lay_rows(copies, x.shape[3], w.shape[4], mine, other, w)
    blocks, records, local, model = x.shape
    length = blocks * local
    width = model // blocks
    rows = min(256, length)
    lane = lax.broadcasted_iota(jnp.int32, (rows, width), 1)
    scaling = head_dim**-0.5
    wait(*get_w)
    for rec in range(records):
        packed = dot(x[:, rec].reshape(length, model), w[...].reshape(model, 3 * width))
        packed = packed.astype(BF)
        q = packed[:, :width]
        k = packed[:, width : 2 * width]
        v = packed[:, 2 * width :]
        key_ok = lax.broadcasted_iota(jnp.int32, (rows, length), 1) < frames[rec]
        for r in range(0, length, rows):
            qr = q[r : r + rows]
            attended = jnp.zeros((rows, width), F32)
            for h in range(width // head_dim):
                here = (lane >= h * head_dim) & (lane < (h + 1) * head_dim)
                scores = dot_t(jnp.where(here, qr, jnp.zeros_like(qr)), k) * scaling
                scores = jnp.where(key_ok, scores, -1e30)
                top = jnp.max(scores, -1, keepdims=True)
                numer = jnp.where(key_ok, jnp.exp(scores - top), 0.0)
                denom = jnp.sum(numer, -1, keepdims=True)
                attended = jnp.where(here, dot(numer.astype(BF), v) / denom, attended)
            got = attended.astype(BF).reshape(rows // local, local, width)
            att_s[r // local : (r + rows) // local, rec * local : (rec + 1) * local] = got
    tall = records * local
    wait(copies.start(att_s, back.at[:, 2 * tall : 3 * tall]))


def fill_body(keep, recv, held, back, sems):
    del held
    copies = Copies(sems)
    tall = keep.shape[0]
    base = back.shape[1] - 2 * tall
    going = []
    for i in range(back.shape[0]):
        going.append(copies.start(keep, back.at[i, base : base + tall]))
        going.append(copies.start(recv, back.at[i, base + tall : base + 2 * tall]))
    wait(*going)


def last_body(
    frames, a, mine, other, res, x, go, g1, out, gin, gf, gk,
    wp_s, w1_s, w2_s, res_s, x_s, go_s, g1_s, out_s, gin_s, gf_s, gk_s, sems,
):
    rows, model = x_s.shape
    blocks = a.shape[0]
    width = model // blocks
    depth, taps = gf_s.shape[0], gk_s.shape[0]
    copies = Copies(sems)
    get_w = [
        lay_rows(copies, i * model, model, mine, other, one)
        for i, one in enumerate((wp_s, w1_s, w2_s))
    ]
    get_res = copies.start(res, res_s)
    get_x = copies.start(x, x_s)
    get_go = copies.start(go, go_s)
    get_g1 = copies.start(g1, g1_s)
    tall = (a.shape[1] - 3 * rows) // 4
    base = 3 * rows
    half = tall - depth
    for i in range(blocks):
        lo = i * width
        for h in range(2):
            at = base + h * tall
            far = at + 2 * tall
            total = a[i, at : at + tall].astype(F32) + a[
                (i + blocks // 2) % blocks, far : far + tall
            ].astype(F32)
            gf_s[:, h * model + lo : h * model + lo + width] = total[:depth]
            count = min(half, taps - h * half)
            gk_s[h * half : h * half + count, lo : lo + width] = total[depth : depth + count]
    going = [copies.start(gf_s, gf), copies.start(gk_s, gk)]
    attended = jnp.concatenate([a[i, 2 * rows : 3 * rows] for i in range(blocks)], 1)
    wait(*get_w[0])
    projected = dot(attended, wp_s[...].reshape(model, model))
    records = frames.shape[0]
    local = rows // records
    at = lax.broadcasted_iota(jnp.int32, (local, model), 0) + ctx_index() * local
    present = jnp.concatenate([(at < frames[r]).astype(F32) for r in range(records)], 0)
    wait(get_res)
    out_s[...] = (res_s[...].astype(F32) + present * projected).astype(BF)
    going.append(copies.start(out_s, out))
    linear = jnp.concatenate([a[i, :rows] for i in range(blocks)], 1)
    gating = jnp.concatenate([a[i, rows : 2 * rows] for i in range(blocks)], 1)
    wait(*get_w[1])
    back_one = dot_t(linear, w1_s[...].reshape(model, model))
    wait(*get_w[2])
    back_one = back_one + dot_t(gating, w2_s[...].reshape(model, model))
    wait(get_x, get_go, get_g1)
    centre, inv = centred(x_s[...].astype(F32))
    pulled = norm_pull(back_one * g1_s[...], centre, inv)
    gin_s[...] = (go_s[...].astype(F32) + pulled).astype(BF)
    going.append(copies.start(gin_s, gin))
    wait(*going)


def swap_core(v):
    return lax.ppermute(v, "core", [(0, 1), (1, 0)])


def swap_yh(v):
    return lax.ppermute(v, ("yh", "yl"), [(0, 3), (3, 0), (1, 2), (2, 1)])


def pair_z(v, by):
    return lax.ppermute(v, "z", [(i, i ^ by) for i in range(lax.axis_size("z"))])


def local(
    inputs,
    frames,
    gain_first,
    w_first,
    depth_kernel,
    gain_second,
    w_second,
    gain_attn,
    w_qkv,
    w_proj,
    grad_out,
):
    records, local_len, model = inputs.shape
    taps = depth_kernel.shape[0]
    blocks = lax.axis_size(CTX)
    zs = lax.axis_size("z")
    depth = w_first.shape[0]
    width = model // blocks
    length = blocks * local_len
    rows = records * local_len
    head_dim = model // HEADS
    barrier = lax.optimization_barrier
    x = inputs.reshape(rows, model)
    cot = grad_out.reshape(rows, model)
    gains = [g.reshape(1, model) for g in (gain_first, gain_second, gain_attn)]

    part = model + 3 * width
    own, w1_own, beside = run(
        functools.partial(cut_body, blocks),
        [
            ((depth, part), BF, HBM),
            ((depth, 2 * width), BF, HBM),
            ((depth, part + 2 * width), BF, HBM),
        ],
        [(w_second, HBM), (w_qkv, HBM), (w_first, HBM)],
        "cut",
        sems=12,
    )
    beside = swap_yh(beside)
    (sent,) = run(
        first_body,
        [((blocks, rows, model), BF, HBM)],
        [(x, HBM), (gains[0], HBM)],
        "first_norm",
        [((rows, model), BF), ((1, model), F32), ((rows, model), BF)],
        blocks + 2,
    )
    beside, sent = barrier((beside, sent))
    shard_a = jnp.stack([own, beside[:, :part]])
    all_a = lax.all_gather(shard_a, "z", axis=0, tiled=False)
    normed = lax.all_to_all(sent, CTX, 0, 0, tiled=True).reshape(blocks, records, local_len, model)

    w1_part = jnp.stack([w1_own, beside[:, part:]])
    two = jnp.stack([w1_part, pair_z(w1_part, 1)])
    w1_mine = jnp.concatenate([two] + [pair_z(two, s) for s in range(2, zs, 2)])
    w1_other = swap_core(w1_mine)

    (own_b,) = run(
        pack_body,
        [((depth, 3 * model), BF, HBM)],
        [(w_proj, HBM), (w_first, HBM)],
        "pack",
        sems=2,
    )
    shard_b = jnp.stack([own_b, swap_yh(own_b)])

    conv, hidden, gated = run(
        functools.partial(gate_body, taps),
        [
            ((blocks, records, local_len, width), BF, HBM),
            ((records, length, 2 * width), F32, HBM),
            ((records, length, width), BF, HBM),
        ],
        [(frames, SMEM), (normed, VMEM), (w1_mine, VMEM), (w1_other, VMEM), (depth_kernel, HBM)],
        "gate_conv",
        [
            ((2, zs, 2, depth, 2 * width), BF),
            ((taps, width), F32),
            ((length + 32, width), F32),
            ((blocks, records, local_len, width), BF),
            ((records, length, 2 * width), F32),
            ((records, length, width), BF),
        ],
        1 + 3 * records,
    )

    conv_rows = lax.all_to_all(conv, CTX, 0, 0, tiled=True).reshape(blocks, rows, width)
    all_a, conv_rows = barrier((all_a, conv_rows))
    other_a = swap_core(all_a)
    shard_b, all_a = barrier((shard_b, all_a))
    all_b = lax.all_gather(shard_b, "z", axis=0, tiled=False)

    sent, residual, grad_conv = run(
        token_body,
        [
            ((blocks, rows, model), BF, HBM),
            ((rows, model), BF, HBM),
            ((blocks, rows, width), BF, HBM),
        ],
        [
            (conv_rows, VMEM), (all_a, HBM), (other_a, ANY), (x, HBM), (cot, HBM), (gains[1], HBM),
            (gains[2], HBM),
        ],
        "token_rows",
        [
            ((2, zs, 2, depth, model), BF),
            ((rows, model), BF),
            ((rows, model), BF),
            ((1, model), F32),
            ((1, model), F32),
            ((rows, model), BF),
            ((rows, model), BF),
            ((blocks, rows, width), BF),
        ],
        blocks + 10,
    )
    grad_conv = lax.all_to_all(grad_conv, CTX, 0, 0, tiled=True)
    sent, grad_conv = barrier((sent, grad_conv))
    grad_conv = grad_conv.reshape(blocks, records, local_len, width)
    attn_in = lax.all_to_all(sent, CTX, 0, 0, tiled=True)
    attn_in = attn_in.reshape(blocks, records, local_len, model)

    tall = depth + 16
    half_share = (2, zs, depth, 2 * width)
    back, keep, send, gk = run(
        functools.partial(back_body, taps),
        [
            ((blocks, 3 * rows + 4 * tall, width), BF, HBM),
            (half_share, BF, HBM),
            (half_share, BF, HBM),
            ((16, 2 * width), F32, HBM),
        ],
        [
            (frames, SMEM), (grad_conv, VMEM), (normed, VMEM), (hidden, HBM), (gated, HBM),
            (depth_kernel, HBM),
        ],
        "conv_back",
        [
            ((taps, width), F32),
            ((records, length, 2 * width), F32),
            ((records, length, width), BF),
            ((length + 32, width), F32),
            ((length + 32, width), F32),
            ((length, 2 * width), BF),
            ((2, zs, 2, depth, 2 * width), BF),
            ((2, zs, 2, depth, 2 * width), F32),
            ((32, 8, width), F32),
            ((blocks, 2 * rows, width), BF),
            ((16, 2 * width), F32),
        ],
        7,
    )

    chunk = (2, 2 * tall, width)
    chunks = run(
        pair_body,
        [(chunk, BF, HBM)] * zs,
        [(keep, HBM), (swap_core(send), VMEM), (gk, HBM), (swap_core(gk), VMEM)],
        "pair_sum",
        [
            (half_share, BF),
            ((16, 2 * width), F32),
            (half_share, BF),
            ((zs,) + chunk, BF),
        ],
        zs + 2,
    )
    sums = [chunks[0]] + [pair_z(chunks[s], s) for s in range(1, zs)]
    keep, send = run(
        sum_body,
        [(chunk[1:], BF, HBM)] * 2,
        [(sums[0], HBM)] + [(one, VMEM) for one in sums[1:]],
        "share_sum",
        [(chunk, BF), (chunk, BF)],
        3,
    )
    attn_in, keep, send = barrier((attn_in, keep, send))
    recv = swap_yh(send)

    (back,) = run(
        functools.partial(heads_body, head_dim),
        [(back.shape, BF, HBM)],
        [(frames, SMEM), (attn_in, VMEM), (all_a, HBM), (other_a, ANY), (back, HBM)],
        "heads",
        [((2, zs, 2, depth, 3 * width), BF), ((blocks, rows, width), BF)],
        5,
        {4: 0},
    )
    (back,) = run(
        fill_body,
        [(back.shape, BF, HBM)],
        [(keep, HBM), (recv, ANY), (back, HBM)],
        "fill",
        sems=2 * blocks,
        alias={2: 0},
    )
    all_b, back = barrier((all_b, back))
    other_b = swap_core(all_b)
    back = lax.all_to_all(back, CTX, 0, 0, tiled=True)
    result, grad_in, grad_first, grad_kernel = run(
        last_body,
        [
            ((rows, model), BF, HBM),
            ((rows, model), BF, HBM),
            ((depth, 2 * model), F32, HBM),
            ((taps, model), F32, HBM),
        ],
        [
            (frames, SMEM), (back, VMEM), (all_b, HBM), (other_b, ANY), (residual, HBM), (x, HBM),
            (cot, HBM), (gains[0], HBM),
        ],
        "result_rows",
        [
            ((2, zs, 2, depth, model), BF),
            ((2, zs, 2, depth, model), BF),
            ((2, zs, 2, depth, model), BF),
            ((rows, model), BF),
            ((rows, model), BF),
            ((rows, model), BF),
            ((1, model), F32),
            ((rows, model), BF),
            ((rows, model), BF),
            ((depth, 2 * model), F32),
            ((taps, model), F32),
        ],
        20,
    )
    return (
        result.reshape(records, local_len, model),
        grad_in.reshape(records, local_len, model),
        grad_first,
        grad_kernel,
    )


def solution(mesh):
    dp, ctx = mesh.devices.shape
    split = Mesh(
        mesh.devices.reshape(2, dp // 4, 2, 2, ctx // 2), ("yh", "z", "core", "yl", "x")
    )
    tokens = P(DP, CTX, None)
    placed = (
        tokens,
        P(DP),
        P(),
        P(DP, None),
        P(),
        P(),
        P(DP, None),
        P(),
        P(DP, None),
        P(DP, None),
        tokens,
    )
    return jax.shard_map(
        local,
        mesh=split,
        in_specs=placed,
        out_specs=(tokens, tokens, P(DP, None), P()),
        check_vma=False,
    )
```

time: 929 us -> 185 us (0.20)
  waiting for transfers between devices: 785 us -> 26.5 us
  Pallas kernels: 0 us -> 56.2 us
  matrix products: 54.7 us -> 0 us
  blocking collectives: 0 us -> 34.2 us
  local copies, waits for them, and re-layouts: 34.5 us -> 2.66 us
  starting transfers between devices: 16.4 us -> 47 us
  other arithmetic: 22.4 us -> 1.49 us
    all_gather x6 -> x2, waiting for transfers between devices: 350 us -> 0.02 us  [the longest x1 0.02 us: local(): all_b = lax.all_gather(shard_b, 'z', axis=0, tiled=False)]
    psum x2 -> x0, waiting for transfers between devices: 307 us -> none  [the longest x1 243 us: local(): grad_kernel = lax.psum(kernel_term, ('dp', 'ctx'))]
    reduce_scatter x1 -> x0, waiting for transfers between devices: 121 us -> none  [local(): lax.psum_scatter(jnp.dot(normed.T, grad_hidden, preferred_element_type=jn...]
    pallas_call x0 -> x11, Pallas kernels: none -> 56.2 us  [run(): pl.pallas_call(body, out_shape=tuple((o[2](o[0], o[1]) for o in outs)), i...]
    dot_general x39 -> x0, matrix products: 54.7 us -> none  [the longest x16 28.5 us: per_head(): jnp.einsum('rqk,rke->rqe', numerator.astype(jnp.bfloat16), value_h, prefe...]
    all_to_all x0 -> x2, blocking collectives: none -> 34.2 us  [the longest x1 22.3 us: local(): back = lax.all_to_all(back, CTX, 0, 0, tiled=True)]
    all_to_all x0 -> x3, starting transfers between devices: none -> 19.5 us  [the longest x1 6.93 us: local(): lax.all_to_all(sent, CTX, 0, 0, tiled=True)]
    all_gather x2 -> x0, local copies, waits for them, and re-layouts: 19.5 us -> none  [the longest x1 10.5 us: local(): lax.all_gather(packed[:, :, 2], 'ctx', axis=1, tiled=True)]
  transfers between devices with their start and end apart: 13 -> 24, of which waited for: 12 -> 10; matrix products, arithmetic and copies ran while one was open for 12% -> 0% of each run, Pallas kernels for 0% -> 23%
where the time goes in v2:
time: 185 us; the launch traced here: 182 us
  Pallas kernels  56.2 us (30%)
  starting transfers between devices  47 us (25%)
  blocking collectives  34.2 us (18%)
  waiting for transfers between devices  26.5 us (14%)
  between operations  14.3 us (8%)
  local copies, waits for them, and re-layouts  2.66 us (1%)
    pallas_call x11, Pallas kernels, run(): pl.pallas_call(body, out_shape=tuple((o[2](o[0], o[1]) for o in outs)), i...  56.2 us
    ppermute x11, starting transfers between devices, pair_z(): lax.ppermute(v, 'z', [(i, i ^ by) for i in range(lax.axis_size('z'))])  22.7 us
    all_to_all x1, blocking collectives, local(): back = lax.all_to_all(back, CTX, 0, 0, tiled=True)  22.3 us
    ppermute x11, waiting for transfers between devices, pair_z(): lax.ppermute(v, 'z', [(i, i ^ by) for i in range(lax.axis_size('z'))])  15.7 us
    all_to_all x1, blocking collectives, local(): grad_conv = lax.all_to_all(grad_conv, CTX, 0, 0, tiled=True)  11.9 us
    all_to_all x1, starting transfers between devices, local(): lax.all_to_all(sent, CTX, 0, 0, tiled=True)  6.93 us
    all_to_all x1, starting transfers between devices, local(): lax.all_to_all(conv, CTX, 0, 0, tiled=True).reshape(blocks, rows, width)  6.87 us
    all_to_all x1, starting transfers between devices, local(): attn_in = lax.all_to_all(sent, CTX, 0, 0, tiled=True)  5.73 us
  transfers between devices with their start and end apart: 24, of which 10 were waited for; matrix products, arithmetic and copies ran while one was open for 0% of the time, Pallas kernels for 23%

profile of v2, /device:TPU:8, one launch (start us, length us, event | category | flops | bytes accessed | tf_op | source)
XLA Modules:
  0.0 182.3 jit_solution(8120431343885521534)
XLA Ops:
  7.2 7.7 %cut.1 = (bf16[32,1408]{1,0:T(8,128)(2,1)}, bf16[32,256]{1,0:T(8,128)(2,1)}, bf16[32,1664]{1,0:T(8,128)(2,1)}) custom-call(bf16[32,1024]{1,0:T(8,128)(2,1)} %w2.1, bf16[32,3072]{1,0:T(8,128)(2,1)} %wq.1, bf16[32,2048]{1,0:T(8,128)(2,1)} %w1.3), custom_call_target="tpu_custom_call" | custom-call | tf_op jit(solution)/shard_map/cut/pallas_call | solution.py:26
  16.6 2.6 %first_norm.1 = bf16[8,128,1024]{2,1,0:T(8,128)(2,1)} custom-call(bf16[128,1024]{1,0:T(8,128)(2,1)} %bitcast.35, f32[1,1024]{1,0:T(1,128)} %bitcast.46), custom_call_target="tpu_custom_call" | custom-call | tf_op jit(solution)/shard_map/first_norm/pallas_call | solution.py:26
  20.7 6.9 %all-to-all-start = ((bf16[8,128,1024]{2,1,0:T(8,128)(2,1)}), bf16[8,128,1024]{2,1,0:T(8,128)(2,1)S(1)}, u32[]{:S(2)}, u32[]{:S(2)}) async-start(bf16[8,128,1024]{2,1,0:T(8,128)(2,1)} %first_norm.1), calls=%async_computation | async-start | bytes 4194304 | tf_op jit(solution)/shard_map/all_to_all | solution.py:481
  28.7 2.9 %collective-permute-done.2 = bf16[2,32,256]{2,1,0:T(8,128)(2,1)S(1)} collective-permute-done((bf16[2,32,256]{2,1,0:T(8,128)(2,1)S(1)}, bf16[2,32,256]{2,1,0:T(8,128)(2,1)S(1)}, u32[]{:S(2)}, u32[]{:S(2)}) %collective-permute-start.2) | collective-permute-done | bytes 32800 | tf_op jit(solution)/shard_map/ppermute | solution.py:427
  31.6 2.5 %collective-permute-start.3 = (bf16[2,2,32,256]{3,2,1,0:T(8,128)(2,1)S(1)}, bf16[2,2,32,256]{3,2,1,0:T(8,128)(2,1)S(1)}, u32[]{:S(2)}, u32[]{:S(2)}) collective-permute-start(bf16[2,2,32,256]{3,2,1,0:T(8,128)(2,1)S(1)} %pad_maximum_fusion.2), channel_id=1, source_target_pairs={{0,32},{16,48},{32,0},{48,16},{64,96},{80,112},{96,64},{112,80},{1... | collective-permute-start | bytes 196616 | tf_op jit(solution)/shard_map/ppermute | solution.py:427
  34.1 5.4 %collective-permute-start.4 = (bf16[2,2,32,256]{3,2,1,0:T(8,128)(2,1)S(1)}, bf16[2,2,32,256]{3,2,1,0:T(8,128)(2,1)S(1)}, u32[]{:S(2)}, u32[]{:S(2)}) collective-permute-start(bf16[2,2,32,256]{3,2,1,0:T(8,128)(2,1)S(1)} %pad_maximum_fusion.2), channel_id=1, source_target_pairs={{0,64},{16,80},{32,96},{48,112},{64,0},{80,16},{96,32},{112,48},{1... | collective-permute-start | bytes 196616 | tf_op jit(solution)/shard_map/ppermute | solution.py:427
  39.5 6.4 %collective-permute-done.4 = bf16[2,2,32,256]{3,2,1,0:T(8,128)(2,1)S(1)} collective-permute-done((bf16[2,2,32,256]{3,2,1,0:T(8,128)(2,1)S(1)}, bf16[2,2,32,256]{3,2,1,0:T(8,128)(2,1)S(1)}, u32[]{:S(2)}, u32[]{:S(2)}) %collective-permute-start.4) | collective-permute-done | bytes 65568 | tf_op jit(solution)/shard_map/ppermute | solution.py:427
  47.3 7.1 %pack.1 = bf16[32,3072]{1,0:T(8,128)(2,1)} custom-call(bf16[32,1024]{1,0:T(8,128)(2,1)} %wp.1, bf16[32,2048]{1,0:T(8,128)(2,1)} %w1.3), custom_call_target="tpu_custom_call" | custom-call | tf_op jit(solution)/shard_map/pack/pallas_call | solution.py:26
  56.4 4.4 %gate_conv.1 = (bf16[8,2,64,128]{3,2,1,0:T(8,128)(2,1)}, f32[2,512,256]{2,1,0:T(8,128)}, bf16[2,512,128]{2,1,0:T(8,128)(2,1)}) custom-call(s32[2]{0:T(128)S(1)} %copy-done.3, bf16[8,2,64,1024]{3,2,1,0:T(8,128)(2,1)S(1)} %bitcast.26, bf16[8,2,32,256]{3,2,1,0:T(8,128)(2,1)S(1)} %constant_dynamic-update-slice_fusion.wm, ...), custom_call_target="tpu_custom_call" | custom-call | tf_op jit(solution)/shard_map/gate_conv/pallas_call | solution.py:26
  60.8 6.9 %all-to-all-start.1 = ((bf16[8,2,64,128]{3,2,1,0:T(8,128)(2,1)}), bf16[8,2,64,128]{3,2,1,0:T(8,128)(2,1)S(1)}, u32[]{:S(2)}, u32[]{:S(2)}) async-start(bf16[8,2,64,128]{3,2,1,0:T(8,128)(2,1)} %get-tuple-element.49), calls=%async_computation.1 | async-start | bytes 524288 | tf_op jit(solution)/shard_map/all_to_all | solution.py:517
  68.4 5.4 %all-to-all-done.1 = bf16[8,2,64,128]{3,2,1,0:T(8,128)(2,1)S(1)} async-done(((bf16[8,2,64,128]{3,2,1,0:T(8,128)(2,1)}), bf16[8,2,64,128]{3,2,1,0:T(8,128)(2,1)S(1)}, u32[]{:S(2)}, u32[]{:S(2)}) %all-to-all-start.1) | async-done | bytes 262176 | tf_op jit(solution)/shard_map/all_to_all | solution.py:517
  74.7 3.4 %collective-permute-done.7.other = bf16[8,2,32,1408]{3,2,1,0:T(8,128)(2,1)S(1)} collective-permute-done((bf16[8,2,32,1408]{3,2,1,0:T(8,128)(2,1)}, bf16[8,2,32,1408]{3,2,1,0:T(8,128)(2,1)S(1)}, u32[]{:S(2)}, u32[]{:S(2)}) %collective-permute-start.7) | collective-permute-done | bytes 1441824 | tf_op jit(solution)/shard_map/ppermute | solution.py:419
  79.0 4.5 %token_rows.1 = (bf16[8,128,1024]{2,1,0:T(8,128)(2,1)}, bf16[128,1024]{1,0:T(8,128)(2,1)}, bf16[8,128,128]{2,1,0:T(8,128)(2,1)}) custom-call(bf16[8,128,128]{2,1,0:T(8,128)(2,1)S(1)} %bitcast.28, bf16[8,2,32,1408]{3,2,1,0:T(8,128)(2,1)} %bitcast.31, bf16[8,2,32,1408]{3,2,1,0:T(8,128)(2,1)S(1)} %collective-permute-done.7.other, bf16[128,1024]{1,0:T(8,128)(2,1)} %bitcast.36, ...), custom_call_target="tpu_custom_call" | custom-call | tf_op jit(solution)/shard_map/token_rows/pallas_call | solution.py:26
  83.5 11.9 %all_to_all.25 = bf16[8,128,128]{2,1,0:T(8,128)(2,1)} all-to-all(bf16[8,128,128]{2,1,0:T(8,128)(2,1)} %get-tuple-element.55), channel_id=1, replica_groups=mesh['yh'=2,'z'=8,'core'=2,'yl'=2,'x'=4] {'yl','x'}, dimensions={0} | all-to-all | bytes 524288 | tf_op jit(solution)/shard_map/all_to_all | solution.py:547
  95.4 5.7 %all-to-all-start.3 = ((bf16[8,128,1024]{2,1,0:T(8,128)(2,1)}), bf16[8,128,1024]{2,1,0:T(8,128)(2,1)}, u32[]{:S(2)}, u32[]{:S(2)}) async-start(bf16[8,128,1024]{2,1,0:T(8,128)(2,1)} %get-tuple-element.56), calls=%async_computation.3 | async-start | bytes 4194304 | tf_op jit(solution)/shard_map/all_to_all | solution.py:550
  102.1 6.3 %conv_back.1 = (bf16[8,576,128]{2,1,0:T(8,128)(2,1)}, bf16[2,8,32,256]{3,2,1,0:T(8,128)(2,1)}, bf16[2,8,32,256]{3,2,1,0:T(8,128)(2,1)}, f32[16,256]{1,0:T(8,128)}) custom-call(s32[2]{0:T(128)S(1)} %copy-done.3, bf16[8,2,64,128]{3,2,1,0:T(8,128)(2,1)S(1)} %bitcast.29, bf16[8,2,64,1024]{3,2,1,0:T(8,128)(2,1)S(1)} %bitcast.27, ...), custom_call_target="tpu_custom_call" | custom-call | tf_op jit(solution)/shard_map/conv_back/pallas_call | solution.py:26
  112.1 2.1 %collective-permute-start.10 = (bf16[2,96,128]{2,1,0:T(8,128)(2,1)}, bf16[2,96,128]{2,1,0:T(8,128)(2,1)S(1)}, u32[]{:S(2)}, u32[]{:S(2)}) collective-permute-start(bf16[2,96,128]{2,1,0:T(8,128)(2,1)} %get-tuple-element.64), channel_id=1, source_target_pairs={{0,16},{16,0},{32,48},{48,32},{64,80},{80,64},{96,112},{112,96},{1... | collective-permute-start | bytes 147464 | tf_op jit(solution)/shard_map/ppermute | solution.py:427
  116.7 3.5 %collective-permute-start.13 = (bf16[2,96,128]{2,1,0:T(8,128)(2,1)}, bf16[2,96,128]{2,1,0:T(8,128)(2,1)S(1)}, u32[]{:S(2)}, u32[]{:S(2)}) collective-permute-start(bf16[2,96,128]{2,1,0:T(8,128)(2,1)} %get-tuple-element.67), channel_id=1, source_target_pairs={{0,64},{16,80},{32,96},{48,112},{64,0},{80,16},{96,32},{112,48},{1... | collective-permute-start | bytes 147464 | tf_op jit(solution)/shard_map/ppermute | solution.py:427
  123.2 2.6 %collective-permute-start.16 = (bf16[2,96,128]{2,1,0:T(8,128)(2,1)}, bf16[2,96,128]{2,1,0:T(8,128)(2,1)S(1)}, u32[]{:S(2)}, u32[]{:S(2)}) collective-permute-start(bf16[2,96,128]{2,1,0:T(8,128)(2,1)} %get-tuple-element.70), channel_id=1, source_target_pairs={{0,112},{16,96},{32,80},{48,64},{64,48},{80,32},{96,16},{112,0},{1... | collective-permute-start | bytes 147464 | tf_op jit(solution)/shard_map/ppermute | solution.py:427
  128.6 2.3 %collective-permute-done.16.refs_7_ = bf16[2,96,128]{2,1,0:T(8,128)(2,1)S(1)} collective-permute-done((bf16[2,96,128]{2,1,0:T(8,128)(2,1)}, bf16[2,96,128]{2,1,0:T(8,128)(2,1)S(1)}, u32[]{:S(2)}, u32[]{:S(2)}) %collective-permute-start.16) | collective-permute-done | bytes 49184 | tf_op jit(solution)/shard_map/ppermute | solution.py:427
  132.6 7.3 %heads.1.held = bf16[8,576,128]{2,1,0:T(8,128)(2,1)} custom-call(s32[2]{0:T(128)S(1)} %copy-done.3, bf16[8,2,64,1024]{3,2,1,0:T(8,128)(2,1)} %bitcast.17.x, bf16[8,2,32,1408]{3,2,1,0:T(8,128)(2,1)} %bitcast.32, bf16[8,2,32,1408]{3,2,1,0:T(8,128)(2,1)S(1)} %collective-permute-done.7.other, ...), custom_call_target="tpu_custom_call", output_to_operand_aliasing={{}: (4, {})} | custom-call | tf_op jit(solution)/shard_map/heads/pallas_call | solution.py:26
  140.0 7.2 %fill.1 = bf16[8,576,128]{2,1,0:T(8,128)(2,1)} custom-call(bf16[96,128]{1,0:T(8,128)(2,1)} %get-tuple-element.73.keep, bf16[96,128]{1,0:T(8,128)(2,1)S(1)} %collective-permute-done.17.recv, bf16[8,576,128]{2,1,0:T(8,128)(2,1)} %heads.1.held), custom_call_target="tpu_custom_call", output_to_operand_aliasing={{}: (2, {})} | custom-call | tf_op jit(solution)/shard_map/fill/pallas_call | solution.py:26
  147.3 22.3 %all_to_all.26.a = bf16[8,576,128]{2,1,0:T(8,128)(2,1)S(1)} all-to-all(bf16[8,576,128]{2,1,0:T(8,128)(2,1)} %fill.1), channel_id=1, replica_groups=mesh['yh'=2,'z'=8,'core'=2,'yl'=2,'x'=4] {'yl','x'}, dimensions={0} | all-to-all | bytes 2359296 | tf_op jit(solution)/shard_map/all_to_all | solution.py:629
  169.6 5.8 %result_rows.1 = (bf16[128,1024]{1,0:T(8,128)(2,1)}, bf16[128,1024]{1,0:T(8,128)(2,1)}, f32[32,2048]{1,0:T(8,128)}, f32[31,1024]{1,0:T(8,128)}) custom-call(s32[2]{0:T(128)S(1)} %copy-done.3, bf16[8,576,128]{2,1,0:T(8,128)(2,1)S(1)} %all_to_all.26.a, bf16[8,2,32,3072]{3,2,1,0:T(8,128)(2,1)} %bitcast.34, ...), custom_call_target="tpu_custom_call" | custom-call | tf_op jit(solution)/shard_map/result_rows/pallas_call | solution.py:26
  (64 shorter events, 25.1 us)
Async XLA Ops:
  7.2 67.4 %all-gather.5.cloned.1.call-start = ((), (), s32[]{:S(2)}) async-start(), calls=%async_computation.5 | async-start | bytes 1622016 | tf_op jit(solution)/shard_map/all_gather | solution.py:480
  14.9 5.0 %collective-permute-start.1 = (bf16[32,1664]{1,0:T(8,128)(2,1)}, bf16[32,1664]{1,0:T(8,128)(2,1)S(1)}, u32[]{:S(2)}, u32[]{:S(2)}) collective-permute-start(bf16[32,1664]{1,0:T(8,128)(2,1)} %get-tuple-element.45), channel_id=1, source_target_pairs={{0,132},{132,0},{4,128},{128,4},{1,133},{133,1},{5,129},{129,5},{2... | collective-permute-start | bytes 319496 | tf_op jit(solution)/shard_map/ppermute | solution.py:423
  20.7 35.7 %all-to-all-start = ((bf16[8,128,1024]{2,1,0:T(8,128)(2,1)}), bf16[8,128,1024]{2,1,0:T(8,128)(2,1)S(1)}, u32[]{:S(2)}, u32[]{:S(2)}) async-start(bf16[8,128,1024]{2,1,0:T(8,128)(2,1)} %first_norm.1), calls=%async_computation | async-start | bytes 4194304 | tf_op jit(solution)/shard_map/all_to_all | solution.py:481
  27.6 4.0 %collective-permute-start.2 = (bf16[2,32,256]{2,1,0:T(8,128)(2,1)S(1)}, bf16[2,32,256]{2,1,0:T(8,128)(2,1)S(1)}, u32[]{:S(2)}, u32[]{:S(2)}) collective-permute-start(bf16[2,32,256]{2,1,0:T(8,128)(2,1)S(1)} %get-tuple-element.85), channel_id=1, source_target_pairs={{0,16},{16,0},{32,48},{48,32},{64,80},{80,64},{96,112},{112,96},{1... | collective-permute-start | bytes 98312 | tf_op jit(solution)/shard_map/ppermute | solution.py:427
  31.6 7.9 %collective-permute-start.3 = (bf16[2,2,32,256]{3,2,1,0:T(8,128)(2,1)S(1)}, bf16[2,2,32,256]{3,2,1,0:T(8,128)(2,1)S(1)}, u32[]{:S(2)}, u32[]{:S(2)}) collective-permute-start(bf16[2,2,32,256]{3,2,1,0:T(8,128)(2,1)S(1)} %pad_maximum_fusion.2), channel_id=1, source_target_pairs={{0,32},{16,48},{32,0},{48,16},{64,96},{80,112},{96,64},{112,80},{1... | collective-permute-start | bytes 196616 | tf_op jit(solution)/shard_map/ppermute | solution.py:427
  34.1 11.8 %collective-permute-start.4 = (bf16[2,2,32,256]{3,2,1,0:T(8,128)(2,1)S(1)}, bf16[2,2,32,256]{3,2,1,0:T(8,128)(2,1)S(1)}, u32[]{:S(2)}, u32[]{:S(2)}) collective-permute-start(bf16[2,2,32,256]{3,2,1,0:T(8,128)(2,1)S(1)} %pad_maximum_fusion.2), channel_id=1, source_target_pairs={{0,64},{16,80},{32,96},{48,112},{64,0},{80,16},{96,32},{112,48},{1... | collective-permute-start | bytes 196616 | tf_op jit(solution)/shard_map/ppermute | solution.py:427
  39.5 7.8 %collective-permute-start.5 = (bf16[2,2,32,256]{3,2,1,0:T(8,128)(2,1)S(1)}, bf16[2,2,32,256]{3,2,1,0:T(8,128)(2,1)S(1)}, u32[]{:S(2)}, u32[]{:S(2)}) collective-permute-start(bf16[2,2,32,256]{3,2,1,0:T(8,128)(2,1)S(1)} %pad_maximum_fusion.2), channel_id=1, source_target_pairs={{0,96},{16,112},{32,64},{48,80},{64,32},{80,48},{96,0},{112,16},{1... | collective-permute-start | bytes 196616 | tf_op jit(solution)/shard_map/ppermute | solution.py:427
  47.3 9.1 %collective-permute-start.6 = (bf16[8,2,32,256]{3,2,1,0:T(8,128)(2,1)S(1)}, bf16[8,2,32,256]{3,2,1,0:T(8,128)(2,1)S(1)}, u32[]{:S(2)}, u32[]{:S(2)}) collective-permute-start(bf16[8,2,32,256]{3,2,1,0:T(8,128)(2,1)S(1)} %constant_dynamic-update-slice_fusion.wm), channel_id=1, source_target_pairs={{0,8},{8,0},{1,9},{9,1},{2,10},{10,2},{3,11},{11,3},{4,12},{12,4},... | collective-permute-start | bytes 786440 | tf_op jit(solution)/shard_map/ppermute | solution.py:419
  54.4 13.2 %collective-permute-start = (bf16[32,3072]{1,0:T(8,128)(2,1)}, bf16[32,3072]{1,0:T(8,128)(2,1)S(1)}, u32[]{:S(2)}, u32[]{:S(2)}) collective-permute-start(bf16[32,3072]{1,0:T(8,128)(2,1)} %pack.1), channel_id=1, source_target_pairs={{0,132},{132,0},{4,128},{128,4},{1,133},{133,1},{5,129},{129,5},{2... | collective-permute-start | bytes 589832 | tf_op jit(solution)/shard_map/ppermute | solution.py:423
  60.8 13.1 %all-to-all-start.1 = ((bf16[8,2,64,128]{3,2,1,0:T(8,128)(2,1)}), bf16[8,2,64,128]{3,2,1,0:T(8,128)(2,1)S(1)}, u32[]{:S(2)}, u32[]{:S(2)}) async-start(bf16[8,2,64,128]{3,2,1,0:T(8,128)(2,1)} %get-tuple-element.49), calls=%async_computation.1 | async-start | bytes 524288 | tf_op jit(solution)/shard_map/all_to_all | solution.py:517
  67.6 79.6 %all-gather.7.cloned.1.call-start = ((), (), s32[]{:S(2)}) async-start(), calls=%async_computation.6 | async-start | bytes 3538944 | tf_op jit(solution)/shard_map/all_gather | solution.py:521
  74.6 3.5 %collective-permute-start.7 = (bf16[8,2,32,1408]{3,2,1,0:T(8,128)(2,1)}, bf16[8,2,32,1408]{3,2,1,0:T(8,128)(2,1)S(1)}, u32[]{:S(2)}, u32[]{:S(2)}) collective-permute-start(bf16[8,2,32,1408]{3,2,1,0:T(8,128)(2,1)} %bitcast.30), channel_id=1, source_target_pairs={{0,8},{8,0},{1,9},{9,1},{2,10},{10,2},{3,11},{11,3},{4,12},{12,4},... | collective-permute-start | bytes 4325384 | tf_op jit(solution)/shard_map/ppermute | solution.py:419
  95.4 36.9 %all-to-all-start.3 = ((bf16[8,128,1024]{2,1,0:T(8,128)(2,1)}), bf16[8,128,1024]{2,1,0:T(8,128)(2,1)}, u32[]{:S(2)}, u32[]{:S(2)}) async-start(bf16[8,128,1024]{2,1,0:T(8,128)(2,1)} %get-tuple-element.56), calls=%async_computation.3 | async-start | bytes 4194304 | tf_op jit(solution)/shard_map/all_to_all | solution.py:550
  108.4 1.9 %collective-permute-start.8 = (bf16[2,8,32,256]{3,2,1,0:T(8,128)(2,1)}, bf16[2,8,32,256]{3,2,1,0:T(8,128)(2,1)S(1)}, u32[]{:S(2)}, u32[]{:S(2)}) collective-permute-start(bf16[2,8,32,256]{3,2,1,0:T(8,128)(2,1)} %get-tuple-element.61), channel_id=1, source_target_pairs={{0,8},{8,0},{1,9},{9,1},{2,10},{10,2},{3,11},{11,3},{4,12},{12,4},... | collective-permute-start | bytes 786440 | tf_op jit(solution)/shard_map/ppermute | solution.py:419
  108.5 1.8 collective-permute-start.9
  112.1 10.0 %collective-permute-start.10 = (bf16[2,96,128]{2,1,0:T(8,128)(2,1)}, bf16[2,96,128]{2,1,0:T(8,128)(2,1)S(1)}, u32[]{:S(2)}, u32[]{:S(2)}) collective-permute-start(bf16[2,96,128]{2,1,0:T(8,128)(2,1)} %get-tuple-element.64), channel_id=1, source_target_pairs={{0,16},{16,0},{32,48},{48,32},{64,80},{80,64},{96,112},{112,96},{1... | collective-permute-start | bytes 147464 | tf_op jit(solution)/shard_map/ppermute | solution.py:427
  114.2 9.0 %collective-permute-start.11 = (bf16[2,96,128]{2,1,0:T(8,128)(2,1)}, bf16[2,96,128]{2,1,0:T(8,128)(2,1)S(1)}, u32[]{:S(2)}, u32[]{:S(2)}) collective-permute-start(bf16[2,96,128]{2,1,0:T(8,128)(2,1)} %get-tuple-element.65), channel_id=1, source_target_pairs={{0,32},{16,48},{32,0},{48,16},{64,96},{80,112},{96,64},{112,80},{1... | collective-permute-start | bytes 147464 | tf_op jit(solution)/shard_map/ppermute | solution.py:427
  114.8 11.0 %collective-permute-start.12 = (bf16[2,96,128]{2,1,0:T(8,128)(2,1)}, bf16[2,96,128]{2,1,0:T(8,128)(2,1)S(1)}, u32[]{:S(2)}, u32[]{:S(2)}) collective-permute-start(bf16[2,96,128]{2,1,0:T(8,128)(2,1)} %get-tuple-element.66), channel_id=1, source_target_pairs={{0,48},{16,32},{32,16},{48,0},{64,112},{80,96},{96,80},{112,64},{1... | collective-permute-start | bytes 147464 | tf_op jit(solution)/shard_map/ppermute | solution.py:427
  116.7 9.2 %collective-permute-start.13 = (bf16[2,96,128]{2,1,0:T(8,128)(2,1)}, bf16[2,96,128]{2,1,0:T(8,128)(2,1)S(1)}, u32[]{:S(2)}, u32[]{:S(2)}) collective-permute-start(bf16[2,96,128]{2,1,0:T(8,128)(2,1)} %get-tuple-element.67), channel_id=1, source_target_pairs={{0,64},{16,80},{32,96},{48,112},{64,0},{80,16},{96,32},{112,48},{1... | collective-permute-start | bytes 147464 | tf_op jit(solution)/shard_map/ppermute | solution.py:427
  120.1 7.4 %collective-permute-start.14 = (bf16[2,96,128]{2,1,0:T(8,128)(2,1)}, bf16[2,96,128]{2,1,0:T(8,128)(2,1)S(1)}, u32[]{:S(2)}, u32[]{:S(2)}) collective-permute-start(bf16[2,96,128]{2,1,0:T(8,128)(2,1)} %get-tuple-element.68), channel_id=1, source_target_pairs={{0,80},{16,64},{32,112},{48,96},{64,16},{80,0},{96,48},{112,32},{1... | collective-permute-start | bytes 147464 | tf_op jit(solution)/shard_map/ppermute | solution.py:427
  122.2 6.4 %collective-permute-start.15 = (bf16[2,96,128]{2,1,0:T(8,128)(2,1)}, bf16[2,96,128]{2,1,0:T(8,128)(2,1)S(1)}, u32[]{:S(2)}, u32[]{:S(2)}) collective-permute-start(bf16[2,96,128]{2,1,0:T(8,128)(2,1)} %get-tuple-element.69), channel_id=1, source_target_pairs={{0,96},{16,112},{32,64},{48,80},{64,32},{80,48},{96,0},{112,16},{1... | collective-permute-start | bytes 147464 | tf_op jit(solution)/shard_map/ppermute | solution.py:427
  123.2 7.6 %collective-permute-start.16 = (bf16[2,96,128]{2,1,0:T(8,128)(2,1)}, bf16[2,96,128]{2,1,0:T(8,128)(2,1)S(1)}, u32[]{:S(2)}, u32[]{:S(2)}) collective-permute-start(bf16[2,96,128]{2,1,0:T(8,128)(2,1)} %get-tuple-element.70), channel_id=1, source_target_pairs={{0,112},{16,96},{32,80},{48,64},{64,48},{80,32},{96,16},{112,0},{1... | collective-permute-start | bytes 147464 | tf_op jit(solution)/shard_map/ppermute | solution.py:427
  132.3 7.6 %collective-permute-start.17 = (bf16[96,128]{1,0:T(8,128)(2,1)}, bf16[96,128]{1,0:T(8,128)(2,1)S(1)}, u32[]{:S(2)}, u32[]{:S(2)}) collective-permute-start(bf16[96,128]{1,0:T(8,128)(2,1)} %get-tuple-element.74), channel_id=1, source_target_pairs={{0,132},{132,0},{4,128},{128,4},{1,133},{133,1},{5,129},{129,5},{2... | collective-permute-start | bytes 73736 | tf_op jit(solution)/shard_map/ppermute | solution.py:423
  147.2 22.4 %collective-permute-start.18 = (bf16[8,2,32,3072]{3,2,1,0:T(8,128)(2,1)}, bf16[8,2,32,3072]{3,2,1,0:T(8,128)(2,1)S(1)}, u32[]{:S(2)}, u32[]{:S(2)}) collective-permute-start(bf16[8,2,32,3072]{3,2,1,0:T(8,128)(2,1)} %bitcast.33), channel_id=1, source_target_pairs={{0,8},{8,0},{1,9},{9,1},{2,10},{10,2},{3,11},{11,3},{4,12},{12,4},... | collective-permute-start | bytes 9437192 | tf_op jit(solution)/shard_map/ppermute | solution.py:419
  (7 other events, 63.6 us)
Sparse Core Ops, SparseCore 0:
  20.8 45.6 all-gather.4
  74.7 41.3 all-gather.6

commit v3 on v2

--- a/solution.py
+++ b/solution.py
@@ -89,13 +89,13 @@
     return pl.ds(pl.multiple_of(block * width, width), width)
 
 
-def cut_body(blocks, w2, wq, w1, own, w1_own, beside, sems):
+def cut_body(blocks, w2, wq, w1, own, w1_own, beside, own_s, w1_s, beside_s, sems):
     model = w2.shape[1]
     width = model // blocks
     ctx = ctx_index()
     copies = Copies(sems)
     going = []
-    for dst, block in ((beside, lax.rem(ctx + blocks // 2, blocks)), (own, ctx)):
+    for dst, block in ((beside_s, lax.rem(ctx + blocks // 2, blocks)), (own_s, ctx)):
         going.append(copies.start(w2, dst.at[:, :model]))
         for part in range(3):
             lo = model + part * width
@@ -104,7 +104,7 @@
                     wq.at[:, lanes(part * blocks + block, width)], dst.at[:, lo : lo + width]
                 )
             )
-        to, lo = (beside, model + 3 * width) if dst is beside else (w1_own, 0)
+        to, lo = (beside_s, model + 3 * width) if dst is beside_s else (w1_s, 0)
         for part in range(2):
             at = lo + part * width
             going.append(
@@ -113,12 +113,16 @@
                 )
             )
     wait(*going)
-
-
-def pack_body(wp, w1, out, sems):
+    wait(
+        copies.start(beside_s, beside), copies.start(own_s, own), copies.start(w1_s, w1_own)
+    )
+
+
+def pack_body(wp, w1, out, out_s, sems):
     model = wp.shape[1]
     copies = Copies(sems)
-    wait(copies.start(wp, out.at[:, :model]), copies.start(w1, out.at[:, model:]))
+    wait(copies.start(wp, out_s.at[:, :model]), copies.start(w1, out_s.at[:, model:]))
+    wait(copies.start(out_s, out))
 
 
 def lay_rows(copies, lo, wide, mine, other, out):
@@ -154,15 +158,18 @@
     zeros = jnp.zeros((16, width), F32)
     pad_s[0:16] = zeros
     pad_s[16 + length : 32 + length] = zeros
-    wait(get_k)
     going = []
     for rec in range(records):
         hidden = dot(x[:, rec].reshape(length, model), w_s[...].reshape(model, 2 * width))
         hid_s[rec] = hidden
+        going.append(copies.start(hid_s.at[rec], hid.at[rec]))
         here = lax.broadcasted_iota(jnp.int32, (length, width), 0) < frames[rec]
         value = jnp.where(here, hidden[:, :width] * sigmoid(hidden[:, width:]), 0.0).astype(BF)
         gated_s[rec] = value
+        going.append(copies.start(gated_s.at[rec], gated.at[rec]))
         pad_s[16 : 16 + length] = value.astype(F32)
+        if rec == 0:
+            wait(get_k)
         for b in range(blocks):
             total = jnp.zeros((local, width), F32)
             for j in range(taps):
@@ -170,24 +177,24 @@
                 total = total + k_s[j : j + 1, :] * pad_s[at : at + local, :]
             conv_s[b, rec] = total.astype(BF)
         going.append(copies.start(conv_s.at[:, rec], conv.at[:, rec]))
-        going.append(copies.start(hid_s.at[rec], hid.at[rec]))
-        going.append(copies.start(gated_s.at[rec], gated.at[rec]))
     wait(*going)
 
 
 def token_body(
-    c, mine, other, x, go, g2, ga, sent, res, gc, w2_s, x_s, go_s, g2_s, ga_s, n_s, res_s, gc_s, sems
+    c, mine, other, x, go, g2, ga, sent, res, gc, c_s, w2_s, x_s, go_s, g2_s, ga_s, n_s, res_s, gc_s, sems
 ):
     rows, model = x_s.shape
     blocks = c.shape[0]
     width = model // blocks
     copies = Copies(sems)
+    get_c = copies.start(c, c_s)
     get_w2 = lay_rows(copies, 0, model, mine, other, w2_s)
     get_gain = copies.start(g2, g2_s)
     get_go = copies.start(go, go_s)
     get_x = copies.start(x, x_s)
     get_ga = copies.start(ga, ga_s)
-    conv = jnp.concatenate([c[i] for i in range(blocks)], 1).astype(F32)
+    wait(get_c)
+    conv = jnp.concatenate([c_s[i] for i in range(blocks)], 1).astype(F32)
     centre, inv = centred(conv)
     wait(get_gain)
     gain = g2_s[...]
@@ -213,7 +220,7 @@
 
 def back_body(
     taps, frames, gc, x, hid, gated, k, back, keep, send, gk_out,
-    k_s, hid_s, gated_s, pad_s, gpad_s, gh_s, both_s, gf_s, gk_s, out_s, gko_s, sems,
+    gc_s, k_s, hid_s, gated_s, pad_s, gpad_s, gh_s, both_s, gf_s, gk_s, out_s, gko_s, sems,
 ):
     blocks, records, local, model = x.shape
     length = blocks * local
@@ -221,6 +228,7 @@
     width = k_s.shape[1]
     core = lax.axis_index("core")
     copies = Copies(sems)
+    get_gc = copies.start(gc, gc_s)
     get_k = copies.start(k.at[:, lanes(ctx_index(), width)], k_s)
     get_gated = copies.start(gated, gated_s)
     get_hid = copies.start(hid, hid_s)
@@ -229,9 +237,9 @@
     for ref in (pad_s, gpad_s):
         ref[0:16] = zeros
         ref[16 + length : 32 + length] = zeros
-    wait(get_k, get_gated, get_hid)
+    wait(get_k, get_gc, get_gated)
     for rec in range(records):
-        pad_s[16 : 16 + length] = gc[:, rec].reshape(length, width).astype(F32)
+        pad_s[16 : 16 + length] = gc_s[:, rec].reshape(length, width).astype(F32)
         gpad_s[16 : 16 + length] = gated_s[rec].astype(F32)
         for b in range(blocks):
             base = b * local
@@ -245,6 +253,8 @@
                 gk_s[j] += jnp.sum(term, 0)
             at = lax.broadcasted_iota(jnp.int32, (local, width), 0) + base
             grad_gated = jnp.where(at < frames[rec], total, 0.0)
+            if rec == 0 and b == 0:
+                wait(get_hid)
             linear = hid_s[rec, base : base + local, :width]
             opening = sigmoid(hid_s[rec, base : base + local, width:])
             first = grad_gated * opening
@@ -300,14 +310,10 @@
 
 
 def sum_body(*refs):
-    keep, send, own_s, total_s, sems = refs[-5:]
-    copies = Copies(sems)
-    get_own = copies.start(refs[0], own_s)
-    total = refs[1][...].astype(F32)
-    for ref in refs[2:-5]:
-        total = total + ref[...].astype(F32)
-    wait(get_own)
-    total_s[...] = (total + own_s[...].astype(F32)).astype(BF)
+    keep, send, parts_s, total_s, sems = refs[-5:]
+    copies = Copies(sems)
+    wait(*[copies.start(ref, parts_s.at[i]) for i, ref in enumerate(refs[:-5])])
+    total_s[...] = jnp.sum(parts_s[...].astype(F32), 0).astype(BF)
     yh = lax.axis_index("yh")
     wait(copies.start(total_s.at[1 - yh], send), copies.start(total_s.at[yh], keep))
 
@@ -347,26 +353,12 @@
     wait(copies.start(att_s, back.at[:, 2 * tall : 3 * tall]))
 
 
-def fill_body(keep, recv, held, back, sems):
-    del held
-    copies = Copies(sems)
-    tall = keep.shape[0]
-    base = back.shape[1] - 2 * tall
-    going = []
-    for i in range(back.shape[0]):
-        going.append(copies.start(keep, back.at[i, base : base + tall]))
-        going.append(copies.start(recv, back.at[i, base + tall : base + 2 * tall]))
-    wait(*going)
-
-
-def last_body(
-    frames, a, mine, other, res, x, go, g1, out, gin, gf, gk,
-    wp_s, w1_s, w2_s, res_s, x_s, go_s, g1_s, out_s, gin_s, gf_s, gk_s, sems,
+def result_body(
+    frames, a, mine, other, res, x, go, g1, out, gin,
+    wp_s, w1_s, w2_s, res_s, x_s, go_s, g1_s, out_s, gin_s, sems,
 ):
     rows, model = x_s.shape
     blocks = a.shape[0]
-    width = model // blocks
-    depth, taps = gf_s.shape[0], gk_s.shape[0]
     copies = Copies(sems)
     get_w = [
         lay_rows(copies, i * model, model, mine, other, one)
@@ -376,22 +368,9 @@
     get_x = copies.start(x, x_s)
     get_go = copies.start(go, go_s)
     get_g1 = copies.start(g1, g1_s)
-    tall = (a.shape[1] - 3 * rows) // 4
-    base = 3 * rows
-    half = tall - depth
-    for i in range(blocks):
-        lo = i * width
-        for h in range(2):
-            at = base + h * tall
-            far = at + 2 * tall
-            total = a[i, at : at + tall].astype(F32) + a[
-                (i + blocks // 2) % blocks, far : far + tall
-            ].astype(F32)
-            gf_s[:, h * model + lo : h * model + lo + width] = total[:depth]
-            count = min(half, taps - h * half)
-            gk_s[h * half : h * half + count, lo : lo + width] = total[depth : depth + count]
-    going = [copies.start(gf_s, gf), copies.start(gk_s, gk)]
     attended = jnp.concatenate([a[i, 2 * rows : 3 * rows] for i in range(blocks)], 1)
+    linear = jnp.concatenate([a[i, :rows] for i in range(blocks)], 1)
+    gating = jnp.concatenate([a[i, rows : 2 * rows] for i in range(blocks)], 1)
     wait(*get_w[0])
     projected = dot(attended, wp_s[...].reshape(model, model))
     records = frames.shape[0]
@@ -400,9 +379,7 @@
     present = jnp.concatenate([(at < frames[r]).astype(F32) for r in range(records)], 0)
     wait(get_res)
     out_s[...] = (res_s[...].astype(F32) + present * projected).astype(BF)
-    going.append(copies.start(out_s, out))
-    linear = jnp.concatenate([a[i, :rows] for i in range(blocks)], 1)
-    gating = jnp.concatenate([a[i, rows : 2 * rows] for i in range(blocks)], 1)
+    put_out = copies.start(out_s, out)
     wait(*get_w[1])
     back_one = dot_t(linear, w1_s[...].reshape(model, model))
     wait(*get_w[2])
@@ -411,8 +388,28 @@
     centre, inv = centred(x_s[...].astype(F32))
     pulled = norm_pull(back_one * g1_s[...], centre, inv)
     gin_s[...] = (go_s[...].astype(F32) + pulled).astype(BF)
-    going.append(copies.start(gin_s, gin))
-    wait(*going)
+    wait(put_out, copies.start(gin_s, gin))
+
+
+def lay_body(a, gf, gk, gf_s, gk_s, sems):
+    blocks = a.shape[0]
+    depth, taps = gf_s.shape[0], gk_s.shape[0]
+    model = gk_s.shape[1]
+    width = model // blocks
+    tall = a.shape[2] // 2
+    half = tall - depth
+    for i in range(blocks):
+        lo = i * width
+        total = a[i, 0].astype(F32) + a[(i + blocks // 2) % blocks, 1].astype(F32)
+        for h in range(2):
+            at = h * tall
+            gf_s[:, h * model + lo : h * model + lo + width] = total[at : at + depth]
+            count = min(half, taps - h * half)
+            gk_s[h * half : h * half + count, lo : lo + width] = total[
+                at + depth : at + depth + count
+            ]
+    copies = Copies(sems)
+    wait(copies.start(gf_s, gf), copies.start(gk_s, gk))
 
 
 def swap_core(v):
@@ -464,7 +461,8 @@
         ],
         [(w_second, HBM), (w_qkv, HBM), (w_first, HBM)],
         "cut",
-        sems=12,
+        [((depth, part), BF), ((depth, 2 * width), BF), ((depth, part + 2 * width), BF)],
+        15,
     )
     beside = swap_yh(beside)
     (sent,) = run(
@@ -490,7 +488,8 @@
         [((depth, 3 * model), BF, HBM)],
         [(w_proj, HBM), (w_first, HBM)],
         "pack",
-        sems=2,
+        [((depth, 3 * model), BF)],
+        3,
     )
     shard_b = jnp.stack([own_b, swap_yh(own_b)])
 
@@ -528,11 +527,12 @@
             ((blocks, rows, width), BF, HBM),
         ],
         [
-            (conv_rows, VMEM), (all_a, HBM), (other_a, ANY), (x, HBM), (cot, HBM), (gains[1], HBM),
+            (conv_rows, HBM), (all_a, HBM), (other_a, ANY), (x, HBM), (cot, HBM), (gains[1], HBM),
             (gains[2], HBM),
         ],
         "token_rows",
         [
+            ((blocks, rows, width), BF),
             ((2, zs, 2, depth, model), BF),
             ((rows, model), BF),
             ((rows, model), BF),
@@ -542,7 +542,7 @@
             ((rows, model), BF),
             ((blocks, rows, width), BF),
         ],
-        blocks + 10,
+        blocks + 11,
     )
     grad_conv = lax.all_to_all(grad_conv, CTX, 0, 0, tiled=True)
     sent, grad_conv = barrier((sent, grad_conv))
@@ -555,17 +555,18 @@
     back, keep, send, gk = run(
         functools.partial(back_body, taps),
         [
-            ((blocks, 3 * rows + 4 * tall, width), BF, HBM),
+            ((blocks, 3 * rows, width), BF, HBM),
             (half_share, BF, HBM),
             (half_share, BF, HBM),
             ((16, 2 * width), F32, HBM),
         ],
         [
-            (frames, SMEM), (grad_conv, VMEM), (normed, VMEM), (hidden, HBM), (gated, HBM),
+            (frames, SMEM), (grad_conv, HBM), (normed, VMEM), (hidden, HBM), (gated, HBM),
             (depth_kernel, HBM),
         ],
         "conv_back",
         [
+            ((blocks, records, local_len, width), BF),
             ((taps, width), F32),
             ((records, length, 2 * width), F32),
             ((records, length, width), BF),
@@ -578,7 +579,7 @@
             ((blocks, 2 * rows, width), BF),
             ((16, 2 * width), F32),
         ],
-        7,
+        8,
     )
 
     chunk = (2, 2 * tall, width)
@@ -596,16 +597,17 @@
         zs + 2,
     )
     sums = [chunks[0]] + [pair_z(chunks[s], s) for s in range(1, zs)]
+    attn_in, *sums[1:5] = barrier((attn_in, *sums[1:5]))
     keep, send = run(
         sum_body,
         [(chunk[1:], BF, HBM)] * 2,
-        [(sums[0], HBM)] + [(one, VMEM) for one in sums[1:]],
+        [(one, ANY) for one in sums],
         "share_sum",
-        [(chunk, BF), (chunk, BF)],
-        3,
-    )
-    attn_in, keep, send = barrier((attn_in, keep, send))
-    recv = swap_yh(send)
+        [((zs,) + chunk, BF), (chunk, BF)],
+        zs + 2,
+    )
+    pair = jnp.stack([keep, swap_yh(send)])
+    pair = jnp.broadcast_to(pair, (blocks,) + pair.shape)
 
     (back,) = run(
         functools.partial(heads_body, head_dim),
@@ -616,44 +618,33 @@
         5,
         {4: 0},
     )
-    (back,) = run(
-        fill_body,
-        [(back.shape, BF, HBM)],
-        [(keep, HBM), (recv, ANY), (back, HBM)],
-        "fill",
-        sems=2 * blocks,
-        alias={2: 0},
-    )
     all_b, back = barrier((all_b, back))
     other_b = swap_core(all_b)
     back = lax.all_to_all(back, CTX, 0, 0, tiled=True)
-    result, grad_in, grad_first, grad_kernel = run(
-        last_body,
-        [
-            ((rows, model), BF, HBM),
-            ((rows, model), BF, HBM),
-            ((depth, 2 * model), F32, HBM),
-            ((taps, model), F32, HBM),
-        ],
+    pair, back = barrier((pair, back))
+    pair = lax.all_to_all(pair, CTX, 0, 0, tiled=True)
+    result, grad_in = run(
+        result_body,
+        [((rows, model), BF, HBM)] * 2,
         [
             (frames, SMEM), (back, VMEM), (all_b, HBM), (other_b, ANY), (residual, HBM), (x, HBM),
             (cot, HBM), (gains[0], HBM),
         ],
         "result_rows",
-        [
-            ((2, zs, 2, depth, model), BF),
-            ((2, zs, 2, depth, model), BF),
-            ((2, zs, 2, depth, model), BF),
-            ((rows, model), BF),
-            ((rows, model), BF),
-            ((rows, model), BF),
-            ((1, model), F32),
-            ((rows, model), BF),
-            ((rows, model), BF),
-            ((depth, 2 * model), F32),
-            ((taps, model), F32),
-        ],
-        20,
+        [((2, zs, 2, depth, model), BF)] * 3
+        + [((rows, model), BF)] * 3
+        + [((1, model), F32)]
+        + [((rows, model), BF)] * 2,
+        18,
+    )
+    pair, result, grad_in = barrier((pair, result, grad_in))
+    grad_first, grad_kernel = run(
+        lay_body,
+        [((depth, 2 * model), F32, HBM), ((taps, model), F32, HBM)],
+        [(pair, VMEM)],
+        "lay_out",
+        [((depth, 2 * model), F32), ((taps, model), F32)],
+        2,
     )
     return (
         result.reshape(records, local_len, model),

time: 185 us -> 177 us (0.957)
  blocking collectives: 34.2 us -> 11.9 us
  Pallas kernels: 56.2 us -> 37.9 us
  starting transfers between devices: 47 us -> 65.1 us
  waiting for transfers between devices: 26.5 us -> 34.6 us
  local copies, waits for them, and re-layouts: 2.66 us -> 8.03 us
    all_to_all x1 -> x0, blocking collectives: 22.3 us -> none  [local(): back = lax.all_to_all(back, CTX, 0, 0, tiled=True)]
    pallas_call x11, Pallas kernels: 56.2 us -> 37.9 us  [run(): pl.pallas_call(body, out_shape=tuple((o[2](o[0], o[1]) for o in outs)), i...]
    all_to_all x0 -> x2, starting transfers between devices: none -> 12.5 us  [the longest x1 6.32 us: local(): pair = lax.all_to_all(pair, CTX, 0, 0, tiled=True)]
    ppermute x11, waiting for transfers between devices: 15.7 us -> 20.7 us  [pair_z(): lax.ppermute(v, 'z', [(i, i ^ by) for i in range(lax.axis_size('z'))])]
    ppermute x11, starting transfers between devices: 22.7 us -> 27.3 us  [pair_z(): lax.ppermute(v, 'z', [(i, i ^ by) for i in range(lax.axis_size('z'))])]
    unnamed x17 -> x31, local copies, waits for them, and re-layouts: 2.64 us -> 7.21 us
    ppermute x3, waiting for transfers between devices: 0.7 us -> 2.99 us  [swap_yh(): return lax.ppermute(v, ('yh', 'yl'), [(0, 3), (3, 0), (1, 2), (2, 1)])]
  transfers between devices with their start and end apart: 24 -> 26, of which waited for: 10 -> 15; matrix products, arithmetic and copies ran while one was open for 0% -> 1% of each run, Pallas kernels for 23% -> 20%
where the time goes in v3:
time: 177 us; the launch traced here: 174 us
  starting transfers between devices  65.1 us (37%)
  Pallas kernels  37.9 us (21%)
  waiting for transfers between devices  34.6 us (20%)
  between operations  14.3 us (8%)
  blocking collectives  11.9 us (7%)
  local copies, waits for them, and re-layouts  8.03 us (5%)
  other arithmetic  2.25 us (1%)
    pallas_call x11, Pallas kernels, run(): pl.pallas_call(body, out_shape=tuple((o[2](o[0], o[1]) for o in outs)), i...  37.9 us
    ppermute x11, starting transfers between devices, pair_z(): lax.ppermute(v, 'z', [(i, i ^ by) for i in range(lax.axis_size('z'))])  27.3 us
    ppermute x11, waiting for transfers between devices, pair_z(): lax.ppermute(v, 'z', [(i, i ^ by) for i in range(lax.axis_size('z'))])  20.7 us
    all_to_all x1, blocking collectives, local(): grad_conv = lax.all_to_all(grad_conv, CTX, 0, 0, tiled=True)  11.9 us
    unnamed x31, local copies, waits for them, and re-layouts  7.21 us
    all_to_all x1, starting transfers between devices, local(): lax.all_to_all(sent, CTX, 0, 0, tiled=True)  6.93 us
    all_to_all x1, starting transfers between devices, local(): lax.all_to_all(conv, CTX, 0, 0, tiled=True).reshape(blocks, rows, width)  6.42 us
    all_to_all x1, starting transfers between devices, local(): pair = lax.all_to_all(pair, CTX, 0, 0, tiled=True)  6.32 us
  transfers between devices with their start and end apart: 26, of which 15 were waited for; matrix products, arithmetic and copies ran while one was open for 1% of the time, Pallas kernels for 20%

profile of v3, /device:TPU:8, one launch (start us, length us, event | category | flops | bytes accessed | tf_op | source)
XLA Modules:
  0.0 174.2 jit_solution(10799899129509746110)
XLA Ops:
  10.7 2.6 %first_norm.1 = bf16[8,128,1024]{2,1,0:T(8,128)(2,1)} custom-call(bf16[128,1024]{1,0:T(8,128)(2,1)} %bitcast.35, f32[1,1024]{1,0:T(1,128)} %bitcast.50), custom_call_target="tpu_custom_call" | custom-call | tf_op jit(solution)/shard_map/first_norm/pallas_call | solution.py:26
  14.8 6.9 %all-to-all-start = ((bf16[8,128,1024]{2,1,0:T(8,128)(2,1)}), bf16[8,128,1024]{2,1,0:T(8,128)(2,1)S(1)}, u32[]{:S(2)}, u32[]{:S(2)}) async-start(bf16[8,128,1024]{2,1,0:T(8,128)(2,1)} %first_norm.1), calls=%async_computation | async-start | bytes 4194304 | tf_op jit(solution)/shard_map/all_to_all | solution.py:479
  22.9 2.9 %collective-permute-done.1 = bf16[2,32,256]{2,1,0:T(8,128)(2,1)S(1)} collective-permute-done((bf16[2,32,256]{2,1,0:T(8,128)(2,1)S(1)}, bf16[2,32,256]{2,1,0:T(8,128)(2,1)S(1)}, u32[]{:S(2)}, u32[]{:S(2)}) %collective-permute-start.1) | collective-permute-done | bytes 32800 | tf_op jit(solution)/shard_map/ppermute | solution.py:424
  25.7 2.5 %collective-permute-start.2 = (bf16[2,2,32,256]{3,2,1,0:T(8,128)(2,1)S(1)}, bf16[2,2,32,256]{3,2,1,0:T(8,128)(2,1)S(1)}, u32[]{:S(2)}, u32[]{:S(2)}) collective-permute-start(bf16[2,2,32,256]{3,2,1,0:T(8,128)(2,1)S(1)} %pad_maximum_fusion.2), channel_id=1, source_target_pairs={{0,32},{16,48},{32,0},{48,16},{64,96},{80,112},{96,64},{112,80},{1... | collective-permute-start | bytes 196616 | tf_op jit(solution)/shard_map/ppermute | solution.py:424
  28.2 5.4 %collective-permute-start.3 = (bf16[2,2,32,256]{3,2,1,0:T(8,128)(2,1)S(1)}, bf16[2,2,32,256]{3,2,1,0:T(8,128)(2,1)S(1)}, u32[]{:S(2)}, u32[]{:S(2)}) collective-permute-start(bf16[2,2,32,256]{3,2,1,0:T(8,128)(2,1)S(1)} %pad_maximum_fusion.2), channel_id=1, source_target_pairs={{0,64},{16,80},{32,96},{48,112},{64,0},{80,16},{96,32},{112,48},{1... | collective-permute-start | bytes 196616 | tf_op jit(solution)/shard_map/ppermute | solution.py:424
  33.6 6.4 %collective-permute-done.3 = bf16[2,2,32,256]{3,2,1,0:T(8,128)(2,1)S(1)} collective-permute-done((bf16[2,2,32,256]{3,2,1,0:T(8,128)(2,1)S(1)}, bf16[2,2,32,256]{3,2,1,0:T(8,128)(2,1)S(1)}, u32[]{:S(2)}, u32[]{:S(2)}) %collective-permute-start.3) | collective-permute-done | bytes 65568 | tf_op jit(solution)/shard_map/ppermute | solution.py:424
  45.5 3.9 %gate_conv.1 = (bf16[8,2,64,128]{3,2,1,0:T(8,128)(2,1)}, f32[2,512,256]{2,1,0:T(8,128)}, bf16[2,512,128]{2,1,0:T(8,128)(2,1)}) custom-call(s32[2]{0:T(128)S(1)} %copy-done.9, bf16[8,2,64,1024]{3,2,1,0:T(8,128)(2,1)S(1)} %bitcast.28, bf16[8,2,32,256]{3,2,1,0:T(8,128)(2,1)S(1)} %constant_dynamic-update-slice_fusion.wm, ...), custom_call_target="tpu_custom_call" | custom-call | tf_op jit(solution)/shard_map/gate_conv/pallas_call | solution.py:26
  49.4 6.4 %all-to-all-start.1 = ((bf16[8,2,64,128]{3,2,1,0:T(8,128)(2,1)}), bf16[8,2,64,128]{3,2,1,0:T(8,128)(2,1)S(1)}, u32[]{:S(2)}, u32[]{:S(2)}) async-start(bf16[8,2,64,128]{3,2,1,0:T(8,128)(2,1)} %get-tuple-element.56), calls=%async_computation.1 | async-start | bytes 524288 | tf_op jit(solution)/shard_map/all_to_all | solution.py:516
  56.6 5.4 %all-to-all-done.1 = bf16[8,2,64,128]{3,2,1,0:T(8,128)(2,1)S(1)} async-done(((bf16[8,2,64,128]{3,2,1,0:T(8,128)(2,1)}), bf16[8,2,64,128]{3,2,1,0:T(8,128)(2,1)S(1)}, u32[]{:S(2)}, u32[]{:S(2)}) %all-to-all-start.1) | async-done | bytes 262176 | tf_op jit(solution)/shard_map/all_to_all | solution.py:516
  62.8 3.4 %collective-permute-done.7.other = bf16[8,2,32,1408]{3,2,1,0:T(8,128)(2,1)S(1)} collective-permute-done((bf16[8,2,32,1408]{3,2,1,0:T(8,128)(2,1)}, bf16[8,2,32,1408]{3,2,1,0:T(8,128)(2,1)S(1)}, u32[]{:S(2)}, u32[]{:S(2)}) %collective-permute-start.7) | collective-permute-done | bytes 1441824 | tf_op jit(solution)/shard_map/ppermute | solution.py:416
  66.3 4.5 %token_rows.1 = (bf16[8,128,1024]{2,1,0:T(8,128)(2,1)}, bf16[128,1024]{1,0:T(8,128)(2,1)}, bf16[8,128,128]{2,1,0:T(8,128)(2,1)}) custom-call(bf16[8,128,128]{2,1,0:T(8,128)(2,1)} %bitcast.40, bf16[8,2,32,1408]{3,2,1,0:T(8,128)(2,1)} %bitcast.31, bf16[8,2,32,1408]{3,2,1,0:T(8,128)(2,1)S(1)} %collective-permute-done.7.other, bf16[128,1024]{1,0:T(8,128)(2,1)} %bitcast.36, ...), custom_call_target="tpu_custom_call" | custom-call | tf_op jit(solution)/shard_map/token_rows/pallas_call | solution.py:26
  70.8 11.9 %all_to_all.30 = bf16[8,128,128]{2,1,0:T(8,128)(2,1)} all-to-all(bf16[8,128,128]{2,1,0:T(8,128)(2,1)} %get-tuple-element.61), channel_id=1, replica_groups=mesh['yh'=2,'z'=8,'core'=2,'yl'=2,'x'=4] {'yl','x'}, dimensions={0} | all-to-all | bytes 524288 | tf_op jit(solution)/shard_map/all_to_all | solution.py:547
  82.7 5.7 %all-to-all-start.3 = ((bf16[8,128,1024]{2,1,0:T(8,128)(2,1)}), bf16[8,128,1024]{2,1,0:T(8,128)(2,1)}, u32[]{:S(2)}, u32[]{:S(2)}) async-start(bf16[8,128,1024]{2,1,0:T(8,128)(2,1)} %get-tuple-element.69), calls=%async_computation.3 | async-start | bytes 4194304 | tf_op jit(solution)/shard_map/all_to_all | solution.py:550
  88.4 6.1 %conv_back.1 = (bf16[8,384,128]{2,1,0:T(8,128)(2,1)}, bf16[2,8,32,256]{3,2,1,0:T(8,128)(2,1)}, bf16[2,8,32,256]{3,2,1,0:T(8,128)(2,1)}, f32[16,256]{1,0:T(8,128)}) custom-call(s32[2]{0:T(128)S(1)} %copy-done.9, bf16[8,2,64,128]{3,2,1,0:T(8,128)(2,1)} %bitcast.41, bf16[8,2,64,1024]{3,2,1,0:T(8,128)(2,1)S(1)} %bitcast.29, ...), custom_call_target="tpu_custom_call" | custom-call | tf_op jit(solution)/shard_map/conv_back/pallas_call | solution.py:26
  102.8 5.2 %collective-permute-start.13 = (bf16[2,96,128]{2,1,0:T(8,128)(2,1)}, bf16[2,96,128]{2,1,0:T(8,128)(2,1)S(1)}, u32[]{:S(2)}, u32[]{:S(2)}) collective-permute-start(bf16[2,96,128]{2,1,0:T(8,128)(2,1)} %get-tuple-element.73), channel_id=1, source_target_pairs={{0,64},{16,80},{32,96},{48,112},{64,0},{80,16},{96,32},{112,48},{1... | collective-permute-start | bytes 147464 | tf_op jit(solution)/shard_map/ppermute | solution.py:424
  110.7 4.7 %collective-permute-done.13.refs_4_ = bf16[2,96,128]{2,1,0:T(8,128)(2,1)S(1)} collective-permute-done((bf16[2,96,128]{2,1,0:T(8,128)(2,1)}, bf16[2,96,128]{2,1,0:T(8,128)(2,1)S(1)}, u32[]{:S(2)}, u32[]{:S(2)}) %collective-permute-start.13) | collective-permute-done | bytes 49184 | tf_op jit(solution)/shard_map/ppermute | solution.py:424
  116.0 7.3 %heads.1 = bf16[8,384,128]{2,1,0:T(8,128)(2,1)} custom-call(s32[2]{0:T(128)S(1)} %copy-done.9, bf16[8,2,64,1024]{3,2,1,0:T(8,128)(2,1)} %bitcast.17.x, bf16[8,2,32,1408]{3,2,1,0:T(8,128)(2,1)} %bitcast.32, bf16[8,2,32,1408]{3,2,1,0:T(8,128)(2,1)S(1)} %collective-permute-done.7.other, ...), custom_call_target="tpu_custom_call", output_to_operand_aliasing={{}: (4, {})} | custom-call | tf_op jit(solution)/shard_map/heads/pallas_call | solution.py:26
  123.4 6.2 %all-to-all-start.4 = ((bf16[8,384,128]{2,1,0:T(8,128)(2,1)}), bf16[8,384,128]{2,1,0:T(8,128)(2,1)}, u32[]{:S(2)}, u32[]{:S(2)}) async-start(bf16[8,384,128]{2,1,0:T(8,128)(2,1)} %heads.1), calls=%async_computation.4 | async-start | bytes 1572864 | tf_op jit(solution)/shard_map/all_to_all | solution.py:623
  129.5 4.9 %collective-permute-start.14 = (bf16[2,96,128]{2,1,0:T(8,128)(2,1)}, bf16[2,96,128]{2,1,0:T(8,128)(2,1)S(1)}, u32[]{:S(2)}, u32[]{:S(2)}) collective-permute-start(bf16[2,96,128]{2,1,0:T(8,128)(2,1)} %get-tuple-element.78), channel_id=1, source_target_pairs={{0,80},{16,64},{32,112},{48,96},{64,16},{80,0},{96,48},{112,32},{1... | collective-permute-start | bytes 147464 | tf_op jit(solution)/shard_map/ppermute | solution.py:424
  135.0 3.1 %collective-permute-start.16 = (bf16[2,96,128]{2,1,0:T(8,128)(2,1)}, bf16[2,96,128]{2,1,0:T(8,128)(2,1)S(1)}, u32[]{:S(2)}, u32[]{:S(2)}) collective-permute-start(bf16[2,96,128]{2,1,0:T(8,128)(2,1)} %get-tuple-element.80), channel_id=1, source_target_pairs={{0,112},{16,96},{32,80},{48,64},{64,48},{80,32},{96,16},{112,0},{1... | collective-permute-start | bytes 147464 | tf_op jit(solution)/shard_map/ppermute | solution.py:424
  138.8 2.2 %collective-permute-done.15.refs_6_ = bf16[2,96,128]{2,1,0:T(8,128)(2,1)S(1)} collective-permute-done((bf16[2,96,128]{2,1,0:T(8,128)(2,1)}, bf16[2,96,128]{2,1,0:T(8,128)(2,1)S(1)}, u32[]{:S(2)}, u32[]{:S(2)}) %collective-permute-start.15) | collective-permute-done | bytes 49184 | tf_op jit(solution)/shard_map/ppermute | solution.py:424
  149.8 2.3 %collective-permute-done.17 = bf16[96,128]{1,0:T(8,128)(2,1)S(1)} collective-permute-done((bf16[96,128]{1,0:T(8,128)(2,1)}, bf16[96,128]{1,0:T(8,128)(2,1)S(1)}, u32[]{:S(2)}, u32[]{:S(2)}) %collective-permute-start.17) | collective-permute-done | bytes 24608 | tf_op jit(solution)/shard_map/ppermute | solution.py:420
  153.7 6.3 %all-to-all-start.5 = ((bf16[8,2,96,128]{3,2,1,0:T(8,128)(2,1)}), bf16[8,2,96,128]{3,2,1,0:T(8,128)(2,1)S(1)}, u32[]{:S(2)}, u32[]{:S(2)}) async-start(bf16[8,2,96,128]{3,2,1,0:T(8,128)(2,1)} %broadcast_in_dim.3), calls=%async_computation.5 | async-start | bytes 786432 | tf_op jit(solution)/shard_map/all_to_all | solution.py:625
  160.0 6.2 %result_rows.1 = (bf16[128,1024]{1,0:T(8,128)(2,1)}, bf16[128,1024]{1,0:T(8,128)(2,1)}) custom-call(s32[2]{0:T(128)S(1)} %copy-done.9, bf16[8,384,128]{2,1,0:T(8,128)(2,1)} %all-to-all-done.4.a, bf16[8,2,32,3072]{3,2,1,0:T(8,128)(2,1)} %bitcast.34, bf16[8,2,32,3072]{3,2,1,0:T(8,128)(2,1)S(1)} %collective-permute-done.18.other, ...), custom_call_target="tpu_custom_call" | custom-call | tf_op jit(solution)/shard_map/result_rows/pallas_call | solution.py:26
  (83 shorter events, 37.5 us)
Async XLA Ops:
  7.2 54.8 %all-gather.5.cloned.1.call-start = ((), (), s32[]{:S(2)}) async-start(), calls=%async_computation.6 | async-start | bytes 1622016 | tf_op jit(solution)/shard_map/all_gather | solution.py:478
  9.0 5.0 %collective-permute-start = (bf16[32,1664]{1,0:T(8,128)(2,1)}, bf16[32,1664]{1,0:T(8,128)(2,1)S(1)}, u32[]{:S(2)}, u32[]{:S(2)}) collective-permute-start(bf16[32,1664]{1,0:T(8,128)(2,1)} %get-tuple-element.52), channel_id=1, source_target_pairs={{0,132},{132,0},{4,128},{128,4},{1,133},{133,1},{5,129},{129,5},{2... | collective-permute-start | bytes 319496 | tf_op jit(solution)/shard_map/ppermute | solution.py:420
  14.8 30.7 %all-to-all-start = ((bf16[8,128,1024]{2,1,0:T(8,128)(2,1)}), bf16[8,128,1024]{2,1,0:T(8,128)(2,1)S(1)}, u32[]{:S(2)}, u32[]{:S(2)}) async-start(bf16[8,128,1024]{2,1,0:T(8,128)(2,1)} %first_norm.1), calls=%async_computation | async-start | bytes 4194304 | tf_op jit(solution)/shard_map/all_to_all | solution.py:479
  21.7 4.0 %collective-permute-start.1 = (bf16[2,32,256]{2,1,0:T(8,128)(2,1)S(1)}, bf16[2,32,256]{2,1,0:T(8,128)(2,1)S(1)}, u32[]{:S(2)}, u32[]{:S(2)}) collective-permute-start(bf16[2,32,256]{2,1,0:T(8,128)(2,1)S(1)} %get-tuple-element.99), channel_id=1, source_target_pairs={{0,16},{16,0},{32,48},{48,32},{64,80},{80,64},{96,112},{112,96},{1... | collective-permute-start | bytes 98312 | tf_op jit(solution)/shard_map/ppermute | solution.py:424
  25.7 7.9 %collective-permute-start.2 = (bf16[2,2,32,256]{3,2,1,0:T(8,128)(2,1)S(1)}, bf16[2,2,32,256]{3,2,1,0:T(8,128)(2,1)S(1)}, u32[]{:S(2)}, u32[]{:S(2)}) collective-permute-start(bf16[2,2,32,256]{3,2,1,0:T(8,128)(2,1)S(1)} %pad_maximum_fusion.2), channel_id=1, source_target_pairs={{0,32},{16,48},{32,0},{48,16},{64,96},{80,112},{96,64},{112,80},{1... | collective-permute-start | bytes 196616 | tf_op jit(solution)/shard_map/ppermute | solution.py:424
  28.2 11.8 %collective-permute-start.3 = (bf16[2,2,32,256]{3,2,1,0:T(8,128)(2,1)S(1)}, bf16[2,2,32,256]{3,2,1,0:T(8,128)(2,1)S(1)}, u32[]{:S(2)}, u32[]{:S(2)}) collective-permute-start(bf16[2,2,32,256]{3,2,1,0:T(8,128)(2,1)S(1)} %pad_maximum_fusion.2), channel_id=1, source_target_pairs={{0,64},{16,80},{32,96},{48,112},{64,0},{80,16},{96,32},{112,48},{1... | collective-permute-start | bytes 196616 | tf_op jit(solution)/shard_map/ppermute | solution.py:424
  33.6 7.8 %collective-permute-start.4 = (bf16[2,2,32,256]{3,2,1,0:T(8,128)(2,1)S(1)}, bf16[2,2,32,256]{3,2,1,0:T(8,128)(2,1)S(1)}, u32[]{:S(2)}, u32[]{:S(2)}) collective-permute-start(bf16[2,2,32,256]{3,2,1,0:T(8,128)(2,1)S(1)} %pad_maximum_fusion.2), channel_id=1, source_target_pairs={{0,96},{16,112},{32,64},{48,80},{64,32},{80,48},{96,0},{112,16},{1... | collective-permute-start | bytes 196616 | tf_op jit(solution)/shard_map/ppermute | solution.py:424
  41.4 3.6 %collective-permute-start.5 = (bf16[8,2,32,256]{3,2,1,0:T(8,128)(2,1)S(1)}, bf16[8,2,32,256]{3,2,1,0:T(8,128)(2,1)S(1)}, u32[]{:S(2)}, u32[]{:S(2)}) collective-permute-start(bf16[8,2,32,256]{3,2,1,0:T(8,128)(2,1)S(1)} %constant_dynamic-update-slice_fusion.wm), channel_id=1, source_target_pairs={{0,8},{8,0},{1,9},{9,1},{2,10},{10,2},{3,11},{11,3},{4,12},{12,4},... | collective-permute-start | bytes 786440 | tf_op jit(solution)/shard_map/ppermute | solution.py:416
  43.1 12.7 %collective-permute-start.6 = (bf16[32,3072]{1,0:T(8,128)(2,1)}, bf16[32,3072]{1,0:T(8,128)(2,1)S(1)}, u32[]{:S(2)}, u32[]{:S(2)}) collective-permute-start(bf16[32,3072]{1,0:T(8,128)(2,1)} %pack.1), channel_id=1, source_target_pairs={{0,132},{132,0},{4,128},{128,4},{1,133},{133,1},{5,129},{129,5},{2... | collective-permute-start | bytes 589832 | tf_op jit(solution)/shard_map/ppermute | solution.py:420
  49.4 12.6 %all-to-all-start.1 = ((bf16[8,2,64,128]{3,2,1,0:T(8,128)(2,1)}), bf16[8,2,64,128]{3,2,1,0:T(8,128)(2,1)S(1)}, u32[]{:S(2)}, u32[]{:S(2)}) async-start(bf16[8,2,64,128]{3,2,1,0:T(8,128)(2,1)} %get-tuple-element.56), calls=%async_computation.1 | async-start | bytes 524288 | tf_op jit(solution)/shard_map/all_to_all | solution.py:516
  55.8 67.5 %all-gather.7.cloned.1.call-start = ((), (), s32[]{:S(2)}) async-start(), calls=%async_computation.7 | async-start | bytes 3538944 | tf_op jit(solution)/shard_map/all_gather | solution.py:520
  62.7 3.5 %collective-permute-start.7 = (bf16[8,2,32,1408]{3,2,1,0:T(8,128)(2,1)}, bf16[8,2,32,1408]{3,2,1,0:T(8,128)(2,1)S(1)}, u32[]{:S(2)}, u32[]{:S(2)}) collective-permute-start(bf16[8,2,32,1408]{3,2,1,0:T(8,128)(2,1)} %bitcast.30), channel_id=1, source_target_pairs={{0,8},{8,0},{1,9},{9,1},{2,10},{10,2},{3,11},{11,3},{4,12},{12,4},... | collective-permute-start | bytes 4325384 | tf_op jit(solution)/shard_map/ppermute | solution.py:416
  82.7 33.3 %all-to-all-start.3 = ((bf16[8,128,1024]{2,1,0:T(8,128)(2,1)}), bf16[8,128,1024]{2,1,0:T(8,128)(2,1)}, u32[]{:S(2)}, u32[]{:S(2)}) async-start(bf16[8,128,1024]{2,1,0:T(8,128)(2,1)} %get-tuple-element.69), calls=%async_computation.3 | async-start | bytes 4194304 | tf_op jit(solution)/shard_map/all_to_all | solution.py:550
  98.3 9.8 %collective-permute-start.10 = (bf16[2,96,128]{2,1,0:T(8,128)(2,1)}, bf16[2,96,128]{2,1,0:T(8,128)(2,1)S(1)}, u32[]{:S(2)}, u32[]{:S(2)}) collective-permute-start(bf16[2,96,128]{2,1,0:T(8,128)(2,1)} %get-tuple-element.70), channel_id=1, source_target_pairs={{0,16},{16,0},{32,48},{48,32},{64,80},{80,64},{96,112},{112,96},{1... | collective-permute-start | bytes 147464 | tf_op jit(solution)/shard_map/ppermute | solution.py:424
  100.4 8.3 %collective-permute-start.11 = (bf16[2,96,128]{2,1,0:T(8,128)(2,1)}, bf16[2,96,128]{2,1,0:T(8,128)(2,1)S(1)}, u32[]{:S(2)}, u32[]{:S(2)}) collective-permute-start(bf16[2,96,128]{2,1,0:T(8,128)(2,1)} %get-tuple-element.71), channel_id=1, source_target_pairs={{0,32},{16,48},{32,0},{48,16},{64,96},{80,112},{96,64},{112,80},{1... | collective-permute-start | bytes 147464 | tf_op jit(solution)/shard_map/ppermute | solution.py:424
  101.7 8.4 %collective-permute-start.12 = (bf16[2,96,128]{2,1,0:T(8,128)(2,1)}, bf16[2,96,128]{2,1,0:T(8,128)(2,1)S(1)}, u32[]{:S(2)}, u32[]{:S(2)}) collective-permute-start(bf16[2,96,128]{2,1,0:T(8,128)(2,1)} %get-tuple-element.72), channel_id=1, source_target_pairs={{0,48},{16,32},{32,16},{48,0},{64,112},{80,96},{96,80},{112,64},{1... | collective-permute-start | bytes 147464 | tf_op jit(solution)/shard_map/ppermute | solution.py:424
  102.8 12.5 %collective-permute-start.13 = (bf16[2,96,128]{2,1,0:T(8,128)(2,1)}, bf16[2,96,128]{2,1,0:T(8,128)(2,1)S(1)}, u32[]{:S(2)}, u32[]{:S(2)}) collective-permute-start(bf16[2,96,128]{2,1,0:T(8,128)(2,1)} %get-tuple-element.73), channel_id=1, source_target_pairs={{0,64},{16,80},{32,96},{48,112},{64,0},{80,16},{96,32},{112,48},{1... | collective-permute-start | bytes 147464 | tf_op jit(solution)/shard_map/ppermute | solution.py:424
  123.3 36.7 %collective-permute-start.18 = (bf16[8,2,32,3072]{3,2,1,0:T(8,128)(2,1)}, bf16[8,2,32,3072]{3,2,1,0:T(8,128)(2,1)S(1)}, u32[]{:S(2)}, u32[]{:S(2)}) collective-permute-start(bf16[8,2,32,3072]{3,2,1,0:T(8,128)(2,1)} %bitcast.33), channel_id=1, source_target_pairs={{0,8},{8,0},{1,9},{9,1},{2,10},{10,2},{3,11},{11,3},{4,12},{12,4},... | collective-permute-start | bytes 9437192 | tf_op jit(solution)/shard_map/ppermute | solution.py:416
  123.4 29.5 %all-to-all-start.4 = ((bf16[8,384,128]{2,1,0:T(8,128)(2,1)}), bf16[8,384,128]{2,1,0:T(8,128)(2,1)}, u32[]{:S(2)}, u32[]{:S(2)}) async-start(bf16[8,384,128]{2,1,0:T(8,128)(2,1)} %heads.1), calls=%async_computation.4 | async-start | bytes 1572864 | tf_op jit(solution)/shard_map/all_to_all | solution.py:623
  129.5 9.3 %collective-permute-start.14 = (bf16[2,96,128]{2,1,0:T(8,128)(2,1)}, bf16[2,96,128]{2,1,0:T(8,128)(2,1)S(1)}, u32[]{:S(2)}, u32[]{:S(2)}) collective-permute-start(bf16[2,96,128]{2,1,0:T(8,128)(2,1)} %get-tuple-element.78), channel_id=1, source_target_pairs={{0,80},{16,64},{32,112},{48,96},{64,16},{80,0},{96,48},{112,32},{1... | collective-permute-start | bytes 147464 | tf_op jit(solution)/shard_map/ppermute | solution.py:424
  134.4 6.6 %collective-permute-start.15 = (bf16[2,96,128]{2,1,0:T(8,128)(2,1)}, bf16[2,96,128]{2,1,0:T(8,128)(2,1)S(1)}, u32[]{:S(2)}, u32[]{:S(2)}) collective-permute-start(bf16[2,96,128]{2,1,0:T(8,128)(2,1)} %get-tuple-element.79), channel_id=1, source_target_pairs={{0,96},{16,112},{32,64},{48,80},{64,32},{80,48},{96,0},{112,16},{1... | collective-permute-start | bytes 147464 | tf_op jit(solution)/shard_map/ppermute | solution.py:424
  135.0 7.8 %collective-permute-start.16 = (bf16[2,96,128]{2,1,0:T(8,128)(2,1)}, bf16[2,96,128]{2,1,0:T(8,128)(2,1)S(1)}, u32[]{:S(2)}, u32[]{:S(2)}) collective-permute-start(bf16[2,96,128]{2,1,0:T(8,128)(2,1)} %get-tuple-element.80), channel_id=1, source_target_pairs={{0,112},{16,96},{32,80},{48,64},{64,48},{80,32},{96,16},{112,0},{1... | collective-permute-start | bytes 147464 | tf_op jit(solution)/shard_map/ppermute | solution.py:424
  148.0 4.1 %collective-permute-start.17 = (bf16[96,128]{1,0:T(8,128)(2,1)}, bf16[96,128]{1,0:T(8,128)(2,1)S(1)}, u32[]{:S(2)}, u32[]{:S(2)}) collective-permute-start(bf16[96,128]{1,0:T(8,128)(2,1)} %get-tuple-element.82), channel_id=1, source_target_pairs={{0,132},{132,0},{4,128},{128,4},{1,133},{133,1},{5,129},{129,5},{2... | collective-permute-start | bytes 73736 | tf_op jit(solution)/shard_map/ppermute | solution.py:420
  153.7 12.8 %all-to-all-start.5 = ((bf16[8,2,96,128]{3,2,1,0:T(8,128)(2,1)}), bf16[8,2,96,128]{3,2,1,0:T(8,128)(2,1)S(1)}, u32[]{:S(2)}, u32[]{:S(2)}) async-start(bf16[8,2,96,128]{3,2,1,0:T(8,128)(2,1)} %broadcast_in_dim.3), calls=%async_computation.5 | async-start | bytes 786432 | tf_op jit(solution)/shard_map/all_to_all | solution.py:625
  (16 other events, 66.2 us)
Sparse Core Ops, SparseCore 0:
  14.9 45.6 all-gather.4
  62.9 48.8 all-gather.6

commit v4 on v3

--- a/solution.py
+++ b/solution.py
@@ -492,6 +492,7 @@
         3,
     )
     shard_b = jnp.stack([own_b, swap_yh(own_b)])
+    shard_b, normed = barrier((shard_b, normed))
 
     conv, hidden, gated = run(
         functools.partial(gate_body, taps),
@@ -597,18 +598,7 @@
         zs + 2,
     )
     sums = [chunks[0]] + [pair_z(chunks[s], s) for s in range(1, zs)]
-    attn_in, *sums[1:5] = barrier((attn_in, *sums[1:5]))
-    keep, send = run(
-        sum_body,
-        [(chunk[1:], BF, HBM)] * 2,
-        [(one, ANY) for one in sums],
-        "share_sum",
-        [((zs,) + chunk, BF), (chunk, BF)],
-        zs + 2,
-    )
-    pair = jnp.stack([keep, swap_yh(send)])
-    pair = jnp.broadcast_to(pair, (blocks,) + pair.shape)
-
+    attn_in, *sums[1:3] = barrier((attn_in, *sums[1:3]))
     (back,) = run(
         functools.partial(heads_body, head_dim),
         [(back.shape, BF, HBM)],
@@ -618,7 +608,18 @@
         5,
         {4: 0},
     )
-    all_b, back = barrier((all_b, back))
+    keep, send = run(
+        sum_body,
+        [(chunk[1:], BF, HBM)] * 2,
+        [(one, ANY) for one in sums[:3]] + [(one, VMEM) for one in sums[3:]],
+        "share_sum",
+        [((zs,) + chunk, BF), (chunk, BF)],
+        zs + 2,
+    )
+    all_b, back, keep, send = barrier((all_b, back, keep, send))
+    pair = jnp.stack([keep, swap_yh(send)])
+    pair = jnp.broadcast_to(pair, (blocks,) + pair.shape)
+
     other_b = swap_core(all_b)
     back = lax.all_to_all(back, CTX, 0, 0, tiled=True)
     pair, back = barrier((pair, back))

time: 177 us -> 169 us (0.955)
  blocking collectives: 11.9 us -> 25.3 us
  starting transfers between devices: 65.1 us -> 53.6 us
  local copies, waits for them, and re-layouts: 8.03 us -> 0.86 us
  waiting for transfers between devices: 34.6 us -> 30.4 us
    all_to_all x0 -> x1, blocking collectives: none -> 13.4 us  [local(): lax.all_to_all(conv, CTX, 0, 0, tiled=True).reshape(blocks, rows, width)]
    ppermute x11, waiting for transfers between devices: 20.7 us -> 10.2 us  [pair_z(): lax.ppermute(v, 'z', [(i, i ^ by) for i in range(lax.axis_size('z'))])]
    all_to_all x1, waiting for transfers between devices: 0.01 us -> 7.4 us  [local(): back = lax.all_to_all(back, CTX, 0, 0, tiled=True)]
    unnamed x31 -> x11, local copies, waits for them, and re-layouts: 7.21 us -> 0.04 us
    all_to_all x1 -> x0, starting transfers between devices: 6.42 us -> none  [local(): lax.all_to_all(conv, CTX, 0, 0, tiled=True).reshape(blocks, rows, width)]
    all_to_all x1 -> x0, waiting for transfers between devices: 5.39 us -> none  [local(): lax.all_to_all(conv, CTX, 0, 0, tiled=True).reshape(blocks, rows, width)]
    ppermute x11, starting transfers between devices: 27.3 us -> 24.4 us  [pair_z(): lax.ppermute(v, 'z', [(i, i ^ by) for i in range(lax.axis_size('z'))])]
    ppermute x3, starting transfers between devices: 5.46 us -> 2.69 us  [swap_yh(): return lax.ppermute(v, ('yh', 'yl'), [(0, 3), (3, 0), (1, 2), (2, 1)])]
  transfers between devices with their start and end apart: 26 -> 25, of which waited for: 15 -> 10; matrix products, arithmetic and copies ran while one was open for 1% -> 2% of each run, Pallas kernels for 20% -> 21%
where the time goes in v4:
time: 169 us; the launch traced here: 166 us
  starting transfers between devices  53.6 us (32%)
  Pallas kernels  38.1 us (23%)
  waiting for transfers between devices  30.4 us (18%)
  blocking collectives  25.3 us (15%)
  between operations  14.3 us (8%)
  other arithmetic  3.17 us (2%)
    pallas_call x11, Pallas kernels, run(): pl.pallas_call(body, out_shape=tuple((o[2](o[0], o[1]) for o in outs)), i...  38.1 us
    ppermute x11, starting transfers between devices, pair_z(): lax.ppermute(v, 'z', [(i, i ^ by) for i in range(lax.axis_size('z'))])  24.4 us
    all_to_all x1, blocking collectives, local(): lax.all_to_all(conv, CTX, 0, 0, tiled=True).reshape(blocks, rows, width)  13.4 us
    all_to_all x1, blocking collectives, local(): grad_conv = lax.all_to_all(grad_conv, CTX, 0, 0, tiled=True)  11.9 us
    ppermute x11, waiting for transfers between devices, pair_z(): lax.ppermute(v, 'z', [(i, i ^ by) for i in range(lax.axis_size('z'))])  10.2 us
    all_to_all x1, starting transfers between devices, local(): back = lax.all_to_all(back, CTX, 0, 0, tiled=True)  8.02 us
    all_to_all x1, waiting for transfers between devices, local(): back = lax.all_to_all(back, CTX, 0, 0, tiled=True)  7.4 us
    all_to_all x1, starting transfers between devices, local(): lax.all_to_all(sent, CTX, 0, 0, tiled=True)  6.93 us
  transfers between devices with their start and end apart: 25, of which 10 were waited for; matrix products, arithmetic and copies ran while one was open for 2% of the time, Pallas kernels for 21%

profile of v4, /device:TPU:8, one launch (start us, length us, event | category | flops | bytes accessed | tf_op | source)
XLA Modules:
  0.0 165.8 jit_solution(15034370825076472209)
XLA Ops:
  10.7 2.6 %first_norm.1 = bf16[8,128,1024]{2,1,0:T(8,128)(2,1)} custom-call(bf16[128,1024]{1,0:T(8,128)(2,1)} %bitcast.35, f32[1,1024]{1,0:T(1,128)} %bitcast.50), custom_call_target="tpu_custom_call" | custom-call | tf_op jit(solution)/shard_map/first_norm/pallas_call | solution.py:26
  14.8 6.9 %all-to-all-start = ((bf16[8,128,1024]{2,1,0:T(8,128)(2,1)}), bf16[8,128,1024]{2,1,0:T(8,128)(2,1)S(1)}, u32[]{:S(2)}, u32[]{:S(2)}) async-start(bf16[8,128,1024]{2,1,0:T(8,128)(2,1)} %first_norm.1), calls=%async_computation | async-start | bytes 4194304 | tf_op jit(solution)/shard_map/all_to_all | solution.py:479
  24.4 2.0 %collective-permute-start.2 = (bf16[2,32,256]{2,1,0:T(8,128)(2,1)S(1)}, bf16[2,32,256]{2,1,0:T(8,128)(2,1)S(1)}, u32[]{:S(2)}, u32[]{:S(2)}) collective-permute-start(bf16[2,32,256]{2,1,0:T(8,128)(2,1)S(1)} %get-tuple-element.103), channel_id=1, source_target_pairs={{0,16},{16,0},{32,48},{48,32},{64,80},{80,64},{96,112},{112,96},{1... | collective-permute-start | bytes 98312 | tf_op jit(solution)/shard_map/ppermute | solution.py:424
  26.4 2.0 %collective-permute-done.2 = bf16[2,32,256]{2,1,0:T(8,128)(2,1)S(1)} collective-permute-done((bf16[2,32,256]{2,1,0:T(8,128)(2,1)S(1)}, bf16[2,32,256]{2,1,0:T(8,128)(2,1)S(1)}, u32[]{:S(2)}, u32[]{:S(2)}) %collective-permute-start.2) | collective-permute-done | bytes 32800 | tf_op jit(solution)/shard_map/ppermute | solution.py:424
  28.4 3.4 %collective-permute-start.3 = (bf16[2,2,32,256]{3,2,1,0:T(8,128)(2,1)S(1)}, bf16[2,2,32,256]{3,2,1,0:T(8,128)(2,1)S(1)}, u32[]{:S(2)}, u32[]{:S(2)}) collective-permute-start(bf16[2,2,32,256]{3,2,1,0:T(8,128)(2,1)S(1)} %pad_maximum_fusion.2), channel_id=1, source_target_pairs={{0,32},{16,48},{32,0},{48,16},{64,96},{80,112},{96,64},{112,80},{1... | collective-permute-start | bytes 196616 | tf_op jit(solution)/shard_map/ppermute | solution.py:424
  31.8 5.4 %collective-permute-start.4 = (bf16[2,2,32,256]{3,2,1,0:T(8,128)(2,1)S(1)}, bf16[2,2,32,256]{3,2,1,0:T(8,128)(2,1)S(1)}, u32[]{:S(2)}, u32[]{:S(2)}) collective-permute-start(bf16[2,2,32,256]{3,2,1,0:T(8,128)(2,1)S(1)} %pad_maximum_fusion.2), channel_id=1, source_target_pairs={{0,64},{16,80},{32,96},{48,112},{64,0},{80,16},{96,32},{112,48},{1... | collective-permute-start | bytes 196616 | tf_op jit(solution)/shard_map/ppermute | solution.py:424
  37.2 6.9 %collective-permute-done.4 = bf16[2,2,32,256]{3,2,1,0:T(8,128)(2,1)S(1)} collective-permute-done((bf16[2,2,32,256]{3,2,1,0:T(8,128)(2,1)S(1)}, bf16[2,2,32,256]{3,2,1,0:T(8,128)(2,1)S(1)}, u32[]{:S(2)}, u32[]{:S(2)}) %collective-permute-start.4) | collective-permute-done | bytes 65568 | tf_op jit(solution)/shard_map/ppermute | solution.py:424
  47.1 3.9 %gate_conv.1 = (bf16[8,2,64,128]{3,2,1,0:T(8,128)(2,1)}, f32[2,512,256]{2,1,0:T(8,128)}, bf16[2,512,128]{2,1,0:T(8,128)(2,1)}) custom-call(s32[2]{0:T(128)S(1)} %copy-done.1, bf16[8,2,64,1024]{3,2,1,0:T(8,128)(2,1)S(1)} %bitcast.28, bf16[8,2,32,256]{3,2,1,0:T(8,128)(2,1)S(1)} %constant_dynamic-update-slice_fusion.wm, ...), custom_call_target="tpu_custom_call" | custom-call | tf_op jit(solution)/shard_map/gate_conv/pallas_call | solution.py:26
  51.0 13.4 %all_to_all.30 = bf16[8,2,64,128]{3,2,1,0:T(8,128)(2,1)} all-to-all(bf16[8,2,64,128]{3,2,1,0:T(8,128)(2,1)} %get-tuple-element.60), channel_id=1, replica_groups=mesh['yh'=2,'z'=8,'core'=2,'yl'=2,'x'=4] {'yl','x'}, dimensions={0} | all-to-all | bytes 524288 | tf_op jit(solution)/shard_map/all_to_all | solution.py:517
  64.6 3.4 %collective-permute-done.7.other = bf16[8,2,32,1408]{3,2,1,0:T(8,128)(2,1)S(1)} collective-permute-done((bf16[8,2,32,1408]{3,2,1,0:T(8,128)(2,1)}, bf16[8,2,32,1408]{3,2,1,0:T(8,128)(2,1)S(1)}, u32[]{:S(2)}, u32[]{:S(2)}) %collective-permute-start.7) | collective-permute-done | bytes 1441824 | tf_op jit(solution)/shard_map/ppermute | solution.py:416
  68.0 4.5 %token_rows.1 = (bf16[8,128,1024]{2,1,0:T(8,128)(2,1)}, bf16[128,1024]{1,0:T(8,128)(2,1)}, bf16[8,128,128]{2,1,0:T(8,128)(2,1)}) custom-call(bf16[8,128,128]{2,1,0:T(8,128)(2,1)} %bitcast.40, bf16[8,2,32,1408]{3,2,1,0:T(8,128)(2,1)} %bitcast.31, bf16[8,2,32,1408]{3,2,1,0:T(8,128)(2,1)S(1)} %collective-permute-done.7.other, bf16[128,1024]{1,0:T(8,128)(2,1)} %bitcast.36, ...), custom_call_target="tpu_custom_call" | custom-call | tf_op jit(solution)/shard_map/token_rows/pallas_call | solution.py:26
  72.5 11.9 %all_to_all.31 = bf16[8,128,128]{2,1,0:T(8,128)(2,1)} all-to-all(bf16[8,128,128]{2,1,0:T(8,128)(2,1)} %get-tuple-element.66), channel_id=1, replica_groups=mesh['yh'=2,'z'=8,'core'=2,'yl'=2,'x'=4] {'yl','x'}, dimensions={0} | all-to-all | bytes 524288 | tf_op jit(solution)/shard_map/all_to_all | solution.py:548
  84.4 5.7 %all-to-all-start.3 = ((bf16[8,128,1024]{2,1,0:T(8,128)(2,1)}), bf16[8,128,1024]{2,1,0:T(8,128)(2,1)}, u32[]{:S(2)}, u32[]{:S(2)}) async-start(bf16[8,128,1024]{2,1,0:T(8,128)(2,1)} %get-tuple-element.67), calls=%async_computation.3 | async-start | bytes 4194304 | tf_op jit(solution)/shard_map/all_to_all | solution.py:551
  90.2 6.1 %conv_back.1 = (bf16[8,384,128]{2,1,0:T(8,128)(2,1)}, bf16[2,8,32,256]{3,2,1,0:T(8,128)(2,1)}, bf16[2,8,32,256]{3,2,1,0:T(8,128)(2,1)}, f32[16,256]{1,0:T(8,128)}) custom-call(s32[2]{0:T(128)S(1)} %copy-done.1, bf16[8,2,64,128]{3,2,1,0:T(8,128)(2,1)} %bitcast.41, bf16[8,2,64,1024]{3,2,1,0:T(8,128)(2,1)S(1)} %bitcast.29, ...), custom_call_target="tpu_custom_call" | custom-call | tf_op jit(solution)/shard_map/conv_back/pallas_call | solution.py:26
  98.2 1.9 %pair_sum.1 = (bf16[2,96,128]{2,1,0:T(8,128)(2,1)}, bf16[2,96,128]{2,1,0:T(8,128)(2,1)}, bf16[2,96,128]{2,1,0:T(8,128)(2,1)}, bf16[2,96,128]{2,1,0:T(8,128)(2,1)...) custom-call(bf16[2,8,32,256]{3,2,1,0:T(8,128)(2,1)} %get-tuple-eleme, ...), custom_call_target="tpu_custom_call" | custom-call | tf_op jit(solution)/shard_map/pair_sum/pallas_call | solution.py:26
  104.6 3.5 %collective-permute-start.13 = (bf16[2,96,128]{2,1,0:T(8,128)(2,1)}, bf16[2,96,128]{2,1,0:T(8,128)(2,1)S(1)}, u32[]{:S(2)}, u32[]{:S(2)}) collective-permute-start(bf16[2,96,128]{2,1,0:T(8,128)(2,1)} %get-tuple-element.82), channel_id=1, source_target_pairs={{0,64},{16,80},{32,96},{48,112},{64,0},{80,16},{96,32},{112,48},{1... | collective-permute-start | bytes 147464 | tf_op jit(solution)/shard_map/ppermute | solution.py:424
  109.7 3.0 %collective-permute-start.15 = (bf16[2,96,128]{2,1,0:T(8,128)(2,1)}, bf16[2,96,128]{2,1,0:T(8,128)(2,1)S(1)}, u32[]{:S(2)}, u32[]{:S(2)}) collective-permute-start(bf16[2,96,128]{2,1,0:T(8,128)(2,1)} %get-tuple-element.84), channel_id=1, source_target_pairs={{0,96},{16,112},{32,64},{48,80},{64,32},{80,48},{96,0},{112,16},{1... | collective-permute-start | bytes 147464 | tf_op jit(solution)/shard_map/ppermute | solution.py:424
  113.7 2.1 %all-to-all-done.3 = bf16[8,128,1024]{2,1,0:T(8,128)(2,1)} async-done(((bf16[8,128,1024]{2,1,0:T(8,128)(2,1)}), bf16[8,128,1024]{2,1,0:T(8,128)(2,1)}, u32[]{:S(2)}, u32[]{:S(2)}) %all-to-all-start.3) | async-done | bytes 2097184 | tf_op jit(solution)/shard_map/all_to_all | solution.py:551
  115.9 7.3 %heads.1 = bf16[8,384,128]{2,1,0:T(8,128)(2,1)} custom-call(s32[2]{0:T(128)S(1)} %copy-done.1, bf16[8,2,64,1024]{3,2,1,0:T(8,128)(2,1)} %bitcast.17.x, bf16[8,2,32,1408]{3,2,1,0:T(8,128)(2,1)} %bitcast.32, bf16[8,2,32,1408]{3,2,1,0:T(8,128)(2,1)S(1)} %collective-permute-done.7.other, ...), custom_call_target="tpu_custom_call", output_to_operand_aliasing={{}: (4, {})} | custom-call | tf_op jit(solution)/shard_map/heads/pallas_call | solution.py:26
  124.9 8.0 %all-to-all-start.4 = ((bf16[8,384,128]{2,1,0:T(8,128)(2,1)}), bf16[8,384,128]{2,1,0:T(8,128)(2,1)}, u32[]{:S(2)}, u32[]{:S(2)}) async-start(bf16[8,384,128]{2,1,0:T(8,128)(2,1)} %heads.1), calls=%async_computation.4 | async-start | bytes 1572864 | tf_op jit(solution)/shard_map/all_to_all | solution.py:624
  132.9 4.0 %collective-permute-done.17 = bf16[96,128]{1,0:T(8,128)(2,1)S(1)} collective-permute-done((bf16[96,128]{1,0:T(8,128)(2,1)}, bf16[96,128]{1,0:T(8,128)(2,1)S(1)}, u32[]{:S(2)}, u32[]{:S(2)}) %collective-permute-start.17) | collective-permute-done | bytes 24608 | tf_op jit(solution)/shard_map/ppermute | solution.py:420
  137.7 7.4 %all-to-all-done.4.a = bf16[8,384,128]{2,1,0:T(8,128)(2,1)} async-done(((bf16[8,384,128]{2,1,0:T(8,128)(2,1)}), bf16[8,384,128]{2,1,0:T(8,128)(2,1)}, u32[]{:S(2)}, u32[]{:S(2)}) %all-to-all-start.4) | async-done | bytes 786464 | tf_op jit(solution)/shard_map/all_to_all | solution.py:624
  145.9 4.8 %all-to-all-start.5 = ((bf16[8,2,96,128]{3,2,1,0:T(8,128)(2,1)}), bf16[8,2,96,128]{3,2,1,0:T(8,128)(2,1)S(1)}, u32[]{:S(2)}, u32[]{:S(2)}) async-start(bf16[8,2,96,128]{3,2,1,0:T(8,128)(2,1)} %broadcast_in_dim.3), calls=%async_computation.5 | async-start | bytes 786432 | tf_op jit(solution)/shard_map/all_to_all | solution.py:626
  150.8 6.2 %result_rows.1 = (bf16[128,1024]{1,0:T(8,128)(2,1)}, bf16[128,1024]{1,0:T(8,128)(2,1)}) custom-call(s32[2]{0:T(128)S(1)} %copy-done.1, bf16[8,384,128]{2,1,0:T(8,128)(2,1)} %all-to-all-done.4.a, bf16[8,2,32,3072]{3,2,1,0:T(8,128)(2,1)} %bitcast.34, bf16[8,2,32,3072]{3,2,1,0:T(8,128)(2,1)S(1)} %collective-permute-done.18.other, ...), custom_call_target="tpu_custom_call" | custom-call | tf_op jit(solution)/shard_map/result_rows/pallas_call | solution.py:26
  (62 shorter events, 24.9 us)
Async XLA Ops:
  7.2 57.3 %all-gather.5.cloned.1.call-start = ((), (), s32[]{:S(2)}) async-start(), calls=%async_computation.6 | async-start | bytes 1622016 | tf_op jit(solution)/shard_map/all_gather | solution.py:478
  9.0 5.0 %collective-permute-start.1 = (bf16[32,1664]{1,0:T(8,128)(2,1)}, bf16[32,1664]{1,0:T(8,128)(2,1)S(1)}, u32[]{:S(2)}, u32[]{:S(2)}) collective-permute-start(bf16[32,1664]{1,0:T(8,128)(2,1)} %get-tuple-element.53), channel_id=1, source_target_pairs={{0,132},{132,0},{4,128},{128,4},{1,133},{133,1},{5,129},{129,5},{2... | collective-permute-start | bytes 319496 | tf_op jit(solution)/shard_map/ppermute | solution.py:420
  14.8 32.3 %all-to-all-start = ((bf16[8,128,1024]{2,1,0:T(8,128)(2,1)}), bf16[8,128,1024]{2,1,0:T(8,128)(2,1)S(1)}, u32[]{:S(2)}, u32[]{:S(2)}) async-start(bf16[8,128,1024]{2,1,0:T(8,128)(2,1)} %first_norm.1), calls=%async_computation | async-start | bytes 4194304 | tf_op jit(solution)/shard_map/all_to_all | solution.py:479
  21.7 102.9 %all-gather.7.cloned.1.call-start = ((), (), s32[]{:S(2)}) async-start(), calls=%async_computation.7 | async-start | bytes 3538944 | tf_op jit(solution)/shard_map/all_gather | solution.py:521
  23.4 22.0 %collective-permute-start = (bf16[32,3072]{1,0:T(8,128)(2,1)}, bf16[32,3072]{1,0:T(8,128)(2,1)S(1)}, u32[]{:S(2)}, u32[]{:S(2)}) collective-permute-start(bf16[32,3072]{1,0:T(8,128)(2,1)} %pack.1), channel_id=1, source_target_pairs={{0,132},{132,0},{4,128},{128,4},{1,133},{133,1},{5,129},{129,5},{2... | collective-permute-start | bytes 589832 | tf_op jit(solution)/shard_map/ppermute | solution.py:420
  24.4 4.0 %collective-permute-start.2 = (bf16[2,32,256]{2,1,0:T(8,128)(2,1)S(1)}, bf16[2,32,256]{2,1,0:T(8,128)(2,1)S(1)}, u32[]{:S(2)}, u32[]{:S(2)}) collective-permute-start(bf16[2,32,256]{2,1,0:T(8,128)(2,1)S(1)} %get-tuple-element.103), channel_id=1, source_target_pairs={{0,16},{16,0},{32,48},{48,32},{64,80},{80,64},{96,112},{112,96},{1... | collective-permute-start | bytes 98312 | tf_op jit(solution)/shard_map/ppermute | solution.py:424
  28.4 8.8 %collective-permute-start.3 = (bf16[2,2,32,256]{3,2,1,0:T(8,128)(2,1)S(1)}, bf16[2,2,32,256]{3,2,1,0:T(8,128)(2,1)S(1)}, u32[]{:S(2)}, u32[]{:S(2)}) collective-permute-start(bf16[2,2,32,256]{3,2,1,0:T(8,128)(2,1)S(1)} %pad_maximum_fusion.2), channel_id=1, source_target_pairs={{0,32},{16,48},{32,0},{48,16},{64,96},{80,112},{96,64},{112,80},{1... | collective-permute-start | bytes 196616 | tf_op jit(solution)/shard_map/ppermute | solution.py:424
  31.8 12.3 %collective-permute-start.4 = (bf16[2,2,32,256]{3,2,1,0:T(8,128)(2,1)S(1)}, bf16[2,2,32,256]{3,2,1,0:T(8,128)(2,1)S(1)}, u32[]{:S(2)}, u32[]{:S(2)}) collective-permute-start(bf16[2,2,32,256]{3,2,1,0:T(8,128)(2,1)S(1)} %pad_maximum_fusion.2), channel_id=1, source_target_pairs={{0,64},{16,80},{32,96},{48,112},{64,0},{80,16},{96,32},{112,48},{1... | collective-permute-start | bytes 196616 | tf_op jit(solution)/shard_map/ppermute | solution.py:424
  37.2 8.2 %collective-permute-start.5 = (bf16[2,2,32,256]{3,2,1,0:T(8,128)(2,1)S(1)}, bf16[2,2,32,256]{3,2,1,0:T(8,128)(2,1)S(1)}, u32[]{:S(2)}, u32[]{:S(2)}) collective-permute-start(bf16[2,2,32,256]{3,2,1,0:T(8,128)(2,1)S(1)} %pad_maximum_fusion.2), channel_id=1, source_target_pairs={{0,96},{16,112},{32,64},{48,80},{64,32},{80,48},{96,0},{112,16},{1... | collective-permute-start | bytes 196616 | tf_op jit(solution)/shard_map/ppermute | solution.py:424
  64.5 3.5 %collective-permute-start.7 = (bf16[8,2,32,1408]{3,2,1,0:T(8,128)(2,1)}, bf16[8,2,32,1408]{3,2,1,0:T(8,128)(2,1)S(1)}, u32[]{:S(2)}, u32[]{:S(2)}) collective-permute-start(bf16[8,2,32,1408]{3,2,1,0:T(8,128)(2,1)} %bitcast.30), channel_id=1, source_target_pairs={{0,8},{8,0},{1,9},{9,1},{2,10},{10,2},{3,11},{11,3},{4,12},{12,4},... | collective-permute-start | bytes 4325384 | tf_op jit(solution)/shard_map/ppermute | solution.py:416
  84.4 31.5 %all-to-all-start.3 = ((bf16[8,128,1024]{2,1,0:T(8,128)(2,1)}), bf16[8,128,1024]{2,1,0:T(8,128)(2,1)}, u32[]{:S(2)}, u32[]{:S(2)}) async-start(bf16[8,128,1024]{2,1,0:T(8,128)(2,1)} %get-tuple-element.67), calls=%async_computation.3 | async-start | bytes 4194304 | tf_op jit(solution)/shard_map/all_to_all | solution.py:551
  96.3 1.9 %collective-permute-start.8 = (bf16[2,8,32,256]{3,2,1,0:T(8,128)(2,1)}, bf16[2,8,32,256]{3,2,1,0:T(8,128)(2,1)S(1)}, u32[]{:S(2)}, u32[]{:S(2)}) collective-permute-start(bf16[2,8,32,256]{3,2,1,0:T(8,128)(2,1)} %get-tuple-element.72), channel_id=1, source_target_pairs={{0,8},{8,0},{1,9},{9,1},{2,10},{10,2},{3,11},{11,3},{4,12},{12,4},... | collective-permute-start | bytes 786440 | tf_op jit(solution)/shard_map/ppermute | solution.py:416
  96.4 1.8 %collective-permute-start.9 = (f32[16,256]{1,0:T(8,128)}, f32[16,256]{1,0:T(8,128)S(1)}, u32[]{:S(2)}, u32[]{:S(2)}) collective-permute-start(f32[16,256]{1,0:T(8,128)} %get-tuple-element.73.gk), channel_id=1, source_target_pairs={{0,8},{8,0},{1,9},{9,1},{2,10},{10,2},{3,11},{11,3},{4,12},{12,4},... | collective-permute-start | bytes 49160 | tf_op jit(solution)/shard_map/ppermute | solution.py:416
  100.1 9.6 %collective-permute-start.10 = (bf16[2,96,128]{2,1,0:T(8,128)(2,1)}, bf16[2,96,128]{2,1,0:T(8,128)(2,1)S(1)}, u32[]{:S(2)}, u32[]{:S(2)}) collective-permute-start(bf16[2,96,128]{2,1,0:T(8,128)(2,1)} %get-tuple-element.74), channel_id=1, source_target_pairs={{0,16},{16,0},{32,48},{48,32},{64,80},{80,64},{96,112},{112,96},{1... | collective-permute-start | bytes 147464 | tf_op jit(solution)/shard_map/ppermute | solution.py:424
  101.7 11.0 %collective-permute-start.11 = (bf16[2,96,128]{2,1,0:T(8,128)(2,1)}, bf16[2,96,128]{2,1,0:T(8,128)(2,1)S(1)}, u32[]{:S(2)}, u32[]{:S(2)}) collective-permute-start(bf16[2,96,128]{2,1,0:T(8,128)(2,1)} %get-tuple-element.75), channel_id=1, source_target_pairs={{0,32},{16,48},{32,0},{48,16},{64,96},{80,112},{96,64},{112,80},{1... | collective-permute-start | bytes 147464 | tf_op jit(solution)/shard_map/ppermute | solution.py:424
  102.8 20.4 %collective-permute-start.12 = (bf16[2,96,128]{2,1,0:T(8,128)(2,1)}, bf16[2,96,128]{2,1,0:T(8,128)(2,1)S(1)}, u32[]{:S(2)}, u32[]{:S(2)}) collective-permute-start(bf16[2,96,128]{2,1,0:T(8,128)(2,1)} %get-tuple-element.81), channel_id=1, source_target_pairs={{0,48},{16,32},{32,16},{48,0},{64,112},{80,96},{96,80},{112,64},{1... | collective-permute-start | bytes 147464 | tf_op jit(solution)/shard_map/ppermute | solution.py:424
  104.6 18.7 %collective-permute-start.13 = (bf16[2,96,128]{2,1,0:T(8,128)(2,1)}, bf16[2,96,128]{2,1,0:T(8,128)(2,1)S(1)}, u32[]{:S(2)}, u32[]{:S(2)}) collective-permute-start(bf16[2,96,128]{2,1,0:T(8,128)(2,1)} %get-tuple-element.82), channel_id=1, source_target_pairs={{0,64},{16,80},{32,96},{48,112},{64,0},{80,16},{96,32},{112,48},{1... | collective-permute-start | bytes 147464 | tf_op jit(solution)/shard_map/ppermute | solution.py:424
  108.1 15.2 %collective-permute-start.14 = (bf16[2,96,128]{2,1,0:T(8,128)(2,1)}, bf16[2,96,128]{2,1,0:T(8,128)(2,1)S(1)}, u32[]{:S(2)}, u32[]{:S(2)}) collective-permute-start(bf16[2,96,128]{2,1,0:T(8,128)(2,1)} %get-tuple-element.83), channel_id=1, source_target_pairs={{0,80},{16,64},{32,112},{48,96},{64,16},{80,0},{96,48},{112,32},{1... | collective-permute-start | bytes 147464 | tf_op jit(solution)/shard_map/ppermute | solution.py:424
  109.7 13.5 %collective-permute-start.15 = (bf16[2,96,128]{2,1,0:T(8,128)(2,1)}, bf16[2,96,128]{2,1,0:T(8,128)(2,1)S(1)}, u32[]{:S(2)}, u32[]{:S(2)}) collective-permute-start(bf16[2,96,128]{2,1,0:T(8,128)(2,1)} %get-tuple-element.84), channel_id=1, source_target_pairs={{0,96},{16,112},{32,64},{48,80},{64,32},{80,48},{96,0},{112,16},{1... | collective-permute-start | bytes 147464 | tf_op jit(solution)/shard_map/ppermute | solution.py:424
  112.7 10.5 %collective-permute-start.16 = (bf16[2,96,128]{2,1,0:T(8,128)(2,1)}, bf16[2,96,128]{2,1,0:T(8,128)(2,1)S(1)}, u32[]{:S(2)}, u32[]{:S(2)}) collective-permute-start(bf16[2,96,128]{2,1,0:T(8,128)(2,1)} %get-tuple-element.85), channel_id=1, source_target_pairs={{0,112},{16,96},{32,80},{48,64},{64,48},{80,32},{96,16},{112,0},{1... | collective-permute-start | bytes 147464 | tf_op jit(solution)/shard_map/ppermute | solution.py:424
  124.6 26.2 %collective-permute-start.18 = (bf16[8,2,32,3072]{3,2,1,0:T(8,128)(2,1)}, bf16[8,2,32,3072]{3,2,1,0:T(8,128)(2,1)S(1)}, u32[]{:S(2)}, u32[]{:S(2)}) collective-permute-start(bf16[8,2,32,3072]{3,2,1,0:T(8,128)(2,1)} %bitcast.33), channel_id=1, source_target_pairs={{0,8},{8,0},{1,9},{9,1},{2,10},{10,2},{3,11},{11,3},{4,12},{12,4},... | collective-permute-start | bytes 9437192 | tf_op jit(solution)/shard_map/ppermute | solution.py:416
  124.9 20.2 %all-to-all-start.4 = ((bf16[8,384,128]{2,1,0:T(8,128)(2,1)}), bf16[8,384,128]{2,1,0:T(8,128)(2,1)}, u32[]{:S(2)}, u32[]{:S(2)}) async-start(bf16[8,384,128]{2,1,0:T(8,128)(2,1)} %heads.1), calls=%async_computation.4 | async-start | bytes 1572864 | tf_op jit(solution)/shard_map/all_to_all | solution.py:624
  132.9 4.0 %collective-permute-start.17 = (bf16[96,128]{1,0:T(8,128)(2,1)}, bf16[96,128]{1,0:T(8,128)(2,1)S(1)}, u32[]{:S(2)}, u32[]{:S(2)}) collective-permute-start(bf16[96,128]{1,0:T(8,128)(2,1)} %get-tuple-element.89), channel_id=1, source_target_pairs={{0,132},{132,0},{4,128},{128,4},{1,133},{133,1},{5,129},{129,5},{2... | collective-permute-start | bytes 73736 | tf_op jit(solution)/shard_map/ppermute | solution.py:420
  145.9 12.2 %all-to-all-start.5 = ((bf16[8,2,96,128]{3,2,1,0:T(8,128)(2,1)}), bf16[8,2,96,128]{3,2,1,0:T(8,128)(2,1)S(1)}, u32[]{:S(2)}, u32[]{:S(2)}) async-start(bf16[8,2,96,128]{3,2,1,0:T(8,128)(2,1)} %broadcast_in_dim.3), calls=%async_computation.5 | async-start | bytes 786432 | tf_op jit(solution)/shard_map/all_to_all | solution.py:626
  (5 other events, 56.1 us)
Sparse Core Ops, SparseCore 0:
  14.9 46.3 all-gather.4
  64.6 45.2 all-gather.6

commit v5 on v4

--- a/solution.py
+++ b/solution.py
@@ -237,6 +237,7 @@
     for ref in (pad_s, gpad_s):
         ref[0:16] = zeros
         ref[16 + length : 32 + length] = zeros
+    going = []
     wait(get_k, get_gc, get_gated)
     for rec in range(records):
         pad_s[16 : 16 + length] = gc_s[:, rec].reshape(length, width).astype(F32)
@@ -264,6 +265,11 @@
             gh_s[base : base + local, width:] = second
             out_s[b, rec * local : (rec + 1) * local] = first
             out_s[b, rows + rec * local : rows + (rec + 1) * local] = second
+        for part in range(2):
+            at = part * rows + rec * local
+            going.append(
+                copies.start(out_s.at[:, at : at + local], back.at[:, at : at + local])
+            )
         grad_first = lax.dot_general(
             x[:, rec].reshape(length, model),
             gh_s[...],
@@ -282,7 +288,7 @@
         copies.start(both_s.at[:, :, 1 - core], send),
         copies.start(gko_s, gk_out),
         copies.start(both_s.at[:, :, core], keep),
-        copies.start(out_s, back.at[:, : 2 * rows]),
+        *going,
     )
 
 
@@ -318,6 +324,12 @@
     wait(copies.start(total_s.at[1 - yh], send), copies.start(total_s.at[yh], keep))
 
 
+def spread_body(keep, recv, out, pair_s, sems):
+    copies = Copies(sems)
+    wait(copies.start(keep, pair_s.at[0]), copies.start(recv, pair_s.at[1]))
+    wait(*[copies.start(pair_s, out.at[i]) for i in range(out.shape[0])])
+
+
 def heads_body(head_dim, frames, x, mine, other, held, back, w, att_s, sems):
     del held
     copies = Copies(sems)
@@ -332,19 +344,20 @@
     for rec in range(records):
         packed = dot(x[:, rec].reshape(length, model), w[...].reshape(model, 3 * width))
         packed = packed.astype(BF)
-        q = packed[:, :width]
+        q = packed[:, :width] * jnp.asarray(scaling, BF)
         k = packed[:, width : 2 * width]
         v = packed[:, 2 * width :]
-        key_ok = lax.broadcasted_iota(jnp.int32, (rows, length), 1) < frames[rec]
+        bias = jnp.where(
+            lax.broadcasted_iota(jnp.int32, (1, length), 1) < frames[rec], 0.0, -1e30
+        )
         for r in range(0, length, rows):
             qr = q[r : r + rows]
             attended = jnp.zeros((rows, width), F32)
             for h in range(width // head_dim):
                 here = (lane >= h * head_dim) & (lane < (h + 1) * head_dim)
-                scores = dot_t(jnp.where(here, qr, jnp.zeros_like(qr)), k) * scaling
-                scores = jnp.where(key_ok, scores, -1e30)
+                scores = dot_t(jnp.where(here, qr, jnp.zeros_like(qr)), k) + bias
                 top = jnp.max(scores, -1, keepdims=True)
-                numer = jnp.where(key_ok, jnp.exp(scores - top), 0.0)
+                numer = jnp.exp(scores - top)
                 denom = jnp.sum(numer, -1, keepdims=True)
                 attended = jnp.where(here, dot(numer.astype(BF), v) / denom, attended)
             got = attended.astype(BF).reshape(rows // local, local, width)
@@ -492,8 +505,6 @@
         3,
     )
     shard_b = jnp.stack([own_b, swap_yh(own_b)])
-    shard_b, normed = barrier((shard_b, normed))
-
     conv, hidden, gated = run(
         functools.partial(gate_body, taps),
         [
@@ -580,7 +591,7 @@
             ((blocks, 2 * rows, width), BF),
             ((16, 2 * width), F32),
         ],
-        8,
+        7 + 2 * records,
     )
 
     chunk = (2, 2 * tall, width)
@@ -617,8 +628,14 @@
         zs + 2,
     )
     all_b, back, keep, send = barrier((all_b, back, keep, send))
-    pair = jnp.stack([keep, swap_yh(send)])
-    pair = jnp.broadcast_to(pair, (blocks,) + pair.shape)
+    (pair,) = run(
+        spread_body,
+        [((blocks,) + chunk, BF, HBM)],
+        [(keep, HBM), (swap_yh(send), ANY)],
+        "spread",
+        [(chunk, BF)],
+        blocks + 2,
+    )
 
     other_b = swap_core(all_b)
     back = lax.all_to_all(back, CTX, 0, 0, tiled=True)

time: 169 us -> 166 us (0.982)
  blocking collectives: 25.3 us -> 11.9 us
  starting transfers between devices: 53.6 us -> 59.9 us
  waiting for transfers between devices: 30.4 us -> 35.3 us
    all_to_all x1 -> x0, blocking collectives: 13.4 us -> none  [local(): lax.all_to_all(conv, CTX, 0, 0, tiled=True).reshape(blocks, rows, width)]
    all_to_all x0 -> x1, starting transfers between devices: none -> 6.43 us  [local(): lax.all_to_all(conv, CTX, 0, 0, tiled=True).reshape(blocks, rows, width)]
    all_to_all x0 -> x1, waiting for transfers between devices: none -> 5.4 us  [local(): lax.all_to_all(conv, CTX, 0, 0, tiled=True).reshape(blocks, rows, width)]
    pallas_call x11 -> x12, Pallas kernels: 38.1 us -> 39.5 us  [run(): pl.pallas_call(body, out_shape=tuple((o[2](o[0], o[1]) for o in outs)), i...]
  transfers between devices with their start and end apart: 25 -> 26, of which waited for: 10 -> 12; matrix products, arithmetic and copies ran while one was open for 2% -> 1% of each run, Pallas kernels for 21% -> 23%
where the time goes in v5:
time: 166 us; the launch traced here: 163 us
  starting transfers between devices  59.9 us (36%)
  Pallas kernels  39.5 us (24%)
  waiting for transfers between devices  35.3 us (21%)
  between operations  14.3 us (9%)
  blocking collectives  11.9 us (7%)
    pallas_call x12, Pallas kernels, run(): pl.pallas_call(body, out_shape=tuple((o[2](o[0], o[1]) for o in outs)), i...  39.5 us
    ppermute x11, starting transfers between devices, pair_z(): lax.ppermute(v, 'z', [(i, i ^ by) for i in range(lax.axis_size('z'))])  23.4 us
    all_to_all x1, blocking collectives, local(): grad_conv = lax.all_to_all(grad_conv, CTX, 0, 0, tiled=True)  11.9 us
    ppermute x11, waiting for transfers between devices, pair_z(): lax.ppermute(v, 'z', [(i, i ^ by) for i in range(lax.axis_size('z'))])  10.7 us
    all_to_all x1, starting transfers between devices, local(): back = lax.all_to_all(back, CTX, 0, 0, tiled=True)  7.98 us
    all_to_all x1, starting transfers between devices, local(): lax.all_to_all(sent, CTX, 0, 0, tiled=True)  6.93 us
    all_to_all x1, waiting for transfers between devices, local(): back = lax.all_to_all(back, CTX, 0, 0, tiled=True)  6.56 us
    all_to_all x1, starting transfers between devices, local(): lax.all_to_all(conv, CTX, 0, 0, tiled=True).reshape(blocks, rows, width)  6.43 us
  transfers between devices with their start and end apart: 26, of which 12 were waited for; matrix products, arithmetic and copies ran while one was open for 1% of the time, Pallas kernels for 23%

profile of v5, /device:TPU:8, one launch (start us, length us, event | category | flops | bytes accessed | tf_op | source)
XLA Modules:
  0.0 163.2 jit_solution(2698583626646434193)
XLA Ops:
  10.7 2.6 %first_norm.1 = bf16[8,128,1024]{2,1,0:T(8,128)(2,1)} custom-call(bf16[128,1024]{1,0:T(8,128)(2,1)} %bitcast.33, f32[1,1024]{1,0:T(1,128)} %bitcast.46), custom_call_target="tpu_custom_call" | custom-call | tf_op jit(solution)/shard_map/first_norm/pallas_call | solution.py:26
  14.8 6.9 %all-to-all-start = ((bf16[8,128,1024]{2,1,0:T(8,128)(2,1)}), bf16[8,128,1024]{2,1,0:T(8,128)(2,1)S(1)}, u32[]{:S(2)}, u32[]{:S(2)}) async-start(bf16[8,128,1024]{2,1,0:T(8,128)(2,1)} %first_norm.1), calls=%async_computation | async-start | bytes 4194304 | tf_op jit(solution)/shard_map/all_to_all | solution.py:492
  22.8 2.9 %collective-permute-done.2 = bf16[2,32,256]{2,1,0:T(8,128)(2,1)S(1)} collective-permute-done((bf16[2,32,256]{2,1,0:T(8,128)(2,1)S(1)}, bf16[2,32,256]{2,1,0:T(8,128)(2,1)S(1)}, u32[]{:S(2)}, u32[]{:S(2)}) %collective-permute-start.2) | collective-permute-done | bytes 32800 | tf_op jit(solution)/shard_map/ppermute | solution.py:437
  25.7 2.5 %collective-permute-start.3 = (bf16[2,2,32,256]{3,2,1,0:T(8,128)(2,1)S(1)}, bf16[2,2,32,256]{3,2,1,0:T(8,128)(2,1)S(1)}, u32[]{:S(2)}, u32[]{:S(2)}) collective-permute-start(bf16[2,2,32,256]{3,2,1,0:T(8,128)(2,1)S(1)} %pad_maximum_fusion.2), channel_id=1, source_target_pairs={{0,32},{16,48},{32,0},{48,16},{64,96},{80,112},{96,64},{112,80},{1... | collective-permute-start | bytes 196616 | tf_op jit(solution)/shard_map/ppermute | solution.py:437
  28.2 5.4 %collective-permute-start.4 = (bf16[2,2,32,256]{3,2,1,0:T(8,128)(2,1)S(1)}, bf16[2,2,32,256]{3,2,1,0:T(8,128)(2,1)S(1)}, u32[]{:S(2)}, u32[]{:S(2)}) collective-permute-start(bf16[2,2,32,256]{3,2,1,0:T(8,128)(2,1)S(1)} %pad_maximum_fusion.2), channel_id=1, source_target_pairs={{0,64},{16,80},{32,96},{48,112},{64,0},{80,16},{96,32},{112,48},{1... | collective-permute-start | bytes 196616 | tf_op jit(solution)/shard_map/ppermute | solution.py:437
  33.6 6.4 %collective-permute-done.4 = bf16[2,2,32,256]{3,2,1,0:T(8,128)(2,1)S(1)} collective-permute-done((bf16[2,2,32,256]{3,2,1,0:T(8,128)(2,1)S(1)}, bf16[2,2,32,256]{3,2,1,0:T(8,128)(2,1)S(1)}, u32[]{:S(2)}, u32[]{:S(2)}) %collective-permute-start.4) | collective-permute-done | bytes 65568 | tf_op jit(solution)/shard_map/ppermute | solution.py:437
  43.1 2.0 %collective-permute-start = (bf16[32,3072]{1,0:T(8,128)(2,1)}, bf16[32,3072]{1,0:T(8,128)(2,1)S(1)}, u32[]{:S(2)}, u32[]{:S(2)}) collective-permute-start(bf16[32,3072]{1,0:T(8,128)(2,1)} %pack.1), channel_id=1, source_target_pairs={{0,132},{132,0},{4,128},{128,4},{1,133},{133,1},{5,129},{129,5},{2... | collective-permute-start | bytes 589832 | tf_op jit(solution)/shard_map/ppermute | solution.py:433
  45.5 3.9 %gate_conv.1 = (bf16[8,2,64,128]{3,2,1,0:T(8,128)(2,1)}, f32[2,512,256]{2,1,0:T(8,128)}, bf16[2,512,128]{2,1,0:T(8,128)(2,1)}) custom-call(s32[2]{0:T(128)S(1)} %copy-done.1, bf16[8,2,64,1024]{3,2,1,0:T(8,128)(2,1)S(1)} %bitcast.26, bf16[8,2,32,256]{3,2,1,0:T(8,128)(2,1)S(1)} %constant_dynamic-update-slice_fusion.wm, ...), custom_call_target="tpu_custom_call" | custom-call | tf_op jit(solution)/shard_map/gate_conv/pallas_call | solution.py:26
  49.4 6.4 %all-to-all-start.1 = ((bf16[8,2,64,128]{3,2,1,0:T(8,128)(2,1)}), bf16[8,2,64,128]{3,2,1,0:T(8,128)(2,1)S(1)}, u32[]{:S(2)}, u32[]{:S(2)}) async-start(bf16[8,2,64,128]{3,2,1,0:T(8,128)(2,1)} %get-tuple-element.56), calls=%async_computation.1 | async-start | bytes 524288 | tf_op jit(solution)/shard_map/all_to_all | solution.py:528
  56.6 5.4 %all-to-all-done.1 = bf16[8,2,64,128]{3,2,1,0:T(8,128)(2,1)S(1)} async-done(((bf16[8,2,64,128]{3,2,1,0:T(8,128)(2,1)}), bf16[8,2,64,128]{3,2,1,0:T(8,128)(2,1)S(1)}, u32[]{:S(2)}, u32[]{:S(2)}) %all-to-all-start.1) | async-done | bytes 262176 | tf_op jit(solution)/shard_map/all_to_all | solution.py:528
  62.8 3.4 %collective-permute-done.7.other = bf16[8,2,32,1408]{3,2,1,0:T(8,128)(2,1)S(1)} collective-permute-done((bf16[8,2,32,1408]{3,2,1,0:T(8,128)(2,1)}, bf16[8,2,32,1408]{3,2,1,0:T(8,128)(2,1)S(1)}, u32[]{:S(2)}, u32[]{:S(2)}) %collective-permute-start.7) | collective-permute-done | bytes 1441824 | tf_op jit(solution)/shard_map/ppermute | solution.py:429
  66.3 4.5 %token_rows.1 = (bf16[8,128,1024]{2,1,0:T(8,128)(2,1)}, bf16[128,1024]{1,0:T(8,128)(2,1)}, bf16[8,128,128]{2,1,0:T(8,128)(2,1)}) custom-call(bf16[8,128,128]{2,1,0:T(8,128)(2,1)} %bitcast.38, bf16[8,2,32,1408]{3,2,1,0:T(8,128)(2,1)} %bitcast.29, bf16[8,2,32,1408]{3,2,1,0:T(8,128)(2,1)S(1)} %collective-permute-done.7.other, bf16[128,1024]{1,0:T(8,128)(2,1)} %bitcast.34, ...), custom_call_target="tpu_custom_call" | custom-call | tf_op jit(solution)/shard_map/token_rows/pallas_call | solution.py:26
  70.8 11.9 %all_to_all.30 = bf16[8,128,128]{2,1,0:T(8,128)(2,1)} all-to-all(bf16[8,128,128]{2,1,0:T(8,128)(2,1)} %get-tuple-element.62), channel_id=1, replica_groups=mesh['yh'=2,'z'=8,'core'=2,'yl'=2,'x'=4] {'yl','x'}, dimensions={0} | all-to-all | bytes 524288 | tf_op jit(solution)/shard_map/all_to_all | solution.py:559
  82.7 5.7 %all-to-all-start.3 = ((bf16[8,128,1024]{2,1,0:T(8,128)(2,1)}), bf16[8,128,1024]{2,1,0:T(8,128)(2,1)}, u32[]{:S(2)}, u32[]{:S(2)}) async-start(bf16[8,128,1024]{2,1,0:T(8,128)(2,1)} %get-tuple-element.63), calls=%async_computation.3 | async-start | bytes 4194304 | tf_op jit(solution)/shard_map/all_to_all | solution.py:562
  88.4 6.0 %conv_back.1 = (bf16[8,384,128]{2,1,0:T(8,128)(2,1)}, bf16[2,8,32,256]{3,2,1,0:T(8,128)(2,1)}, bf16[2,8,32,256]{3,2,1,0:T(8,128)(2,1)}, f32[16,256]{1,0:T(8,128)}) custom-call(s32[2]{0:T(128)S(1)} %copy-done.1, bf16[8,2,64,128]{3,2,1,0:T(8,128)(2,1)} %bitcast.39, bf16[8,2,64,1024]{3,2,1,0:T(8,128)(2,1)S(1)} %bitcast.27, ...), custom_call_target="tpu_custom_call" | custom-call | tf_op jit(solution)/shard_map/conv_back/pallas_call | solution.py:26
  98.2 2.1 %collective-permute-start.10 = (bf16[2,96,128]{2,1,0:T(8,128)(2,1)}, bf16[2,96,128]{2,1,0:T(8,128)(2,1)S(1)}, u32[]{:S(2)}, u32[]{:S(2)}) collective-permute-start(bf16[2,96,128]{2,1,0:T(8,128)(2,1)} %get-tuple-element.70), channel_id=1, source_target_pairs={{0,16},{16,0},{32,48},{48,32},{64,80},{80,64},{96,112},{112,96},{1... | collective-permute-start | bytes 147464 | tf_op jit(solution)/shard_map/ppermute | solution.py:437
  102.7 5.2 %collective-permute-start.13 = (bf16[2,96,128]{2,1,0:T(8,128)(2,1)}, bf16[2,96,128]{2,1,0:T(8,128)(2,1)S(1)}, u32[]{:S(2)}, u32[]{:S(2)}) collective-permute-start(bf16[2,96,128]{2,1,0:T(8,128)(2,1)} %get-tuple-element.78), channel_id=1, source_target_pairs={{0,64},{16,80},{32,96},{48,112},{64,0},{80,16},{96,32},{112,48},{1... | collective-permute-start | bytes 147464 | tf_op jit(solution)/shard_map/ppermute | solution.py:437
  108.2 4.3 %collective-permute-start.15 = (bf16[2,96,128]{2,1,0:T(8,128)(2,1)}, bf16[2,96,128]{2,1,0:T(8,128)(2,1)S(1)}, u32[]{:S(2)}, u32[]{:S(2)}) collective-permute-start(bf16[2,96,128]{2,1,0:T(8,128)(2,1)} %get-tuple-element.80), channel_id=1, source_target_pairs={{0,96},{16,112},{32,64},{48,80},{64,32},{80,48},{96,0},{112,16},{1... | collective-permute-start | bytes 147464 | tf_op jit(solution)/shard_map/ppermute | solution.py:437
  114.1 7.3 %heads.1 = bf16[8,384,128]{2,1,0:T(8,128)(2,1)} custom-call(s32[2]{0:T(128)S(1)} %copy-done.1, bf16[8,2,64,1024]{3,2,1,0:T(8,128)(2,1)} %bitcast.17.x, bf16[8,2,32,1408]{3,2,1,0:T(8,128)(2,1)} %bitcast.30, bf16[8,2,32,1408]{3,2,1,0:T(8,128)(2,1)S(1)} %collective-permute-done.7.other, ...), custom_call_target="tpu_custom_call", output_to_operand_aliasing={{}: (4, {})} | custom-call | tf_op jit(solution)/shard_map/heads/pallas_call | solution.py:26
  123.1 8.0 %all-to-all-start.4 = ((bf16[8,384,128]{2,1,0:T(8,128)(2,1)}), bf16[8,384,128]{2,1,0:T(8,128)(2,1)}, u32[]{:S(2)}, u32[]{:S(2)}) async-start(bf16[8,384,128]{2,1,0:T(8,128)(2,1)} %heads.1), calls=%async_computation.4 | async-start | bytes 1572864 | tf_op jit(solution)/shard_map/all_to_all | solution.py:641
  131.1 4.0 %collective-permute-done.17.recv = bf16[96,128]{1,0:T(8,128)(2,1)S(1)} collective-permute-done((bf16[96,128]{1,0:T(8,128)(2,1)}, bf16[96,128]{1,0:T(8,128)(2,1)S(1)}, u32[]{:S(2)}, u32[]{:S(2)}) %collective-permute-start.17) | collective-permute-done | bytes 24608 | tf_op jit(solution)/shard_map/ppermute | solution.py:433
  136.8 6.6 %all-to-all-done.4.a = bf16[8,384,128]{2,1,0:T(8,128)(2,1)} async-done(((bf16[8,384,128]{2,1,0:T(8,128)(2,1)}), bf16[8,384,128]{2,1,0:T(8,128)(2,1)}, u32[]{:S(2)}, u32[]{:S(2)}) %all-to-all-start.4) | async-done | bytes 786464 | tf_op jit(solution)/shard_map/all_to_all | solution.py:641
  143.3 4.8 %all-to-all-start.5 = ((bf16[8,2,96,128]{3,2,1,0:T(8,128)(2,1)}), bf16[8,2,96,128]{3,2,1,0:T(8,128)(2,1)S(1)}, u32[]{:S(2)}, u32[]{:S(2)}) async-start(bf16[8,2,96,128]{3,2,1,0:T(8,128)(2,1)} %spread.1), calls=%async_computation.5 | async-start | bytes 786432 | tf_op jit(solution)/shard_map/all_to_all | solution.py:643
  148.2 6.2 %result_rows.1 = (bf16[128,1024]{1,0:T(8,128)(2,1)}, bf16[128,1024]{1,0:T(8,128)(2,1)}) custom-call(s32[2]{0:T(128)S(1)} %copy-done.1, bf16[8,384,128]{2,1,0:T(8,128)(2,1)} %all-to-all-done.4.a, bf16[8,2,32,3072]{3,2,1,0:T(8,128)(2,1)} %bitcast.32, bf16[8,2,32,3072]{3,2,1,0:T(8,128)(2,1)S(1)} %collective-permute-done.18.other, ...), custom_call_target="tpu_custom_call" | custom-call | tf_op jit(solution)/shard_map/result_rows/pallas_call | solution.py:26
  (66 shorter events, 24.4 us)
Async XLA Ops:
  7.2 54.8 %all-gather.5.cloned.1.call-start = ((), (), s32[]{:S(2)}) async-start(), calls=%async_computation.6 | async-start | bytes 1622016 | tf_op jit(solution)/shard_map/all_gather | solution.py:491
  9.0 5.0 %collective-permute-start.1 = (bf16[32,1664]{1,0:T(8,128)(2,1)}, bf16[32,1664]{1,0:T(8,128)(2,1)S(1)}, u32[]{:S(2)}, u32[]{:S(2)}) collective-permute-start(bf16[32,1664]{1,0:T(8,128)(2,1)} %get-tuple-element.52), channel_id=1, source_target_pairs={{0,132},{132,0},{4,128},{128,4},{1,133},{133,1},{5,129},{129,5},{2... | collective-permute-start | bytes 319496 | tf_op jit(solution)/shard_map/ppermute | solution.py:433
  14.8 30.7 %all-to-all-start = ((bf16[8,128,1024]{2,1,0:T(8,128)(2,1)}), bf16[8,128,1024]{2,1,0:T(8,128)(2,1)S(1)}, u32[]{:S(2)}, u32[]{:S(2)}) async-start(bf16[8,128,1024]{2,1,0:T(8,128)(2,1)} %first_norm.1), calls=%async_computation | async-start | bytes 4194304 | tf_op jit(solution)/shard_map/all_to_all | solution.py:492
  21.7 4.0 %collective-permute-start.2 = (bf16[2,32,256]{2,1,0:T(8,128)(2,1)S(1)}, bf16[2,32,256]{2,1,0:T(8,128)(2,1)S(1)}, u32[]{:S(2)}, u32[]{:S(2)}) collective-permute-start(bf16[2,32,256]{2,1,0:T(8,128)(2,1)S(1)} %get-tuple-element.99), channel_id=1, source_target_pairs={{0,16},{16,0},{32,48},{48,32},{64,80},{80,64},{96,112},{112,96},{1... | collective-permute-start | bytes 98312 | tf_op jit(solution)/shard_map/ppermute | solution.py:437
  25.7 7.9 %collective-permute-start.3 = (bf16[2,2,32,256]{3,2,1,0:T(8,128)(2,1)S(1)}, bf16[2,2,32,256]{3,2,1,0:T(8,128)(2,1)S(1)}, u32[]{:S(2)}, u32[]{:S(2)}) collective-permute-start(bf16[2,2,32,256]{3,2,1,0:T(8,128)(2,1)S(1)} %pad_maximum_fusion.2), channel_id=1, source_target_pairs={{0,32},{16,48},{32,0},{48,16},{64,96},{80,112},{96,64},{112,80},{1... | collective-permute-start | bytes 196616 | tf_op jit(solution)/shard_map/ppermute | solution.py:437
  28.2 11.8 %collective-permute-start.4 = (bf16[2,2,32,256]{3,2,1,0:T(8,128)(2,1)S(1)}, bf16[2,2,32,256]{3,2,1,0:T(8,128)(2,1)S(1)}, u32[]{:S(2)}, u32[]{:S(2)}) collective-permute-start(bf16[2,2,32,256]{3,2,1,0:T(8,128)(2,1)S(1)} %pad_maximum_fusion.2), channel_id=1, source_target_pairs={{0,64},{16,80},{32,96},{48,112},{64,0},{80,16},{96,32},{112,48},{1... | collective-permute-start | bytes 196616 | tf_op jit(solution)/shard_map/ppermute | solution.py:437
  33.6 7.8 %collective-permute-start.5 = (bf16[2,2,32,256]{3,2,1,0:T(8,128)(2,1)S(1)}, bf16[2,2,32,256]{3,2,1,0:T(8,128)(2,1)S(1)}, u32[]{:S(2)}, u32[]{:S(2)}) collective-permute-start(bf16[2,2,32,256]{3,2,1,0:T(8,128)(2,1)S(1)} %pad_maximum_fusion.2), channel_id=1, source_target_pairs={{0,96},{16,112},{32,64},{48,80},{64,32},{80,48},{96,0},{112,16},{1... | collective-permute-start | bytes 196616 | tf_op jit(solution)/shard_map/ppermute | solution.py:437
  41.4 3.6 %collective-permute-start.6 = (bf16[8,2,32,256]{3,2,1,0:T(8,128)(2,1)S(1)}, bf16[8,2,32,256]{3,2,1,0:T(8,128)(2,1)S(1)}, u32[]{:S(2)}, u32[]{:S(2)}) collective-permute-start(bf16[8,2,32,256]{3,2,1,0:T(8,128)(2,1)S(1)} %constant_dynamic-update-slice_fusion.wm), channel_id=1, source_target_pairs={{0,8},{8,0},{1,9},{9,1},{2,10},{10,2},{3,11},{11,3},{4,12},{12,4},... | collective-permute-start | bytes 786440 | tf_op jit(solution)/shard_map/ppermute | solution.py:429
  43.1 12.7 %collective-permute-start = (bf16[32,3072]{1,0:T(8,128)(2,1)}, bf16[32,3072]{1,0:T(8,128)(2,1)S(1)}, u32[]{:S(2)}, u32[]{:S(2)}) collective-permute-start(bf16[32,3072]{1,0:T(8,128)(2,1)} %pack.1), channel_id=1, source_target_pairs={{0,132},{132,0},{4,128},{128,4},{1,133},{133,1},{5,129},{129,5},{2... | collective-permute-start | bytes 589832 | tf_op jit(solution)/shard_map/ppermute | solution.py:433
  49.4 12.6 %all-to-all-start.1 = ((bf16[8,2,64,128]{3,2,1,0:T(8,128)(2,1)}), bf16[8,2,64,128]{3,2,1,0:T(8,128)(2,1)S(1)}, u32[]{:S(2)}, u32[]{:S(2)}) async-start(bf16[8,2,64,128]{3,2,1,0:T(8,128)(2,1)} %get-tuple-element.56), calls=%async_computation.1 | async-start | bytes 524288 | tf_op jit(solution)/shard_map/all_to_all | solution.py:528
  55.8 67.0 %all-gather.7.cloned.1.call-start = ((), (), s32[]{:S(2)}) async-start(), calls=%async_computation.7 | async-start | bytes 3538944 | tf_op jit(solution)/shard_map/all_gather | solution.py:532
  62.7 3.5 %collective-permute-start.7 = (bf16[8,2,32,1408]{3,2,1,0:T(8,128)(2,1)}, bf16[8,2,32,1408]{3,2,1,0:T(8,128)(2,1)S(1)}, u32[]{:S(2)}, u32[]{:S(2)}) collective-permute-start(bf16[8,2,32,1408]{3,2,1,0:T(8,128)(2,1)} %bitcast.28), channel_id=1, source_target_pairs={{0,8},{8,0},{1,9},{9,1},{2,10},{10,2},{3,11},{11,3},{4,12},{12,4},... | collective-permute-start | bytes 4325384 | tf_op jit(solution)/shard_map/ppermute | solution.py:429
  82.7 31.4 %all-to-all-start.3 = ((bf16[8,128,1024]{2,1,0:T(8,128)(2,1)}), bf16[8,128,1024]{2,1,0:T(8,128)(2,1)}, u32[]{:S(2)}, u32[]{:S(2)}) async-start(bf16[8,128,1024]{2,1,0:T(8,128)(2,1)} %get-tuple-element.63), calls=%async_computation.3 | async-start | bytes 4194304 | tf_op jit(solution)/shard_map/all_to_all | solution.py:562
  98.2 10.1 %collective-permute-start.10 = (bf16[2,96,128]{2,1,0:T(8,128)(2,1)}, bf16[2,96,128]{2,1,0:T(8,128)(2,1)S(1)}, u32[]{:S(2)}, u32[]{:S(2)}) collective-permute-start(bf16[2,96,128]{2,1,0:T(8,128)(2,1)} %get-tuple-element.70), channel_id=1, source_target_pairs={{0,16},{16,0},{32,48},{48,32},{64,80},{80,64},{96,112},{112,96},{1... | collective-permute-start | bytes 147464 | tf_op jit(solution)/shard_map/ppermute | solution.py:437
  100.3 12.3 %collective-permute-start.11 = (bf16[2,96,128]{2,1,0:T(8,128)(2,1)}, bf16[2,96,128]{2,1,0:T(8,128)(2,1)S(1)}, u32[]{:S(2)}, u32[]{:S(2)}) collective-permute-start(bf16[2,96,128]{2,1,0:T(8,128)(2,1)} %get-tuple-element.71), channel_id=1, source_target_pairs={{0,32},{16,48},{32,0},{48,16},{64,96},{80,112},{96,64},{112,80},{1... | collective-permute-start | bytes 147464 | tf_op jit(solution)/shard_map/ppermute | solution.py:437
  101.6 19.9 %collective-permute-start.12 = (bf16[2,96,128]{2,1,0:T(8,128)(2,1)}, bf16[2,96,128]{2,1,0:T(8,128)(2,1)S(1)}, u32[]{:S(2)}, u32[]{:S(2)}) collective-permute-start(bf16[2,96,128]{2,1,0:T(8,128)(2,1)} %get-tuple-element.77), channel_id=1, source_target_pairs={{0,48},{16,32},{32,16},{48,0},{64,112},{80,96},{96,80},{112,64},{1... | collective-permute-start | bytes 147464 | tf_op jit(solution)/shard_map/ppermute | solution.py:437
  102.7 18.7 %collective-permute-start.13 = (bf16[2,96,128]{2,1,0:T(8,128)(2,1)}, bf16[2,96,128]{2,1,0:T(8,128)(2,1)S(1)}, u32[]{:S(2)}, u32[]{:S(2)}) collective-permute-start(bf16[2,96,128]{2,1,0:T(8,128)(2,1)} %get-tuple-element.78), channel_id=1, source_target_pairs={{0,64},{16,80},{32,96},{48,112},{64,0},{80,16},{96,32},{112,48},{1... | collective-permute-start | bytes 147464 | tf_op jit(solution)/shard_map/ppermute | solution.py:437
  108.0 13.5 %collective-permute-start.14 = (bf16[2,96,128]{2,1,0:T(8,128)(2,1)}, bf16[2,96,128]{2,1,0:T(8,128)(2,1)S(1)}, u32[]{:S(2)}, u32[]{:S(2)}) collective-permute-start(bf16[2,96,128]{2,1,0:T(8,128)(2,1)} %get-tuple-element.79), channel_id=1, source_target_pairs={{0,80},{16,64},{32,112},{48,96},{64,16},{80,0},{96,48},{112,32},{1... | collective-permute-start | bytes 147464 | tf_op jit(solution)/shard_map/ppermute | solution.py:437
  108.2 13.2 %collective-permute-start.15 = (bf16[2,96,128]{2,1,0:T(8,128)(2,1)}, bf16[2,96,128]{2,1,0:T(8,128)(2,1)S(1)}, u32[]{:S(2)}, u32[]{:S(2)}) collective-permute-start(bf16[2,96,128]{2,1,0:T(8,128)(2,1)} %get-tuple-element.80), channel_id=1, source_target_pairs={{0,96},{16,112},{32,64},{48,80},{64,32},{80,48},{96,0},{112,16},{1... | collective-permute-start | bytes 147464 | tf_op jit(solution)/shard_map/ppermute | solution.py:437
  112.6 8.9 %collective-permute-start.16 = (bf16[2,96,128]{2,1,0:T(8,128)(2,1)}, bf16[2,96,128]{2,1,0:T(8,128)(2,1)S(1)}, u32[]{:S(2)}, u32[]{:S(2)}) collective-permute-start(bf16[2,96,128]{2,1,0:T(8,128)(2,1)} %get-tuple-element.81), channel_id=1, source_target_pairs={{0,112},{16,96},{32,80},{48,64},{64,48},{80,32},{96,16},{112,0},{1... | collective-permute-start | bytes 147464 | tf_op jit(solution)/shard_map/ppermute | solution.py:437
  122.8 25.3 %collective-permute-start.18 = (bf16[8,2,32,3072]{3,2,1,0:T(8,128)(2,1)}, bf16[8,2,32,3072]{3,2,1,0:T(8,128)(2,1)S(1)}, u32[]{:S(2)}, u32[]{:S(2)}) collective-permute-start(bf16[8,2,32,3072]{3,2,1,0:T(8,128)(2,1)} %bitcast.31), channel_id=1, source_target_pairs={{0,8},{8,0},{1,9},{9,1},{2,10},{10,2},{3,11},{11,3},{4,12},{12,4},... | collective-permute-start | bytes 9437192 | tf_op jit(solution)/shard_map/ppermute | solution.py:429
  123.1 20.2 %all-to-all-start.4 = ((bf16[8,384,128]{2,1,0:T(8,128)(2,1)}), bf16[8,384,128]{2,1,0:T(8,128)(2,1)}, u32[]{:S(2)}, u32[]{:S(2)}) async-start(bf16[8,384,128]{2,1,0:T(8,128)(2,1)} %heads.1), calls=%async_computation.4 | async-start | bytes 1572864 | tf_op jit(solution)/shard_map/all_to_all | solution.py:641
  131.1 4.0 %collective-permute-start.17 = (bf16[96,128]{1,0:T(8,128)(2,1)}, bf16[96,128]{1,0:T(8,128)(2,1)S(1)}, u32[]{:S(2)}, u32[]{:S(2)}) collective-permute-start(bf16[96,128]{1,0:T(8,128)(2,1)} %get-tuple-element.85), channel_id=1, source_target_pairs={{0,132},{132,0},{4,128},{128,4},{1,133},{133,1},{5,129},{129,5},{2... | collective-permute-start | bytes 73736 | tf_op jit(solution)/shard_map/ppermute | solution.py:433
  143.3 12.2 %all-to-all-start.5 = ((bf16[8,2,96,128]{3,2,1,0:T(8,128)(2,1)}), bf16[8,2,96,128]{3,2,1,0:T(8,128)(2,1)S(1)}, u32[]{:S(2)}, u32[]{:S(2)}) async-start(bf16[8,2,96,128]{3,2,1,0:T(8,128)(2,1)} %spread.1), calls=%async_computation.5 | async-start | bytes 786432 | tf_op jit(solution)/shard_map/all_to_all | solution.py:643
  (8 other events, 67.2 us)
Sparse Core Ops, SparseCore 0:
  14.9 45.6 all-gather.4
  62.9 49.0 all-gather.6

commit v6 on v5

--- a/solution.py
+++ b/solution.py
@@ -201,21 +201,21 @@
     normal = centre * inv * gain
     opening = sigmoid(normal)
     swished = (normal * opening).astype(BF)
-    wait(get_go, *get_w2)
+    wait(get_x, get_ga, *get_w2)
     w2 = w2_s[...].reshape(model, model)
+    residual = (x_s[...].astype(F32) + dot(swished, w2)).astype(BF)
+    res_s[...] = residual
+    going = [copies.start(res_s, res)]
+    centre_r, inv_r = centred(residual.astype(F32))
+    n_s[...] = (centre_r * inv_r * ga_s[...]).astype(BF)
+    going += [copies.start(n_s, sent.at[i]) for i in range(blocks)]
+    wait(get_go)
     back_two = dot_t(go_s[...], w2)
     slope = opening + normal * opening * (1.0 - opening)
     grad_conv = norm_pull(back_two * slope * gain, centre, inv).astype(BF)
     for i in range(blocks):
         gc_s[i] = grad_conv[:, i * width : (i + 1) * width]
-    going = [copies.start(gc_s, gc)]
-    wait(get_x, get_ga)
-    residual = (x_s[...].astype(F32) + dot(swished, w2)).astype(BF)
-    res_s[...] = residual
-    going.append(copies.start(res_s, res))
-    centre, inv = centred(residual.astype(F32))
-    n_s[...] = (centre * inv * ga_s[...]).astype(BF)
-    wait(*going, *[copies.start(n_s, sent.at[i]) for i in range(blocks)])
+    wait(*going, copies.start(gc_s, gc))
 
 
 def back_body(
@@ -346,7 +346,7 @@
         packed = packed.astype(BF)
         q = packed[:, :width] * jnp.asarray(scaling, BF)
         k = packed[:, width : 2 * width]
-        v = packed[:, 2 * width :]
+        v = jnp.concatenate([packed[:, 2 * width :], jnp.ones((length, width), BF)], 1)
         bias = jnp.where(
             lax.broadcasted_iota(jnp.int32, (1, length), 1) < frames[rec], 0.0, -1e30
         )
@@ -357,9 +357,8 @@
                 here = (lane >= h * head_dim) & (lane < (h + 1) * head_dim)
                 scores = dot_t(jnp.where(here, qr, jnp.zeros_like(qr)), k) + bias
                 top = jnp.max(scores, -1, keepdims=True)
-                numer = jnp.exp(scores - top)
-                denom = jnp.sum(numer, -1, keepdims=True)
-                attended = jnp.where(here, dot(numer.astype(BF), v) / denom, attended)
+                both = dot(jnp.exp(scores - top).astype(BF), v)
+                attended = jnp.where(here, both[:, :width] / both[:, width:], attended)
             got = attended.astype(BF).reshape(rows // local, local, width)
             att_s[r // local : (r + rows) // local, rec * local : (rec + 1) * local] = got
     tall = records * local

time: 166 us -> 164 us (0.988)
  Pallas kernels: 39.5 us -> 37.8 us
    pallas_call x12, Pallas kernels: 39.5 us -> 37.8 us  [run(): pl.pallas_call(body, out_shape=tuple((o[2](o[0], o[1]) for o in outs)), i...]
  transfers between devices with their start and end apart: 26 -> 26, of which waited for: 12 -> 12; matrix products, arithmetic and copies ran while one was open for 1% -> 1% of each run, Pallas kernels for 23% -> 22%
where the time goes in v6:
time: 164 us; the launch traced here: 161 us
  starting transfers between devices  59.7 us (36%)
  Pallas kernels  37.8 us (23%)
  waiting for transfers between devices  35.3 us (22%)
  between operations  14.3 us (9%)
  blocking collectives  11.9 us (7%)
    pallas_call x12, Pallas kernels, run(): pl.pallas_call(body, out_shape=tuple((o[2](o[0], o[1]) for o in outs)), i...  37.8 us
    ppermute x11, starting transfers between devices, pair_z(): lax.ppermute(v, 'z', [(i, i ^ by) for i in range(lax.axis_size('z'))])  23.3 us
    all_to_all x1, blocking collectives, local(): grad_conv = lax.all_to_all(grad_conv, CTX, 0, 0, tiled=True)  11.9 us
    ppermute x11, waiting for transfers between devices, pair_z(): lax.ppermute(v, 'z', [(i, i ^ by) for i in range(lax.axis_size('z'))])  10.7 us
    all_to_all x1, starting transfers between devices, local(): back = lax.all_to_all(back, CTX, 0, 0, tiled=True)  8.02 us
    all_to_all x1, starting transfers between devices, local(): lax.all_to_all(sent, CTX, 0, 0, tiled=True)  6.93 us
    all_to_all x1, waiting for transfers between devices, local(): back = lax.all_to_all(back, CTX, 0, 0, tiled=True)  6.56 us
    all_to_all x1, starting transfers between devices, local(): lax.all_to_all(conv, CTX, 0, 0, tiled=True).reshape(blocks, rows, width)  6.43 us
  transfers between devices with their start and end apart: 26, of which 12 were waited for; matrix products, arithmetic and copies ran while one was open for 1% of the time, Pallas kernels for 22%

profile of v6, /device:TPU:8, one launch (start us, length us, event | category | flops | bytes accessed | tf_op | source)
XLA Modules:
  0.0 161.3 jit_solution(8479751830860393885)
XLA Ops:
  10.7 2.6 %first_norm.1 = bf16[8,128,1024]{2,1,0:T(8,128)(2,1)} custom-call(bf16[128,1024]{1,0:T(8,128)(2,1)} %bitcast.33, f32[1,1024]{1,0:T(1,128)} %bitcast.46), custom_call_target="tpu_custom_call" | custom-call | tf_op jit(solution)/shard_map/first_norm/pallas_call | solution.py:26
  14.8 6.9 %all-to-all-start = ((bf16[8,128,1024]{2,1,0:T(8,128)(2,1)}), bf16[8,128,1024]{2,1,0:T(8,128)(2,1)S(1)}, u32[]{:S(2)}, u32[]{:S(2)}) async-start(bf16[8,128,1024]{2,1,0:T(8,128)(2,1)} %first_norm.1), calls=%async_computation | async-start | bytes 4194304 | tf_op jit(solution)/shard_map/all_to_all | solution.py:491
  22.8 2.9 %collective-permute-done.2 = bf16[2,32,256]{2,1,0:T(8,128)(2,1)S(1)} collective-permute-done((bf16[2,32,256]{2,1,0:T(8,128)(2,1)S(1)}, bf16[2,32,256]{2,1,0:T(8,128)(2,1)S(1)}, u32[]{:S(2)}, u32[]{:S(2)}) %collective-permute-start.2) | collective-permute-done | bytes 32800 | tf_op jit(solution)/shard_map/ppermute | solution.py:436
  25.7 2.5 %collective-permute-start.3 = (bf16[2,2,32,256]{3,2,1,0:T(8,128)(2,1)S(1)}, bf16[2,2,32,256]{3,2,1,0:T(8,128)(2,1)S(1)}, u32[]{:S(2)}, u32[]{:S(2)}) collective-permute-start(bf16[2,2,32,256]{3,2,1,0:T(8,128)(2,1)S(1)} %pad_maximum_fusion.2), channel_id=1, source_target_pairs={{0,32},{16,48},{32,0},{48,16},{64,96},{80,112},{96,64},{112,80},{1... | collective-permute-start | bytes 196616 | tf_op jit(solution)/shard_map/ppermute | solution.py:436
  28.2 5.4 %collective-permute-start.4 = (bf16[2,2,32,256]{3,2,1,0:T(8,128)(2,1)S(1)}, bf16[2,2,32,256]{3,2,1,0:T(8,128)(2,1)S(1)}, u32[]{:S(2)}, u32[]{:S(2)}) collective-permute-start(bf16[2,2,32,256]{3,2,1,0:T(8,128)(2,1)S(1)} %pad_maximum_fusion.2), channel_id=1, source_target_pairs={{0,64},{16,80},{32,96},{48,112},{64,0},{80,16},{96,32},{112,48},{1... | collective-permute-start | bytes 196616 | tf_op jit(solution)/shard_map/ppermute | solution.py:436
  33.6 6.4 %collective-permute-done.4 = bf16[2,2,32,256]{3,2,1,0:T(8,128)(2,1)S(1)} collective-permute-done((bf16[2,2,32,256]{3,2,1,0:T(8,128)(2,1)S(1)}, bf16[2,2,32,256]{3,2,1,0:T(8,128)(2,1)S(1)}, u32[]{:S(2)}, u32[]{:S(2)}) %collective-permute-start.4) | collective-permute-done | bytes 65568 | tf_op jit(solution)/shard_map/ppermute | solution.py:436
  43.1 2.0 %collective-permute-start = (bf16[32,3072]{1,0:T(8,128)(2,1)}, bf16[32,3072]{1,0:T(8,128)(2,1)S(1)}, u32[]{:S(2)}, u32[]{:S(2)}) collective-permute-start(bf16[32,3072]{1,0:T(8,128)(2,1)} %pack.1), channel_id=1, source_target_pairs={{0,132},{132,0},{4,128},{128,4},{1,133},{133,1},{5,129},{129,5},{2... | collective-permute-start | bytes 589832 | tf_op jit(solution)/shard_map/ppermute | solution.py:432
  45.5 3.9 %gate_conv.1 = (bf16[8,2,64,128]{3,2,1,0:T(8,128)(2,1)}, f32[2,512,256]{2,1,0:T(8,128)}, bf16[2,512,128]{2,1,0:T(8,128)(2,1)}) custom-call(s32[2]{0:T(128)S(1)} %copy-done.1, bf16[8,2,64,1024]{3,2,1,0:T(8,128)(2,1)S(1)} %bitcast.26, bf16[8,2,32,256]{3,2,1,0:T(8,128)(2,1)S(1)} %constant_dynamic-update-slice_fusion.wm, ...), custom_call_target="tpu_custom_call" | custom-call | tf_op jit(solution)/shard_map/gate_conv/pallas_call | solution.py:26
  49.4 6.4 %all-to-all-start.1 = ((bf16[8,2,64,128]{3,2,1,0:T(8,128)(2,1)}), bf16[8,2,64,128]{3,2,1,0:T(8,128)(2,1)S(1)}, u32[]{:S(2)}, u32[]{:S(2)}) async-start(bf16[8,2,64,128]{3,2,1,0:T(8,128)(2,1)} %get-tuple-element.56), calls=%async_computation.1 | async-start | bytes 524288 | tf_op jit(solution)/shard_map/all_to_all | solution.py:527
  56.6 5.4 %all-to-all-done.1 = bf16[8,2,64,128]{3,2,1,0:T(8,128)(2,1)S(1)} async-done(((bf16[8,2,64,128]{3,2,1,0:T(8,128)(2,1)}), bf16[8,2,64,128]{3,2,1,0:T(8,128)(2,1)S(1)}, u32[]{:S(2)}, u32[]{:S(2)}) %all-to-all-start.1) | async-done | bytes 262176 | tf_op jit(solution)/shard_map/all_to_all | solution.py:527
  62.8 3.4 %collective-permute-done.7.other = bf16[8,2,32,1408]{3,2,1,0:T(8,128)(2,1)S(1)} collective-permute-done((bf16[8,2,32,1408]{3,2,1,0:T(8,128)(2,1)}, bf16[8,2,32,1408]{3,2,1,0:T(8,128)(2,1)S(1)}, u32[]{:S(2)}, u32[]{:S(2)}) %collective-permute-start.7) | collective-permute-done | bytes 1441824 | tf_op jit(solution)/shard_map/ppermute | solution.py:428
  66.3 4.0 %token_rows.1 = (bf16[8,128,1024]{2,1,0:T(8,128)(2,1)}, bf16[128,1024]{1,0:T(8,128)(2,1)}, bf16[8,128,128]{2,1,0:T(8,128)(2,1)}) custom-call(bf16[8,128,128]{2,1,0:T(8,128)(2,1)} %bitcast.38, bf16[8,2,32,1408]{3,2,1,0:T(8,128)(2,1)} %bitcast.29, bf16[8,2,32,1408]{3,2,1,0:T(8,128)(2,1)S(1)} %collective-permute-done.7.other, bf16[128,1024]{1,0:T(8,128)(2,1)} %bitcast.34, ...), custom_call_target="tpu_custom_call" | custom-call | tf_op jit(solution)/shard_map/token_rows/pallas_call | solution.py:26
  70.2 11.9 %all_to_all.30 = bf16[8,128,128]{2,1,0:T(8,128)(2,1)} all-to-all(bf16[8,128,128]{2,1,0:T(8,128)(2,1)} %get-tuple-element.62), channel_id=1, replica_groups=mesh['yh'=2,'z'=8,'core'=2,'yl'=2,'x'=4] {'yl','x'}, dimensions={0} | all-to-all | bytes 524288 | tf_op jit(solution)/shard_map/all_to_all | solution.py:558
  82.2 5.7 %all-to-all-start.3 = ((bf16[8,128,1024]{2,1,0:T(8,128)(2,1)}), bf16[8,128,1024]{2,1,0:T(8,128)(2,1)}, u32[]{:S(2)}, u32[]{:S(2)}) async-start(bf16[8,128,1024]{2,1,0:T(8,128)(2,1)} %get-tuple-element.63), calls=%async_computation.3 | async-start | bytes 4194304 | tf_op jit(solution)/shard_map/all_to_all | solution.py:561
  87.9 6.0 %conv_back.1 = (bf16[8,384,128]{2,1,0:T(8,128)(2,1)}, bf16[2,8,32,256]{3,2,1,0:T(8,128)(2,1)}, bf16[2,8,32,256]{3,2,1,0:T(8,128)(2,1)}, f32[16,256]{1,0:T(8,128)}) custom-call(s32[2]{0:T(128)S(1)} %copy-done.1, bf16[8,2,64,128]{3,2,1,0:T(8,128)(2,1)} %bitcast.39, bf16[8,2,64,1024]{3,2,1,0:T(8,128)(2,1)S(1)} %bitcast.27, ...), custom_call_target="tpu_custom_call" | custom-call | tf_op jit(solution)/shard_map/conv_back/pallas_call | solution.py:26
  97.7 2.1 %collective-permute-start.10 = (bf16[2,96,128]{2,1,0:T(8,128)(2,1)}, bf16[2,96,128]{2,1,0:T(8,128)(2,1)S(1)}, u32[]{:S(2)}, u32[]{:S(2)}) collective-permute-start(bf16[2,96,128]{2,1,0:T(8,128)(2,1)} %get-tuple-element.70), channel_id=1, source_target_pairs={{0,16},{16,0},{32,48},{48,32},{64,80},{80,64},{96,112},{112,96},{1... | collective-permute-start | bytes 147464 | tf_op jit(solution)/shard_map/ppermute | solution.py:436
  102.2 5.2 %collective-permute-start.13 = (bf16[2,96,128]{2,1,0:T(8,128)(2,1)}, bf16[2,96,128]{2,1,0:T(8,128)(2,1)S(1)}, u32[]{:S(2)}, u32[]{:S(2)}) collective-permute-start(bf16[2,96,128]{2,1,0:T(8,128)(2,1)} %get-tuple-element.78), channel_id=1, source_target_pairs={{0,64},{16,80},{32,96},{48,112},{64,0},{80,16},{96,32},{112,48},{1... | collective-permute-start | bytes 147464 | tf_op jit(solution)/shard_map/ppermute | solution.py:436
  107.7 4.3 %collective-permute-start.15 = (bf16[2,96,128]{2,1,0:T(8,128)(2,1)}, bf16[2,96,128]{2,1,0:T(8,128)(2,1)S(1)}, u32[]{:S(2)}, u32[]{:S(2)}) collective-permute-start(bf16[2,96,128]{2,1,0:T(8,128)(2,1)} %get-tuple-element.80), channel_id=1, source_target_pairs={{0,96},{16,112},{32,64},{48,80},{64,32},{80,48},{96,0},{112,16},{1... | collective-permute-start | bytes 147464 | tf_op jit(solution)/shard_map/ppermute | solution.py:436
  113.6 6.1 %heads.1 = bf16[8,384,128]{2,1,0:T(8,128)(2,1)} custom-call(s32[2]{0:T(128)S(1)} %copy-done.1, bf16[8,2,64,1024]{3,2,1,0:T(8,128)(2,1)} %bitcast.17.x, bf16[8,2,32,1408]{3,2,1,0:T(8,128)(2,1)} %bitcast.30, bf16[8,2,32,1408]{3,2,1,0:T(8,128)(2,1)S(1)} %collective-permute-done.7.other, ...), custom_call_target="tpu_custom_call", output_to_operand_aliasing={{}: (4, {})} | custom-call | tf_op jit(solution)/shard_map/heads/pallas_call | solution.py:26
  121.2 8.0 %all-to-all-start.4 = ((bf16[8,384,128]{2,1,0:T(8,128)(2,1)}), bf16[8,384,128]{2,1,0:T(8,128)(2,1)}, u32[]{:S(2)}, u32[]{:S(2)}) async-start(bf16[8,384,128]{2,1,0:T(8,128)(2,1)} %heads.1), calls=%async_computation.4 | async-start | bytes 1572864 | tf_op jit(solution)/shard_map/all_to_all | solution.py:640
  129.2 4.0 %collective-permute-done.17.recv = bf16[96,128]{1,0:T(8,128)(2,1)S(1)} collective-permute-done((bf16[96,128]{1,0:T(8,128)(2,1)}, bf16[96,128]{1,0:T(8,128)(2,1)S(1)}, u32[]{:S(2)}, u32[]{:S(2)}) %collective-permute-start.17) | collective-permute-done | bytes 24608 | tf_op jit(solution)/shard_map/ppermute | solution.py:432
  134.8 6.6 %all-to-all-done.4.a = bf16[8,384,128]{2,1,0:T(8,128)(2,1)} async-done(((bf16[8,384,128]{2,1,0:T(8,128)(2,1)}), bf16[8,384,128]{2,1,0:T(8,128)(2,1)}, u32[]{:S(2)}, u32[]{:S(2)}) %all-to-all-start.4) | async-done | bytes 786464 | tf_op jit(solution)/shard_map/all_to_all | solution.py:640
  141.4 4.8 %all-to-all-start.5 = ((bf16[8,2,96,128]{3,2,1,0:T(8,128)(2,1)}), bf16[8,2,96,128]{3,2,1,0:T(8,128)(2,1)S(1)}, u32[]{:S(2)}, u32[]{:S(2)}) async-start(bf16[8,2,96,128]{3,2,1,0:T(8,128)(2,1)} %spread.1), calls=%async_computation.5 | async-start | bytes 786432 | tf_op jit(solution)/shard_map/all_to_all | solution.py:642
  146.2 6.2 %result_rows.1 = (bf16[128,1024]{1,0:T(8,128)(2,1)}, bf16[128,1024]{1,0:T(8,128)(2,1)}) custom-call(s32[2]{0:T(128)S(1)} %copy-done.1, bf16[8,384,128]{2,1,0:T(8,128)(2,1)} %all-to-all-done.4.a, bf16[8,2,32,3072]{3,2,1,0:T(8,128)(2,1)} %bitcast.32, bf16[8,2,32,3072]{3,2,1,0:T(8,128)(2,1)S(1)} %collective-permute-done.18.other, ...), custom_call_target="tpu_custom_call" | custom-call | tf_op jit(solution)/shard_map/result_rows/pallas_call | solution.py:26
  (66 shorter events, 24.2 us)
Async XLA Ops:
  7.2 54.8 %all-gather.5.cloned.1.call-start = ((), (), s32[]{:S(2)}) async-start(), calls=%async_computation.6 | async-start | bytes 1622016 | tf_op jit(solution)/shard_map/all_gather | solution.py:490
  9.0 5.0 %collective-permute-start.1 = (bf16[32,1664]{1,0:T(8,128)(2,1)}, bf16[32,1664]{1,0:T(8,128)(2,1)S(1)}, u32[]{:S(2)}, u32[]{:S(2)}) collective-permute-start(bf16[32,1664]{1,0:T(8,128)(2,1)} %get-tuple-element.52), channel_id=1, source_target_pairs={{0,132},{132,0},{4,128},{128,4},{1,133},{133,1},{5,129},{129,5},{2... | collective-permute-start | bytes 319496 | tf_op jit(solution)/shard_map/ppermute | solution.py:432
  14.8 30.7 %all-to-all-start = ((bf16[8,128,1024]{2,1,0:T(8,128)(2,1)}), bf16[8,128,1024]{2,1,0:T(8,128)(2,1)S(1)}, u32[]{:S(2)}, u32[]{:S(2)}) async-start(bf16[8,128,1024]{2,1,0:T(8,128)(2,1)} %first_norm.1), calls=%async_computation | async-start | bytes 4194304 | tf_op jit(solution)/shard_map/all_to_all | solution.py:491
  21.7 4.0 %collective-permute-start.2 = (bf16[2,32,256]{2,1,0:T(8,128)(2,1)S(1)}, bf16[2,32,256]{2,1,0:T(8,128)(2,1)S(1)}, u32[]{:S(2)}, u32[]{:S(2)}) collective-permute-start(bf16[2,32,256]{2,1,0:T(8,128)(2,1)S(1)} %get-tuple-element.99), channel_id=1, source_target_pairs={{0,16},{16,0},{32,48},{48,32},{64,80},{80,64},{96,112},{112,96},{1... | collective-permute-start | bytes 98312 | tf_op jit(solution)/shard_map/ppermute | solution.py:436
  25.7 7.9 %collective-permute-start.3 = (bf16[2,2,32,256]{3,2,1,0:T(8,128)(2,1)S(1)}, bf16[2,2,32,256]{3,2,1,0:T(8,128)(2,1)S(1)}, u32[]{:S(2)}, u32[]{:S(2)}) collective-permute-start(bf16[2,2,32,256]{3,2,1,0:T(8,128)(2,1)S(1)} %pad_maximum_fusion.2), channel_id=1, source_target_pairs={{0,32},{16,48},{32,0},{48,16},{64,96},{80,112},{96,64},{112,80},{1... | collective-permute-start | bytes 196616 | tf_op jit(solution)/shard_map/ppermute | solution.py:436
  28.2 11.8 %collective-permute-start.4 = (bf16[2,2,32,256]{3,2,1,0:T(8,128)(2,1)S(1)}, bf16[2,2,32,256]{3,2,1,0:T(8,128)(2,1)S(1)}, u32[]{:S(2)}, u32[]{:S(2)}) collective-permute-start(bf16[2,2,32,256]{3,2,1,0:T(8,128)(2,1)S(1)} %pad_maximum_fusion.2), channel_id=1, source_target_pairs={{0,64},{16,80},{32,96},{48,112},{64,0},{80,16},{96,32},{112,48},{1... | collective-permute-start | bytes 196616 | tf_op jit(solution)/shard_map/ppermute | solution.py:436
  33.6 7.8 %collective-permute-start.5 = (bf16[2,2,32,256]{3,2,1,0:T(8,128)(2,1)S(1)}, bf16[2,2,32,256]{3,2,1,0:T(8,128)(2,1)S(1)}, u32[]{:S(2)}, u32[]{:S(2)}) collective-permute-start(bf16[2,2,32,256]{3,2,1,0:T(8,128)(2,1)S(1)} %pad_maximum_fusion.2), channel_id=1, source_target_pairs={{0,96},{16,112},{32,64},{48,80},{64,32},{80,48},{96,0},{112,16},{1... | collective-permute-start | bytes 196616 | tf_op jit(solution)/shard_map/ppermute | solution.py:436
  41.4 3.6 %collective-permute-start.6 = (bf16[8,2,32,256]{3,2,1,0:T(8,128)(2,1)S(1)}, bf16[8,2,32,256]{3,2,1,0:T(8,128)(2,1)S(1)}, u32[]{:S(2)}, u32[]{:S(2)}) collective-permute-start(bf16[8,2,32,256]{3,2,1,0:T(8,128)(2,1)S(1)} %constant_dynamic-update-slice_fusion.wm), channel_id=1, source_target_pairs={{0,8},{8,0},{1,9},{9,1},{2,10},{10,2},{3,11},{11,3},{4,12},{12,4},... | collective-permute-start | bytes 786440 | tf_op jit(solution)/shard_map/ppermute | solution.py:428
  43.1 12.7 %collective-permute-start = (bf16[32,3072]{1,0:T(8,128)(2,1)}, bf16[32,3072]{1,0:T(8,128)(2,1)S(1)}, u32[]{:S(2)}, u32[]{:S(2)}) collective-permute-start(bf16[32,3072]{1,0:T(8,128)(2,1)} %pack.1), channel_id=1, source_target_pairs={{0,132},{132,0},{4,128},{128,4},{1,133},{133,1},{5,129},{129,5},{2... | collective-permute-start | bytes 589832 | tf_op jit(solution)/shard_map/ppermute | solution.py:432
  49.4 12.6 %all-to-all-start.1 = ((bf16[8,2,64,128]{3,2,1,0:T(8,128)(2,1)}), bf16[8,2,64,128]{3,2,1,0:T(8,128)(2,1)S(1)}, u32[]{:S(2)}, u32[]{:S(2)}) async-start(bf16[8,2,64,128]{3,2,1,0:T(8,128)(2,1)} %get-tuple-element.56), calls=%async_computation.1 | async-start | bytes 524288 | tf_op jit(solution)/shard_map/all_to_all | solution.py:527
  55.8 65.3 %all-gather.7.cloned.1.call-start = ((), (), s32[]{:S(2)}) async-start(), calls=%async_computation.7 | async-start | bytes 3538944 | tf_op jit(solution)/shard_map/all_gather | solution.py:531
  62.7 3.5 %collective-permute-start.7 = (bf16[8,2,32,1408]{3,2,1,0:T(8,128)(2,1)}, bf16[8,2,32,1408]{3,2,1,0:T(8,128)(2,1)S(1)}, u32[]{:S(2)}, u32[]{:S(2)}) collective-permute-start(bf16[8,2,32,1408]{3,2,1,0:T(8,128)(2,1)} %bitcast.28), channel_id=1, source_target_pairs={{0,8},{8,0},{1,9},{9,1},{2,10},{10,2},{3,11},{11,3},{4,12},{12,4},... | collective-permute-start | bytes 4325384 | tf_op jit(solution)/shard_map/ppermute | solution.py:428
  82.2 31.4 %all-to-all-start.3 = ((bf16[8,128,1024]{2,1,0:T(8,128)(2,1)}), bf16[8,128,1024]{2,1,0:T(8,128)(2,1)}, u32[]{:S(2)}, u32[]{:S(2)}) async-start(bf16[8,128,1024]{2,1,0:T(8,128)(2,1)} %get-tuple-element.63), calls=%async_computation.3 | async-start | bytes 4194304 | tf_op jit(solution)/shard_map/all_to_all | solution.py:561
  97.7 10.1 %collective-permute-start.10 = (bf16[2,96,128]{2,1,0:T(8,128)(2,1)}, bf16[2,96,128]{2,1,0:T(8,128)(2,1)S(1)}, u32[]{:S(2)}, u32[]{:S(2)}) collective-permute-start(bf16[2,96,128]{2,1,0:T(8,128)(2,1)} %get-tuple-element.70), channel_id=1, source_target_pairs={{0,16},{16,0},{32,48},{48,32},{64,80},{80,64},{96,112},{112,96},{1... | collective-permute-start | bytes 147464 | tf_op jit(solution)/shard_map/ppermute | solution.py:436
  99.8 12.3 %collective-permute-start.11 = (bf16[2,96,128]{2,1,0:T(8,128)(2,1)}, bf16[2,96,128]{2,1,0:T(8,128)(2,1)S(1)}, u32[]{:S(2)}, u32[]{:S(2)}) collective-permute-start(bf16[2,96,128]{2,1,0:T(8,128)(2,1)} %get-tuple-element.71), channel_id=1, source_target_pairs={{0,32},{16,48},{32,0},{48,16},{64,96},{80,112},{96,64},{112,80},{1... | collective-permute-start | bytes 147464 | tf_op jit(solution)/shard_map/ppermute | solution.py:436
  101.0 18.7 %collective-permute-start.12 = (bf16[2,96,128]{2,1,0:T(8,128)(2,1)}, bf16[2,96,128]{2,1,0:T(8,128)(2,1)S(1)}, u32[]{:S(2)}, u32[]{:S(2)}) collective-permute-start(bf16[2,96,128]{2,1,0:T(8,128)(2,1)} %get-tuple-element.77), channel_id=1, source_target_pairs={{0,48},{16,32},{32,16},{48,0},{64,112},{80,96},{96,80},{112,64},{1... | collective-permute-start | bytes 147464 | tf_op jit(solution)/shard_map/ppermute | solution.py:436
  102.2 17.5 %collective-permute-start.13 = (bf16[2,96,128]{2,1,0:T(8,128)(2,1)}, bf16[2,96,128]{2,1,0:T(8,128)(2,1)S(1)}, u32[]{:S(2)}, u32[]{:S(2)}) collective-permute-start(bf16[2,96,128]{2,1,0:T(8,128)(2,1)} %get-tuple-element.78), channel_id=1, source_target_pairs={{0,64},{16,80},{32,96},{48,112},{64,0},{80,16},{96,32},{112,48},{1... | collective-permute-start | bytes 147464 | tf_op jit(solution)/shard_map/ppermute | solution.py:436
  107.4 12.3 %collective-permute-start.14 = (bf16[2,96,128]{2,1,0:T(8,128)(2,1)}, bf16[2,96,128]{2,1,0:T(8,128)(2,1)S(1)}, u32[]{:S(2)}, u32[]{:S(2)}) collective-permute-start(bf16[2,96,128]{2,1,0:T(8,128)(2,1)} %get-tuple-element.79), channel_id=1, source_target_pairs={{0,80},{16,64},{32,112},{48,96},{64,16},{80,0},{96,48},{112,32},{1... | collective-permute-start | bytes 147464 | tf_op jit(solution)/shard_map/ppermute | solution.py:436
  107.7 12.0 %collective-permute-start.15 = (bf16[2,96,128]{2,1,0:T(8,128)(2,1)}, bf16[2,96,128]{2,1,0:T(8,128)(2,1)S(1)}, u32[]{:S(2)}, u32[]{:S(2)}) collective-permute-start(bf16[2,96,128]{2,1,0:T(8,128)(2,1)} %get-tuple-element.80), channel_id=1, source_target_pairs={{0,96},{16,112},{32,64},{48,80},{64,32},{80,48},{96,0},{112,16},{1... | collective-permute-start | bytes 147464 | tf_op jit(solution)/shard_map/ppermute | solution.py:436
  112.0 7.7 %collective-permute-start.16 = (bf16[2,96,128]{2,1,0:T(8,128)(2,1)}, bf16[2,96,128]{2,1,0:T(8,128)(2,1)S(1)}, u32[]{:S(2)}, u32[]{:S(2)}) collective-permute-start(bf16[2,96,128]{2,1,0:T(8,128)(2,1)} %get-tuple-element.81), channel_id=1, source_target_pairs={{0,112},{16,96},{32,80},{48,64},{64,48},{80,32},{96,16},{112,0},{1... | collective-permute-start | bytes 147464 | tf_op jit(solution)/shard_map/ppermute | solution.py:436
  121.1 25.1 %collective-permute-start.18 = (bf16[8,2,32,3072]{3,2,1,0:T(8,128)(2,1)}, bf16[8,2,32,3072]{3,2,1,0:T(8,128)(2,1)S(1)}, u32[]{:S(2)}, u32[]{:S(2)}) collective-permute-start(bf16[8,2,32,3072]{3,2,1,0:T(8,128)(2,1)} %bitcast.31), channel_id=1, source_target_pairs={{0,8},{8,0},{1,9},{9,1},{2,10},{10,2},{3,11},{11,3},{4,12},{12,4},... | collective-permute-start | bytes 9437192 | tf_op jit(solution)/shard_map/ppermute | solution.py:428
  121.2 20.2 %all-to-all-start.4 = ((bf16[8,384,128]{2,1,0:T(8,128)(2,1)}), bf16[8,384,128]{2,1,0:T(8,128)(2,1)}, u32[]{:S(2)}, u32[]{:S(2)}) async-start(bf16[8,384,128]{2,1,0:T(8,128)(2,1)} %heads.1), calls=%async_computation.4 | async-start | bytes 1572864 | tf_op jit(solution)/shard_map/all_to_all | solution.py:640
  129.2 4.0 %collective-permute-start.17 = (bf16[96,128]{1,0:T(8,128)(2,1)}, bf16[96,128]{1,0:T(8,128)(2,1)S(1)}, u32[]{:S(2)}, u32[]{:S(2)}) collective-permute-start(bf16[96,128]{1,0:T(8,128)(2,1)} %get-tuple-element.85), channel_id=1, source_target_pairs={{0,132},{132,0},{4,128},{128,4},{1,133},{133,1},{5,129},{129,5},{2... | collective-permute-start | bytes 73736 | tf_op jit(solution)/shard_map/ppermute | solution.py:432
  141.4 12.2 %all-to-all-start.5 = ((bf16[8,2,96,128]{3,2,1,0:T(8,128)(2,1)}), bf16[8,2,96,128]{3,2,1,0:T(8,128)(2,1)S(1)}, u32[]{:S(2)}, u32[]{:S(2)}) async-start(bf16[8,2,96,128]{3,2,1,0:T(8,128)(2,1)} %spread.1), calls=%async_computation.5 | async-start | bytes 786432 | tf_op jit(solution)/shard_map/all_to_all | solution.py:642
  (8 other events, 66.0 us)
Sparse Core Ops, SparseCore 0:
  14.9 45.6 all-gather.4
  62.9 49.4 all-gather.6

commit v7 on v6

--- a/solution.py
+++ b/solution.py
@@ -180,47 +180,52 @@
     wait(*going)
 
 
-def token_body(
-    c, mine, other, x, go, g2, ga, sent, res, gc, c_s, w2_s, x_s, go_s, g2_s, ga_s, n_s, res_s, gc_s, sems
-):
-    rows, model = x_s.shape
+def pull_body(c, mine, other, go, g2, gc, swished, c_s, w2_s, go_s, g2_s, gc_s, sw_s, sems):
+    rows, model = go_s.shape
     blocks = c.shape[0]
     width = model // blocks
     copies = Copies(sems)
     get_c = copies.start(c, c_s)
-    get_w2 = lay_rows(copies, 0, model, mine, other, w2_s)
     get_gain = copies.start(g2, g2_s)
     get_go = copies.start(go, go_s)
-    get_x = copies.start(x, x_s)
-    get_ga = copies.start(ga, ga_s)
-    wait(get_c)
+    get_w2 = lay_rows(copies, 0, model, mine, other, w2_s)
+    wait(get_c, get_gain)
     conv = jnp.concatenate([c_s[i] for i in range(blocks)], 1).astype(F32)
     centre, inv = centred(conv)
-    wait(get_gain)
     gain = g2_s[...]
     normal = centre * inv * gain
     opening = sigmoid(normal)
-    swished = (normal * opening).astype(BF)
-    wait(get_x, get_ga, *get_w2)
-    w2 = w2_s[...].reshape(model, model)
-    residual = (x_s[...].astype(F32) + dot(swished, w2)).astype(BF)
-    res_s[...] = residual
-    going = [copies.start(res_s, res)]
-    centre_r, inv_r = centred(residual.astype(F32))
-    n_s[...] = (centre_r * inv_r * ga_s[...]).astype(BF)
-    going += [copies.start(n_s, sent.at[i]) for i in range(blocks)]
-    wait(get_go)
-    back_two = dot_t(go_s[...], w2)
+    sw_s[...] = (normal * opening).astype(BF)
+    going = [copies.start(sw_s, swished)]
     slope = opening + normal * opening * (1.0 - opening)
+    wait(get_go, *get_w2)
+    back_two = dot_t(go_s[...], w2_s[...].reshape(model, model))
     grad_conv = norm_pull(back_two * slope * gain, centre, inv).astype(BF)
     for i in range(blocks):
         gc_s[i] = grad_conv[:, i * width : (i + 1) * width]
     wait(*going, copies.start(gc_s, gc))
 
 
+def residual_body(swished, mine, other, x, ga, sent, res, sw_s, w2_s, x_s, ga_s, n_s, res_s, sems):
+    model = x_s.shape[1]
+    copies = Copies(sems)
+    get_sw = copies.start(swished, sw_s)
+    get_x = copies.start(x, x_s)
+    get_ga = copies.start(ga, ga_s)
+    get_w2 = lay_rows(copies, 0, model, mine, other, w2_s)
+    wait(get_sw, get_x, get_ga, *get_w2)
+    summed = x_s[...].astype(F32) + dot(sw_s[...], w2_s[...].reshape(model, model))
+    residual = summed.astype(BF)
+    res_s[...] = residual
+    going = [copies.start(res_s, res)]
+    centre, inv = centred(residual.astype(F32))
+    n_s[...] = (centre * inv * ga_s[...]).astype(BF)
+    wait(*going, *[copies.start(n_s, sent.at[i]) for i in range(sent.shape[0])])
+
+
 def back_body(
-    taps, frames, gc, x, hid, gated, k, back, keep, send, gk_out,
-    gc_s, k_s, hid_s, gated_s, pad_s, gpad_s, gh_s, both_s, gf_s, gk_s, out_s, gko_s, sems,
+    taps, frames, gc, x, hid, gated, k, mine, other, back, keep, send, gk_out, wq,
+    gc_s, k_s, hid_s, gated_s, pad_s, gpad_s, gh_s, both_s, gf_s, gk_s, out_s, gko_s, wq_s, sems,
 ):
     blocks, records, local, model = x.shape
     length = blocks * local
@@ -232,6 +237,7 @@
     get_k = copies.start(k.at[:, lanes(ctx_index(), width)], k_s)
     get_gated = copies.start(gated, gated_s)
     get_hid = copies.start(hid, hid_s)
+    get_wq = lay_rows(copies, model, wq_s.shape[4], mine, other, wq_s)
     gk_s[...] = jnp.zeros_like(gk_s)
     zeros = jnp.zeros((16, width), F32)
     for ref in (pad_s, gpad_s):
@@ -280,6 +286,8 @@
             gf_s[...] = grad_first
         else:
             both_s[...] = (gf_s[...] + grad_first).astype(BF)
+    wait(*get_wq)
+    going.append(copies.start(wq_s, wq))
     gk = jnp.sum(gk_s[...], 1)
     half = gko_s.shape[0]
     gko_s[:, :width] = gk[:half]
@@ -330,10 +338,10 @@
     wait(*[copies.start(pair_s, out.at[i]) for i in range(out.shape[0])])
 
 
-def heads_body(head_dim, frames, x, mine, other, held, back, w, att_s, sems):
+def heads_body(head_dim, frames, x, wq, held, back, w, att_s, sems):
     del held
     copies = Copies(sems)
-    get_w = lay_rows(copies, x.shape[3], w.shape[4], mine, other, w)
+    get_w = [copies.start(wq, w)]
     blocks, records, local, model = x.shape
     length = blocks * local
     width = model // blocks
@@ -485,7 +493,7 @@
         [((rows, model), BF), ((1, model), F32), ((rows, model), BF)],
         blocks + 2,
     )
-    beside, sent = barrier((beside, sent))
+    beside, _ = barrier((beside, sent))
     shard_a = jnp.stack([own, beside[:, :part]])
     all_a = lax.all_gather(shard_a, "z", axis=0, tiled=False)
     normed = lax.all_to_all(sent, CTX, 0, 0, tiled=True).reshape(blocks, records, local_len, model)
@@ -530,30 +538,36 @@
     shard_b, all_a = barrier((shard_b, all_a))
     all_b = lax.all_gather(shard_b, "z", axis=0, tiled=False)
 
-    sent, residual, grad_conv = run(
-        token_body,
-        [
-            ((blocks, rows, model), BF, HBM),
-            ((rows, model), BF, HBM),
-            ((blocks, rows, width), BF, HBM),
-        ],
-        [
-            (conv_rows, HBM), (all_a, HBM), (other_a, ANY), (x, HBM), (cot, HBM), (gains[1], HBM),
-            (gains[2], HBM),
-        ],
-        "token_rows",
+    w2_shape = (2, zs, 2, depth, model)
+    grad_conv, swished = run(
+        pull_body,
+        [((blocks, rows, width), BF, HBM), ((rows, model), BF, HBM)],
+        [(conv_rows, HBM), (all_a, HBM), (other_a, ANY), (cot, HBM), (gains[1], HBM)],
+        "token_pull",
         [
             ((blocks, rows, width), BF),
-            ((2, zs, 2, depth, model), BF),
-            ((rows, model), BF),
+            (w2_shape, BF),
             ((rows, model), BF),
             ((1, model), F32),
+            ((blocks, rows, width), BF),
+            ((rows, model), BF),
+        ],
+        9,
+    )
+    sent, residual = run(
+        residual_body,
+        [((blocks, rows, model), BF, HBM), ((rows, model), BF, HBM)],
+        [(swished, HBM), (all_a, HBM), (other_a, ANY), (x, HBM), (gains[2], HBM)],
+        "token_residual",
+        [
+            ((rows, model), BF),
+            (w2_shape, BF),
+            ((rows, model), BF),
             ((1, model), F32),
             ((rows, model), BF),
             ((rows, model), BF),
-            ((blocks, rows, width), BF),
-        ],
-        blocks + 11,
+        ],
+        blocks + 8,
     )
     grad_conv = lax.all_to_all(grad_conv, CTX, 0, 0, tiled=True)
     sent, grad_conv = barrier((sent, grad_conv))
@@ -563,17 +577,18 @@
 
     tall = depth + 16
     half_share = (2, zs, depth, 2 * width)
-    back, keep, send, gk = run(
+    back, keep, send, gk, wq_rows = run(
         functools.partial(back_body, taps),
         [
             ((blocks, 3 * rows, width), BF, HBM),
             (half_share, BF, HBM),
             (half_share, BF, HBM),
             ((16, 2 * width), F32, HBM),
+            ((2, zs, 2, depth, 3 * width), BF, HBM),
         ],
         [
             (frames, SMEM), (grad_conv, HBM), (normed, VMEM), (hidden, HBM), (gated, HBM),
-            (depth_kernel, HBM),
+            (depth_kernel, HBM), (all_a, HBM), (other_a, ANY),
         ],
         "conv_back",
         [
@@ -589,8 +604,9 @@
             ((32, 8, width), F32),
             ((blocks, 2 * rows, width), BF),
             ((16, 2 * width), F32),
-        ],
-        7 + 2 * records,
+            ((2, zs, 2, depth, 3 * width), BF),
+        ],
+        12 + 2 * records,
     )
 
     chunk = (2, 2 * tall, width)
@@ -612,11 +628,11 @@
     (back,) = run(
         functools.partial(heads_body, head_dim),
         [(back.shape, BF, HBM)],
-        [(frames, SMEM), (attn_in, VMEM), (all_a, HBM), (other_a, ANY), (back, HBM)],
+        [(frames, SMEM), (attn_in, VMEM), (wq_rows, HBM), (back, HBM)],
         "heads",
         [((2, zs, 2, depth, 3 * width), BF), ((blocks, rows, width), BF)],
-        5,
-        {4: 0},
+        2,
+        {3: 0},
     )
     keep, send = run(
         sum_body,

time: 164 us -> 163 us (level)
  blocking collectives: 11.9 us -> 0 us
  starting transfers between devices: 59.7 us -> 65.1 us
  Pallas kernels: 37.8 us -> 41.2 us
  waiting for transfers between devices: 35.3 us -> 37.6 us
    all_to_all x1 -> x0, blocking collectives: 11.9 us -> none  [local(): grad_conv = lax.all_to_all(grad_conv, CTX, 0, 0, tiled=True)]
    all_to_all x0 -> x1, starting transfers between devices: none -> 5.43 us  [local(): grad_conv = lax.all_to_all(grad_conv, CTX, 0, 0, tiled=True)]
    pallas_call x12 -> x13, Pallas kernels: 37.8 us -> 41.2 us  [run(): pl.pallas_call(body, out_shape=tuple((o[2](o[0], o[1]) for o in outs)), i...]
    all_to_all x0 -> x1, waiting for transfers between devices: none -> 2.97 us  [local(): grad_conv = lax.all_to_all(grad_conv, CTX, 0, 0, tiled=True)]
  transfers between devices with their start and end apart: 26 -> 27, of which waited for: 12 -> 13; matrix products, arithmetic and copies ran while one was open for 1% -> 1% of each run, Pallas kernels for 22% -> 24%
where the time goes in v7:
time: 163 us; the launch traced here: 160 us
  starting transfers between devices  65.1 us (40%)
  Pallas kernels  41.2 us (25%)
  waiting for transfers between devices  37.6 us (23%)
  between operations  14.3 us (9%)
    pallas_call x13, Pallas kernels, run(): pl.pallas_call(body, out_shape=tuple((o[2](o[0], o[1]) for o in outs)), i...  41.2 us
    ppermute x11, starting transfers between devices, pair_z(): lax.ppermute(v, 'z', [(i, i ^ by) for i in range(lax.axis_size('z'))])  23.4 us
    ppermute x11, waiting for transfers between devices, pair_z(): lax.ppermute(v, 'z', [(i, i ^ by) for i in range(lax.axis_size('z'))])  10.7 us
    all_to_all x1, starting transfers between devices, local(): back = lax.all_to_all(back, CTX, 0, 0, tiled=True)  7.97 us
    all_to_all x1, starting transfers between devices, local(): lax.all_to_all(sent, CTX, 0, 0, tiled=True)  6.93 us
    all_to_all x1, waiting for transfers between devices, local(): back = lax.all_to_all(back, CTX, 0, 0, tiled=True)  6.54 us
    all_to_all x1, starting transfers between devices, local(): lax.all_to_all(conv, CTX, 0, 0, tiled=True).reshape(blocks, rows, width)  6.42 us
    all_to_all x1, starting transfers between devices, local(): attn_in = lax.all_to_all(sent, CTX, 0, 0, tiled=True)  5.74 us
  transfers between devices with their start and end apart: 27, of which 13 were waited for; matrix products, arithmetic and copies ran while one was open for 1% of the time, Pallas kernels for 24%

profile of v7, /device:TPU:8, one launch (start us, length us, event | category | flops | bytes accessed | tf_op | source)
XLA Modules:
  0.0 160.5 jit_solution(18269075833895571793)
XLA Ops:
  10.7 2.6 %first_norm.1 = bf16[8,128,1024]{2,1,0:T(8,128)(2,1)} custom-call(bf16[128,1024]{1,0:T(8,128)(2,1)} %bitcast.34, f32[1,1024]{1,0:T(1,128)} %bitcast.46), custom_call_target="tpu_custom_call" | custom-call | tf_op jit(solution)/shard_map/first_norm/pallas_call | solution.py:26
  14.8 6.9 %all-to-all-start = ((bf16[8,128,1024]{2,1,0:T(8,128)(2,1)}), bf16[8,128,1024]{2,1,0:T(8,128)(2,1)S(1)}, u32[]{:S(2)}, u32[]{:S(2)}) async-start(bf16[8,128,1024]{2,1,0:T(8,128)(2,1)} %first_norm.1), calls=%async_computation | async-start | bytes 4194304 | tf_op jit(solution)/shard_map/all_to_all | solution.py:499
  22.8 2.9 %collective-permute-done.2 = bf16[2,32,256]{2,1,0:T(8,128)(2,1)S(1)} collective-permute-done((bf16[2,32,256]{2,1,0:T(8,128)(2,1)S(1)}, bf16[2,32,256]{2,1,0:T(8,128)(2,1)S(1)}, u32[]{:S(2)}, u32[]{:S(2)}) %collective-permute-start.2) | collective-permute-done | bytes 32800 | tf_op jit(solution)/shard_map/ppermute | solution.py:444
  25.7 2.5 %collective-permute-start.3 = (bf16[2,2,32,256]{3,2,1,0:T(8,128)(2,1)S(1)}, bf16[2,2,32,256]{3,2,1,0:T(8,128)(2,1)S(1)}, u32[]{:S(2)}, u32[]{:S(2)}) collective-permute-start(bf16[2,2,32,256]{3,2,1,0:T(8,128)(2,1)S(1)} %pad_maximum_fusion.2), channel_id=1, source_target_pairs={{0,32},{16,48},{32,0},{48,16},{64,96},{80,112},{96,64},{112,80},{1... | collective-permute-start | bytes 196616 | tf_op jit(solution)/shard_map/ppermute | solution.py:444
  28.2 5.4 %collective-permute-start.4 = (bf16[2,2,32,256]{3,2,1,0:T(8,128)(2,1)S(1)}, bf16[2,2,32,256]{3,2,1,0:T(8,128)(2,1)S(1)}, u32[]{:S(2)}, u32[]{:S(2)}) collective-permute-start(bf16[2,2,32,256]{3,2,1,0:T(8,128)(2,1)S(1)} %pad_maximum_fusion.2), channel_id=1, source_target_pairs={{0,64},{16,80},{32,96},{48,112},{64,0},{80,16},{96,32},{112,48},{1... | collective-permute-start | bytes 196616 | tf_op jit(solution)/shard_map/ppermute | solution.py:444
  33.6 6.4 %collective-permute-done.4 = bf16[2,2,32,256]{3,2,1,0:T(8,128)(2,1)S(1)} collective-permute-done((bf16[2,2,32,256]{3,2,1,0:T(8,128)(2,1)S(1)}, bf16[2,2,32,256]{3,2,1,0:T(8,128)(2,1)S(1)}, u32[]{:S(2)}, u32[]{:S(2)}) %collective-permute-start.4) | collective-permute-done | bytes 65568 | tf_op jit(solution)/shard_map/ppermute | solution.py:444
  45.5 3.9 %gate_conv.1 = (bf16[8,2,64,128]{3,2,1,0:T(8,128)(2,1)}, f32[2,512,256]{2,1,0:T(8,128)}, bf16[2,512,128]{2,1,0:T(8,128)(2,1)}) custom-call(s32[2]{0:T(128)S(1)} %copy-done.1, bf16[8,2,64,1024]{3,2,1,0:T(8,128)(2,1)S(1)} %bitcast.26, bf16[8,2,32,256]{3,2,1,0:T(8,128)(2,1)S(1)} %constant_dynamic-update-slice_fusion.wm, ...), custom_call_target="tpu_custom_call" | custom-call | tf_op jit(solution)/shard_map/gate_conv/pallas_call | solution.py:26
  49.4 6.4 %all-to-all-start.1 = ((bf16[8,2,64,128]{3,2,1,0:T(8,128)(2,1)}), bf16[8,2,64,128]{3,2,1,0:T(8,128)(2,1)S(1)}, u32[]{:S(2)}, u32[]{:S(2)}) async-start(bf16[8,2,64,128]{3,2,1,0:T(8,128)(2,1)} %get-tuple-element.56), calls=%async_computation.1 | async-start | bytes 524288 | tf_op jit(solution)/shard_map/all_to_all | solution.py:535
  56.6 5.4 %all-to-all-done.1 = bf16[8,2,64,128]{3,2,1,0:T(8,128)(2,1)S(1)} async-done(((bf16[8,2,64,128]{3,2,1,0:T(8,128)(2,1)}), bf16[8,2,64,128]{3,2,1,0:T(8,128)(2,1)S(1)}, u32[]{:S(2)}, u32[]{:S(2)}) %all-to-all-start.1) | async-done | bytes 262176 | tf_op jit(solution)/shard_map/all_to_all | solution.py:535
  62.8 3.4 %collective-permute-done.7.other = bf16[8,2,32,1408]{3,2,1,0:T(8,128)(2,1)S(1)} collective-permute-done((bf16[8,2,32,1408]{3,2,1,0:T(8,128)(2,1)}, bf16[8,2,32,1408]{3,2,1,0:T(8,128)(2,1)S(1)}, u32[]{:S(2)}, u32[]{:S(2)}) %collective-permute-start.7) | collective-permute-done | bytes 1441824 | tf_op jit(solution)/shard_map/ppermute | solution.py:436
  66.2 3.1 %token_pull.1 = (bf16[8,128,128]{2,1,0:T(8,128)(2,1)}, bf16[128,1024]{1,0:T(8,128)(2,1)}) custom-call(bf16[8,128,128]{2,1,0:T(8,128)(2,1)} %bitcast.39, bf16[8,2,32,1408]{3,2,1,0:T(8,128)(2,1)} %bitcast.29, bf16[8,2,32,1408]{3,2,1,0:T(8,128)(2,1)S(1)} %collective-permute-done.7.other, bf16[128,1024]{1,0:T(8,128)(2,1)} %bitcast.37, f32[1,1024]{1,0:T(1,128)} %bitcast.48), custom_call_target="tpu_custom_call" | custom-call | tf_op jit(solution)/shard_map/token_pull/pallas_call | solution.py:26
  69.4 5.4 %all-to-all-start.2 = ((bf16[8,128,128]{2,1,0:T(8,128)(2,1)}), bf16[8,128,128]{2,1,0:T(8,128)(2,1)}, u32[]{:S(2)}, u32[]{:S(2)}) async-start(bf16[8,128,128]{2,1,0:T(8,128)(2,1)} %get-tuple-element.63), calls=%async_computation.2 | async-start | bytes 524288 | tf_op jit(solution)/shard_map/all_to_all | solution.py:572
  74.8 3.5 %token_residual.1 = (bf16[8,128,1024]{2,1,0:T(8,128)(2,1)}, bf16[128,1024]{1,0:T(8,128)(2,1)}) custom-call(bf16[128,1024]{1,0:T(8,128)(2,1)} %get-tuple-element.61.swished, bf16[8,2,32,1408]{3,2,1,0:T(8,128)(2,1)} %bitcast.30, bf16[8,2,32,1408]{3,2,1,0:T(8,128)(2,1)S(1)} %collective-permute-done.7.other, bf16[128,1024]{1,0:T(8,128)(2,1)} %bitcast.35, ...), custom_call_target="tpu_custom_call" | custom-call | tf_op jit(solution)/shard_map/token_residual/pallas_call | solution.py:26
  78.3 3.0 %all-to-all-done.2 = bf16[8,128,128]{2,1,0:T(8,128)(2,1)} async-done(((bf16[8,128,128]{2,1,0:T(8,128)(2,1)}), bf16[8,128,128]{2,1,0:T(8,128)(2,1)}, u32[]{:S(2)}, u32[]{:S(2)}) %all-to-all-start.2) | async-done | bytes 262176 | tf_op jit(solution)/shard_map/all_to_all | solution.py:572
  81.3 5.7 %all-to-all-start.3 = ((bf16[8,128,1024]{2,1,0:T(8,128)(2,1)}), bf16[8,128,1024]{2,1,0:T(8,128)(2,1)}, u32[]{:S(2)}, u32[]{:S(2)}) async-start(bf16[8,128,1024]{2,1,0:T(8,128)(2,1)} %get-tuple-element.64), calls=%async_computation.3 | async-start | bytes 4194304 | tf_op jit(solution)/shard_map/all_to_all | solution.py:575
  87.0 6.7 %conv_back.1 = (bf16[8,384,128]{2,1,0:T(8,128)(2,1)}, bf16[2,8,32,256]{3,2,1,0:T(8,128)(2,1)}, bf16[2,8,32,256]{3,2,1,0:T(8,128)(2,1)}, f32[16,256]{1,0:T(8,128)}, bf16[2,8,2,32,384]{4,3,2,1,0:T(8,128)(2,1)}) custom-call(s32[2]{0:T(128)S(1)} %copy-done.1, bf16[8,2,64,128]{3,2,1,0:T(8,128)(2,1)} %bitcast.18.gc, bf16[8,2,64,1024]{3,2,1,0:T(8,128)(2,1)S(1)} %bitcast.27, ...), custom_call_target="tpu_custom_call" | custom-call | tf_op jit(solution)/shard_map/conv_back/pallas_call | solution.py:26
  102.0 5.2 %collective-permute-start.13 = (bf16[2,96,128]{2,1,0:T(8,128)(2,1)}, bf16[2,96,128]{2,1,0:T(8,128)(2,1)S(1)}, u32[]{:S(2)}, u32[]{:S(2)}) collective-permute-start(bf16[2,96,128]{2,1,0:T(8,128)(2,1)} %get-tuple-element.80), channel_id=1, source_target_pairs={{0,64},{16,80},{32,96},{48,112},{64,0},{80,16},{96,32},{112,48},{1... | collective-permute-start | bytes 147464 | tf_op jit(solution)/shard_map/ppermute | solution.py:444
  107.5 4.3 %collective-permute-start.15 = (bf16[2,96,128]{2,1,0:T(8,128)(2,1)}, bf16[2,96,128]{2,1,0:T(8,128)(2,1)S(1)}, u32[]{:S(2)}, u32[]{:S(2)}) collective-permute-start(bf16[2,96,128]{2,1,0:T(8,128)(2,1)} %get-tuple-element.82), channel_id=1, source_target_pairs={{0,96},{16,112},{32,64},{48,80},{64,32},{80,48},{96,0},{112,16},{1... | collective-permute-start | bytes 147464 | tf_op jit(solution)/shard_map/ppermute | solution.py:444
  112.8 6.2 %heads.1 = bf16[8,384,128]{2,1,0:T(8,128)(2,1)} custom-call(s32[2]{0:T(128)S(1)} %copy-done.1, bf16[8,2,64,1024]{3,2,1,0:T(8,128)(2,1)} %bitcast.17.x, bf16[2,8,2,32,384]{4,3,2,1,0:T(8,128)(2,1)} %get-tuple-element.74.wq, bf16[8,384,128]{2,1,0:T(8,128)(2,1)} %get-tuple-element.75.held), custom_call_target="tpu_custom_call", output_to_operand_aliasing={{}: (3, {})} | custom-call | tf_op jit(solution)/shard_map/heads/pallas_call | solution.py:26
  120.4 8.0 %all-to-all-start.4 = ((bf16[8,384,128]{2,1,0:T(8,128)(2,1)}), bf16[8,384,128]{2,1,0:T(8,128)(2,1)}, u32[]{:S(2)}, u32[]{:S(2)}) async-start(bf16[8,384,128]{2,1,0:T(8,128)(2,1)} %heads.1), calls=%async_computation.4 | async-start | bytes 1572864 | tf_op jit(solution)/shard_map/all_to_all | solution.py:656
  128.4 4.0 %collective-permute-done.17.recv = bf16[96,128]{1,0:T(8,128)(2,1)S(1)} collective-permute-done((bf16[96,128]{1,0:T(8,128)(2,1)}, bf16[96,128]{1,0:T(8,128)(2,1)S(1)}, u32[]{:S(2)}, u32[]{:S(2)}) %collective-permute-start.17) | collective-permute-done | bytes 24608 | tf_op jit(solution)/shard_map/ppermute | solution.py:440
  134.1 6.5 %all-to-all-done.4.a = bf16[8,384,128]{2,1,0:T(8,128)(2,1)} async-done(((bf16[8,384,128]{2,1,0:T(8,128)(2,1)}), bf16[8,384,128]{2,1,0:T(8,128)(2,1)}, u32[]{:S(2)}, u32[]{:S(2)}) %all-to-all-start.4) | async-done | bytes 786464 | tf_op jit(solution)/shard_map/all_to_all | solution.py:656
  140.6 4.8 %all-to-all-start.5 = ((bf16[8,2,96,128]{3,2,1,0:T(8,128)(2,1)}), bf16[8,2,96,128]{3,2,1,0:T(8,128)(2,1)S(1)}, u32[]{:S(2)}, u32[]{:S(2)}) async-start(bf16[8,2,96,128]{3,2,1,0:T(8,128)(2,1)} %spread.1), calls=%async_computation.5 | async-start | bytes 786432 | tf_op jit(solution)/shard_map/all_to_all | solution.py:658
  145.4 6.2 %result_rows.1 = (bf16[128,1024]{1,0:T(8,128)(2,1)}, bf16[128,1024]{1,0:T(8,128)(2,1)}) custom-call(s32[2]{0:T(128)S(1)} %copy-done.1, bf16[8,384,128]{2,1,0:T(8,128)(2,1)} %all-to-all-done.4.a, bf16[8,2,32,3072]{3,2,1,0:T(8,128)(2,1)} %bitcast.33, bf16[8,2,32,3072]{3,2,1,0:T(8,128)(2,1)S(1)} %collective-permute-done.18.other, ...), custom_call_target="tpu_custom_call" | custom-call | tf_op jit(solution)/shard_map/result_rows/pallas_call | solution.py:26
  (68 shorter events, 27.6 us)
Async XLA Ops:
  7.2 54.8 %all-gather.5.cloned.1.call-start = ((), (), s32[]{:S(2)}) async-start(), calls=%async_computation.6 | async-start | bytes 1622016 | tf_op jit(solution)/shard_map/all_gather | solution.py:498
  9.0 5.0 %collective-permute-start.1 = (bf16[32,1664]{1,0:T(8,128)(2,1)}, bf16[32,1664]{1,0:T(8,128)(2,1)S(1)}, u32[]{:S(2)}, u32[]{:S(2)}) collective-permute-start(bf16[32,1664]{1,0:T(8,128)(2,1)} %get-tuple-element.53), channel_id=1, source_target_pairs={{0,132},{132,0},{4,128},{128,4},{1,133},{133,1},{5,129},{129,5},{2... | collective-permute-start | bytes 319496 | tf_op jit(solution)/shard_map/ppermute | solution.py:440
  14.8 30.7 %all-to-all-start = ((bf16[8,128,1024]{2,1,0:T(8,128)(2,1)}), bf16[8,128,1024]{2,1,0:T(8,128)(2,1)S(1)}, u32[]{:S(2)}, u32[]{:S(2)}) async-start(bf16[8,128,1024]{2,1,0:T(8,128)(2,1)} %first_norm.1), calls=%async_computation | async-start | bytes 4194304 | tf_op jit(solution)/shard_map/all_to_all | solution.py:499
  21.7 4.0 %collective-permute-start.2 = (bf16[2,32,256]{2,1,0:T(8,128)(2,1)S(1)}, bf16[2,32,256]{2,1,0:T(8,128)(2,1)S(1)}, u32[]{:S(2)}, u32[]{:S(2)}) collective-permute-start(bf16[2,32,256]{2,1,0:T(8,128)(2,1)S(1)} %get-tuple-element.101), channel_id=1, source_target_pairs={{0,16},{16,0},{32,48},{48,32},{64,80},{80,64},{96,112},{112,96},{1... | collective-permute-start | bytes 98312 | tf_op jit(solution)/shard_map/ppermute | solution.py:444
  25.7 7.9 %collective-permute-start.3 = (bf16[2,2,32,256]{3,2,1,0:T(8,128)(2,1)S(1)}, bf16[2,2,32,256]{3,2,1,0:T(8,128)(2,1)S(1)}, u32[]{:S(2)}, u32[]{:S(2)}) collective-permute-start(bf16[2,2,32,256]{3,2,1,0:T(8,128)(2,1)S(1)} %pad_maximum_fusion.2), channel_id=1, source_target_pairs={{0,32},{16,48},{32,0},{48,16},{64,96},{80,112},{96,64},{112,80},{1... | collective-permute-start | bytes 196616 | tf_op jit(solution)/shard_map/ppermute | solution.py:444
  28.2 11.8 %collective-permute-start.4 = (bf16[2,2,32,256]{3,2,1,0:T(8,128)(2,1)S(1)}, bf16[2,2,32,256]{3,2,1,0:T(8,128)(2,1)S(1)}, u32[]{:S(2)}, u32[]{:S(2)}) collective-permute-start(bf16[2,2,32,256]{3,2,1,0:T(8,128)(2,1)S(1)} %pad_maximum_fusion.2), channel_id=1, source_target_pairs={{0,64},{16,80},{32,96},{48,112},{64,0},{80,16},{96,32},{112,48},{1... | collective-permute-start | bytes 196616 | tf_op jit(solution)/shard_map/ppermute | solution.py:444
  33.6 7.8 %collective-permute-start.5 = (bf16[2,2,32,256]{3,2,1,0:T(8,128)(2,1)S(1)}, bf16[2,2,32,256]{3,2,1,0:T(8,128)(2,1)S(1)}, u32[]{:S(2)}, u32[]{:S(2)}) collective-permute-start(bf16[2,2,32,256]{3,2,1,0:T(8,128)(2,1)S(1)} %pad_maximum_fusion.2), channel_id=1, source_target_pairs={{0,96},{16,112},{32,64},{48,80},{64,32},{80,48},{96,0},{112,16},{1... | collective-permute-start | bytes 196616 | tf_op jit(solution)/shard_map/ppermute | solution.py:444
  41.4 3.6 %collective-permute-start.6 = (bf16[8,2,32,256]{3,2,1,0:T(8,128)(2,1)S(1)}, bf16[8,2,32,256]{3,2,1,0:T(8,128)(2,1)S(1)}, u32[]{:S(2)}, u32[]{:S(2)}) collective-permute-start(bf16[8,2,32,256]{3,2,1,0:T(8,128)(2,1)S(1)} %constant_dynamic-update-slice_fusion.wm), channel_id=1, source_target_pairs={{0,8},{8,0},{1,9},{9,1},{2,10},{10,2},{3,11},{11,3},{4,12},{12,4},... | collective-permute-start | bytes 786440 | tf_op jit(solution)/shard_map/ppermute | solution.py:436
  43.1 12.7 %collective-permute-start = (bf16[32,3072]{1,0:T(8,128)(2,1)}, bf16[32,3072]{1,0:T(8,128)(2,1)S(1)}, u32[]{:S(2)}, u32[]{:S(2)}) collective-permute-start(bf16[32,3072]{1,0:T(8,128)(2,1)} %pack.1), channel_id=1, source_target_pairs={{0,132},{132,0},{4,128},{128,4},{1,133},{133,1},{5,129},{129,5},{2... | collective-permute-start | bytes 589832 | tf_op jit(solution)/shard_map/ppermute | solution.py:440
  49.4 12.6 %all-to-all-start.1 = ((bf16[8,2,64,128]{3,2,1,0:T(8,128)(2,1)}), bf16[8,2,64,128]{3,2,1,0:T(8,128)(2,1)S(1)}, u32[]{:S(2)}, u32[]{:S(2)}) async-start(bf16[8,2,64,128]{3,2,1,0:T(8,128)(2,1)} %get-tuple-element.56), calls=%async_computation.1 | async-start | bytes 524288 | tf_op jit(solution)/shard_map/all_to_all | solution.py:535
  55.8 64.5 %all-gather.7.cloned.1.call-start = ((), (), s32[]{:S(2)}) async-start(), calls=%async_computation.7 | async-start | bytes 3538944 | tf_op jit(solution)/shard_map/all_gather | solution.py:539
  69.4 11.9 %all-to-all-start.2 = ((bf16[8,128,128]{2,1,0:T(8,128)(2,1)}), bf16[8,128,128]{2,1,0:T(8,128)(2,1)}, u32[]{:S(2)}, u32[]{:S(2)}) async-start(bf16[8,128,128]{2,1,0:T(8,128)(2,1)} %get-tuple-element.63), calls=%async_computation.2 | async-start | bytes 524288 | tf_op jit(solution)/shard_map/all_to_all | solution.py:572
  81.3 31.5 %all-to-all-start.3 = ((bf16[8,128,1024]{2,1,0:T(8,128)(2,1)}), bf16[8,128,1024]{2,1,0:T(8,128)(2,1)}, u32[]{:S(2)}, u32[]{:S(2)}) async-start(bf16[8,128,1024]{2,1,0:T(8,128)(2,1)} %get-tuple-element.64), calls=%async_computation.3 | async-start | bytes 4194304 | tf_op jit(solution)/shard_map/all_to_all | solution.py:575
  97.5 10.1 %collective-permute-start.10 = (bf16[2,96,128]{2,1,0:T(8,128)(2,1)}, bf16[2,96,128]{2,1,0:T(8,128)(2,1)S(1)}, u32[]{:S(2)}, u32[]{:S(2)}) collective-permute-start(bf16[2,96,128]{2,1,0:T(8,128)(2,1)} %get-tuple-element.71), channel_id=1, source_target_pairs={{0,16},{16,0},{32,48},{48,32},{64,80},{80,64},{96,112},{112,96},{1... | collective-permute-start | bytes 147464 | tf_op jit(solution)/shard_map/ppermute | solution.py:444
  99.6 12.3 %collective-permute-start.11 = (bf16[2,96,128]{2,1,0:T(8,128)(2,1)}, bf16[2,96,128]{2,1,0:T(8,128)(2,1)S(1)}, u32[]{:S(2)}, u32[]{:S(2)}) collective-permute-start(bf16[2,96,128]{2,1,0:T(8,128)(2,1)} %get-tuple-element.72), channel_id=1, source_target_pairs={{0,32},{16,48},{32,0},{48,16},{64,96},{80,112},{96,64},{112,80},{1... | collective-permute-start | bytes 147464 | tf_op jit(solution)/shard_map/ppermute | solution.py:444
  100.9 18.1 %collective-permute-start.12 = (bf16[2,96,128]{2,1,0:T(8,128)(2,1)}, bf16[2,96,128]{2,1,0:T(8,128)(2,1)S(1)}, u32[]{:S(2)}, u32[]{:S(2)}) collective-permute-start(bf16[2,96,128]{2,1,0:T(8,128)(2,1)} %get-tuple-element.79), channel_id=1, source_target_pairs={{0,48},{16,32},{32,16},{48,0},{64,112},{80,96},{96,80},{112,64},{1... | collective-permute-start | bytes 147464 | tf_op jit(solution)/shard_map/ppermute | solution.py:444
  102.0 16.9 %collective-permute-start.13 = (bf16[2,96,128]{2,1,0:T(8,128)(2,1)}, bf16[2,96,128]{2,1,0:T(8,128)(2,1)S(1)}, u32[]{:S(2)}, u32[]{:S(2)}) collective-permute-start(bf16[2,96,128]{2,1,0:T(8,128)(2,1)} %get-tuple-element.80), channel_id=1, source_target_pairs={{0,64},{16,80},{32,96},{48,112},{64,0},{80,16},{96,32},{112,48},{1... | collective-permute-start | bytes 147464 | tf_op jit(solution)/shard_map/ppermute | solution.py:444
  107.3 11.7 %collective-permute-start.14 = (bf16[2,96,128]{2,1,0:T(8,128)(2,1)}, bf16[2,96,128]{2,1,0:T(8,128)(2,1)S(1)}, u32[]{:S(2)}, u32[]{:S(2)}) collective-permute-start(bf16[2,96,128]{2,1,0:T(8,128)(2,1)} %get-tuple-element.81), channel_id=1, source_target_pairs={{0,80},{16,64},{32,112},{48,96},{64,16},{80,0},{96,48},{112,32},{1... | collective-permute-start | bytes 147464 | tf_op jit(solution)/shard_map/ppermute | solution.py:444
  107.5 11.5 %collective-permute-start.15 = (bf16[2,96,128]{2,1,0:T(8,128)(2,1)}, bf16[2,96,128]{2,1,0:T(8,128)(2,1)S(1)}, u32[]{:S(2)}, u32[]{:S(2)}) collective-permute-start(bf16[2,96,128]{2,1,0:T(8,128)(2,1)} %get-tuple-element.82), channel_id=1, source_target_pairs={{0,96},{16,112},{32,64},{48,80},{64,32},{80,48},{96,0},{112,16},{1... | collective-permute-start | bytes 147464 | tf_op jit(solution)/shard_map/ppermute | solution.py:444
  111.9 7.1 %collective-permute-start.16 = (bf16[2,96,128]{2,1,0:T(8,128)(2,1)}, bf16[2,96,128]{2,1,0:T(8,128)(2,1)S(1)}, u32[]{:S(2)}, u32[]{:S(2)}) collective-permute-start(bf16[2,96,128]{2,1,0:T(8,128)(2,1)} %get-tuple-element.83), channel_id=1, source_target_pairs={{0,112},{16,96},{32,80},{48,64},{64,48},{80,32},{96,16},{112,0},{1... | collective-permute-start | bytes 147464 | tf_op jit(solution)/shard_map/ppermute | solution.py:444
  120.3 25.1 %collective-permute-start.18 = (bf16[8,2,32,3072]{3,2,1,0:T(8,128)(2,1)}, bf16[8,2,32,3072]{3,2,1,0:T(8,128)(2,1)S(1)}, u32[]{:S(2)}, u32[]{:S(2)}) collective-permute-start(bf16[8,2,32,3072]{3,2,1,0:T(8,128)(2,1)} %bitcast.32), channel_id=1, source_target_pairs={{0,8},{8,0},{1,9},{9,1},{2,10},{10,2},{3,11},{11,3},{4,12},{12,4},... | collective-permute-start | bytes 9437192 | tf_op jit(solution)/shard_map/ppermute | solution.py:436
  120.4 20.2 %all-to-all-start.4 = ((bf16[8,384,128]{2,1,0:T(8,128)(2,1)}), bf16[8,384,128]{2,1,0:T(8,128)(2,1)}, u32[]{:S(2)}, u32[]{:S(2)}) async-start(bf16[8,384,128]{2,1,0:T(8,128)(2,1)} %heads.1), calls=%async_computation.4 | async-start | bytes 1572864 | tf_op jit(solution)/shard_map/all_to_all | solution.py:656
  128.4 4.0 %collective-permute-start.17 = (bf16[96,128]{1,0:T(8,128)(2,1)}, bf16[96,128]{1,0:T(8,128)(2,1)S(1)}, u32[]{:S(2)}, u32[]{:S(2)}) collective-permute-start(bf16[96,128]{1,0:T(8,128)(2,1)} %get-tuple-element.87), channel_id=1, source_target_pairs={{0,132},{132,0},{4,128},{128,4},{1,133},{133,1},{5,129},{129,5},{2... | collective-permute-start | bytes 73736 | tf_op jit(solution)/shard_map/ppermute | solution.py:440
  140.6 12.2 %all-to-all-start.5 = ((bf16[8,2,96,128]{3,2,1,0:T(8,128)(2,1)}), bf16[8,2,96,128]{3,2,1,0:T(8,128)(2,1)S(1)}, u32[]{:S(2)}, u32[]{:S(2)}) async-start(bf16[8,2,96,128]{3,2,1,0:T(8,128)(2,1)} %spread.1), calls=%async_computation.5 | async-start | bytes 786432 | tf_op jit(solution)/shard_map/all_to_all | solution.py:658
  (9 other events, 69.6 us)
Sparse Core Ops, SparseCore 0:
  14.9 45.6 all-gather.4
  62.8 49.6 all-gather.6

commit v8 on v7

--- a/solution.py
+++ b/solution.py
@@ -652,9 +652,9 @@
         blocks + 2,
     )
 
+    back = lax.all_to_all(back, CTX, 0, 0, tiled=True)
+    pair, back, all_b = barrier((pair, back, all_b))
     other_b = swap_core(all_b)
-    back = lax.all_to_all(back, CTX, 0, 0, tiled=True)
-    pair, back = barrier((pair, back))
     pair = lax.all_to_all(pair, CTX, 0, 0, tiled=True)
     result, grad_in = run(
         result_body,

time: 163 us -> 163 us (level)
  local copies, waits for them, and re-layouts: 0.76 us -> 2.78 us
  waiting for transfers between devices: 37.6 us -> 35.9 us
    unnamed x15 -> x19, local copies, waits for them, and re-layouts: 0.74 us -> 2.77 us
    all_to_all x1, waiting for transfers between devices: 6.54 us -> 4.69 us  [local(): back = lax.all_to_all(back, CTX, 0, 0, tiled=True)]
  transfers between devices with their start and end apart: 27 -> 27, of which waited for: 13 -> 14; matrix products, arithmetic and copies ran while one was open for 1% -> 1% of each run, Pallas kernels for 24% -> 24%
where the time goes in v8:
time: 163 us; the launch traced here: 160 us
  starting transfers between devices  65 us (40%)
  Pallas kernels  40.6 us (25%)
  waiting for transfers between devices  35.9 us (22%)
  between operations  14.3 us (9%)
  local copies, waits for them, and re-layouts  2.78 us (2%)
    pallas_call x13, Pallas kernels, run(): pl.pallas_call(body, out_shape=tuple((o[2](o[0], o[1]) for o in outs)), i...  40.6 us
    ppermute x11, starting transfers between devices, pair_z(): lax.ppermute(v, 'z', [(i, i ^ by) for i in range(lax.axis_size('z'))])  23.4 us
    ppermute x11, waiting for transfers between devices, pair_z(): lax.ppermute(v, 'z', [(i, i ^ by) for i in range(lax.axis_size('z'))])  10.7 us
    all_to_all x1, starting transfers between devices, local(): back = lax.all_to_all(back, CTX, 0, 0, tiled=True)  7.97 us
    all_to_all x1, starting transfers between devices, local(): lax.all_to_all(sent, CTX, 0, 0, tiled=True)  6.93 us
    all_to_all x1, starting transfers between devices, local(): lax.all_to_all(conv, CTX, 0, 0, tiled=True).reshape(blocks, rows, width)  6.42 us
    all_to_all x1, starting transfers between devices, local(): attn_in = lax.all_to_all(sent, CTX, 0, 0, tiled=True)  5.73 us
    ppermute x5, waiting for transfers between devices, swap_core(): return lax.ppermute(v, 'core', [(0, 1), (1, 0)])  5.71 us
  transfers between devices with their start and end apart: 27, of which 14 were waited for; matrix products, arithmetic and copies ran while one was open for 1% of the time, Pallas kernels for 24%

profile of v8, /device:TPU:8, one launch (start us, length us, event | category | flops | bytes accessed | tf_op | source)
XLA Modules:
  0.0 160.2 jit_solution(10640274421142159736)
XLA Ops:
  10.7 2.6 %first_norm.1 = bf16[8,128,1024]{2,1,0:T(8,128)(2,1)} custom-call(bf16[128,1024]{1,0:T(8,128)(2,1)} %bitcast.34, f32[1,1024]{1,0:T(1,128)} %bitcast.46), custom_call_target="tpu_custom_call" | custom-call | tf_op jit(solution)/shard_map/first_norm/pallas_call | solution.py:26
  14.8 6.9 %all-to-all-start = ((bf16[8,128,1024]{2,1,0:T(8,128)(2,1)}), bf16[8,128,1024]{2,1,0:T(8,128)(2,1)S(1)}, u32[]{:S(2)}, u32[]{:S(2)}) async-start(bf16[8,128,1024]{2,1,0:T(8,128)(2,1)} %first_norm.1), calls=%async_computation | async-start | bytes 4194304 | tf_op jit(solution)/shard_map/all_to_all | solution.py:499
  22.9 2.9 %collective-permute-done.2 = bf16[2,32,256]{2,1,0:T(8,128)(2,1)S(1)} collective-permute-done((bf16[2,32,256]{2,1,0:T(8,128)(2,1)S(1)}, bf16[2,32,256]{2,1,0:T(8,128)(2,1)S(1)}, u32[]{:S(2)}, u32[]{:S(2)}) %collective-permute-start.2) | collective-permute-done | bytes 32800 | tf_op jit(solution)/shard_map/ppermute | solution.py:444
  25.8 2.5 %collective-permute-start.3 = (bf16[2,2,32,256]{3,2,1,0:T(8,128)(2,1)S(1)}, bf16[2,2,32,256]{3,2,1,0:T(8,128)(2,1)S(1)}, u32[]{:S(2)}, u32[]{:S(2)}) collective-permute-start(bf16[2,2,32,256]{3,2,1,0:T(8,128)(2,1)S(1)} %pad_maximum_fusion.2), channel_id=1, source_target_pairs={{0,32},{16,48},{32,0},{48,16},{64,96},{80,112},{96,64},{112,80},{1... | collective-permute-start | bytes 196616 | tf_op jit(solution)/shard_map/ppermute | solution.py:444
  28.2 5.4 %collective-permute-start.4 = (bf16[2,2,32,256]{3,2,1,0:T(8,128)(2,1)S(1)}, bf16[2,2,32,256]{3,2,1,0:T(8,128)(2,1)S(1)}, u32[]{:S(2)}, u32[]{:S(2)}) collective-permute-start(bf16[2,2,32,256]{3,2,1,0:T(8,128)(2,1)S(1)} %pad_maximum_fusion.2), channel_id=1, source_target_pairs={{0,64},{16,80},{32,96},{48,112},{64,0},{80,16},{96,32},{112,48},{1... | collective-permute-start | bytes 196616 | tf_op jit(solution)/shard_map/ppermute | solution.py:444
  33.6 6.4 %collective-permute-done.4 = bf16[2,2,32,256]{3,2,1,0:T(8,128)(2,1)S(1)} collective-permute-done((bf16[2,2,32,256]{3,2,1,0:T(8,128)(2,1)S(1)}, bf16[2,2,32,256]{3,2,1,0:T(8,128)(2,1)S(1)}, u32[]{:S(2)}, u32[]{:S(2)}) %collective-permute-start.4) | collective-permute-done | bytes 65568 | tf_op jit(solution)/shard_map/ppermute | solution.py:444
  45.5 3.9 %gate_conv.1 = (bf16[8,2,64,128]{3,2,1,0:T(8,128)(2,1)}, f32[2,512,256]{2,1,0:T(8,128)}, bf16[2,512,128]{2,1,0:T(8,128)(2,1)}) custom-call(s32[2]{0:T(128)S(1)} %copy-done.3, bf16[8,2,64,1024]{3,2,1,0:T(8,128)(2,1)S(1)} %bitcast.26, bf16[8,2,32,256]{3,2,1,0:T(8,128)(2,1)S(1)} %constant_dynamic-update-slice_fusion.wm, ...), custom_call_target="tpu_custom_call" | custom-call | tf_op jit(solution)/shard_map/gate_conv/pallas_call | solution.py:26
  49.4 6.4 %all-to-all-start.1 = ((bf16[8,2,64,128]{3,2,1,0:T(8,128)(2,1)}), bf16[8,2,64,128]{3,2,1,0:T(8,128)(2,1)S(1)}, u32[]{:S(2)}, u32[]{:S(2)}) async-start(bf16[8,2,64,128]{3,2,1,0:T(8,128)(2,1)} %get-tuple-element.57), calls=%async_computation.1 | async-start | bytes 524288 | tf_op jit(solution)/shard_map/all_to_all | solution.py:535
  56.6 5.4 %all-to-all-done.1 = bf16[8,2,64,128]{3,2,1,0:T(8,128)(2,1)S(1)} async-done(((bf16[8,2,64,128]{3,2,1,0:T(8,128)(2,1)}), bf16[8,2,64,128]{3,2,1,0:T(8,128)(2,1)S(1)}, u32[]{:S(2)}, u32[]{:S(2)}) %all-to-all-start.1) | async-done | bytes 262176 | tf_op jit(solution)/shard_map/all_to_all | solution.py:535
  62.8 3.4 %collective-permute-done.7.other = bf16[8,2,32,1408]{3,2,1,0:T(8,128)(2,1)S(1)} collective-permute-done((bf16[8,2,32,1408]{3,2,1,0:T(8,128)(2,1)}, bf16[8,2,32,1408]{3,2,1,0:T(8,128)(2,1)S(1)}, u32[]{:S(2)}, u32[]{:S(2)}) %collective-permute-start.7) | collective-permute-done | bytes 1441824 | tf_op jit(solution)/shard_map/ppermute | solution.py:436
  66.3 3.1 %token_pull.1 = (bf16[8,128,128]{2,1,0:T(8,128)(2,1)}, bf16[128,1024]{1,0:T(8,128)(2,1)}) custom-call(bf16[8,128,128]{2,1,0:T(8,128)(2,1)} %bitcast.39, bf16[8,2,32,1408]{3,2,1,0:T(8,128)(2,1)} %bitcast.29, bf16[8,2,32,1408]{3,2,1,0:T(8,128)(2,1)S(1)} %collective-permute-done.7.other, bf16[128,1024]{1,0:T(8,128)(2,1)} %bitcast.37, f32[1,1024]{1,0:T(1,128)} %bitcast.48), custom_call_target="tpu_custom_call" | custom-call | tf_op jit(solution)/shard_map/token_pull/pallas_call | solution.py:26
  69.4 5.4 %all-to-all-start.2 = ((bf16[8,128,128]{2,1,0:T(8,128)(2,1)}), bf16[8,128,128]{2,1,0:T(8,128)(2,1)}, u32[]{:S(2)}, u32[]{:S(2)}) async-start(bf16[8,128,128]{2,1,0:T(8,128)(2,1)} %get-tuple-element.64), calls=%async_computation.2 | async-start | bytes 524288 | tf_op jit(solution)/shard_map/all_to_all | solution.py:572
  74.8 3.5 %token_residual.1 = (bf16[8,128,1024]{2,1,0:T(8,128)(2,1)}, bf16[128,1024]{1,0:T(8,128)(2,1)}) custom-call(bf16[128,1024]{1,0:T(8,128)(2,1)} %get-tuple-element.62.swished, bf16[8,2,32,1408]{3,2,1,0:T(8,128)(2,1)} %bitcast.30, bf16[8,2,32,1408]{3,2,1,0:T(8,128)(2,1)S(1)} %collective-permute-done.7.other, bf16[128,1024]{1,0:T(8,128)(2,1)} %bitcast.35, ...), custom_call_target="tpu_custom_call" | custom-call | tf_op jit(solution)/shard_map/token_residual/pallas_call | solution.py:26
  78.3 3.0 %all-to-all-done.2 = bf16[8,128,128]{2,1,0:T(8,128)(2,1)} async-done(((bf16[8,128,128]{2,1,0:T(8,128)(2,1)}), bf16[8,128,128]{2,1,0:T(8,128)(2,1)}, u32[]{:S(2)}, u32[]{:S(2)}) %all-to-all-start.2) | async-done | bytes 262176 | tf_op jit(solution)/shard_map/all_to_all | solution.py:572
  81.3 5.7 %all-to-all-start.3 = ((bf16[8,128,1024]{2,1,0:T(8,128)(2,1)}), bf16[8,128,1024]{2,1,0:T(8,128)(2,1)}, u32[]{:S(2)}, u32[]{:S(2)}) async-start(bf16[8,128,1024]{2,1,0:T(8,128)(2,1)} %get-tuple-element.65), calls=%async_computation.3 | async-start | bytes 4194304 | tf_op jit(solution)/shard_map/all_to_all | solution.py:575
  87.0 6.7 %conv_back.1 = (bf16[8,384,128]{2,1,0:T(8,128)(2,1)}, bf16[2,8,32,256]{3,2,1,0:T(8,128)(2,1)}, bf16[2,8,32,256]{3,2,1,0:T(8,128)(2,1)}, f32[16,256]{1,0:T(8,128)}, bf16[2,8,2,32,384]{4,3,2,1,0:T(8,128)(2,1)}) custom-call(s32[2]{0:T(128)S(1)} %copy-done.3, bf16[8,2,64,128]{3,2,1,0:T(8,128)(2,1)} %bitcast.18.gc, bf16[8,2,64,1024]{3,2,1,0:T(8,128)(2,1)S(1)} %bitcast.27, ...), custom_call_target="tpu_custom_call" | custom-call | tf_op jit(solution)/shard_map/conv_back/pallas_call | solution.py:26
  102.1 5.2 %collective-permute-start.13 = (bf16[2,96,128]{2,1,0:T(8,128)(2,1)}, bf16[2,96,128]{2,1,0:T(8,128)(2,1)S(1)}, u32[]{:S(2)}, u32[]{:S(2)}) collective-permute-start(bf16[2,96,128]{2,1,0:T(8,128)(2,1)} %get-tuple-element.81), channel_id=1, source_target_pairs={{0,64},{16,80},{32,96},{48,112},{64,0},{80,16},{96,32},{112,48},{1... | collective-permute-start | bytes 147464 | tf_op jit(solution)/shard_map/ppermute | solution.py:444
  107.6 4.3 %collective-permute-start.15 = (bf16[2,96,128]{2,1,0:T(8,128)(2,1)}, bf16[2,96,128]{2,1,0:T(8,128)(2,1)S(1)}, u32[]{:S(2)}, u32[]{:S(2)}) collective-permute-start(bf16[2,96,128]{2,1,0:T(8,128)(2,1)} %get-tuple-element.83), channel_id=1, source_target_pairs={{0,96},{16,112},{32,64},{48,80},{64,32},{80,48},{96,0},{112,16},{1... | collective-permute-start | bytes 147464 | tf_op jit(solution)/shard_map/ppermute | solution.py:444
  112.8 6.2 %heads.1 = bf16[8,384,128]{2,1,0:T(8,128)(2,1)} custom-call(s32[2]{0:T(128)S(1)} %copy-done.3, bf16[8,2,64,1024]{3,2,1,0:T(8,128)(2,1)} %bitcast.17.x, bf16[2,8,2,32,384]{4,3,2,1,0:T(8,128)(2,1)} %get-tuple-element.75.wq, bf16[8,384,128]{2,1,0:T(8,128)(2,1)} %get-tuple-element.76.held), custom_call_target="tpu_custom_call", output_to_operand_aliasing={{}: (3, {})} | custom-call | tf_op jit(solution)/shard_map/heads/pallas_call | solution.py:26
  120.3 8.0 %all-to-all-start.4 = ((bf16[8,384,128]{2,1,0:T(8,128)(2,1)}), bf16[8,384,128]{2,1,0:T(8,128)(2,1)S(1)}, u32[]{:S(2)}, u32[]{:S(2)}) async-start(bf16[8,384,128]{2,1,0:T(8,128)(2,1)} %heads.1), calls=%async_computation.4 | async-start | bytes 1572864 | tf_op jit(solution)/shard_map/all_to_all | solution.py:655
  128.3 4.0 %collective-permute-done.17.recv = bf16[96,128]{1,0:T(8,128)(2,1)S(1)} collective-permute-done((bf16[96,128]{1,0:T(8,128)(2,1)}, bf16[96,128]{1,0:T(8,128)(2,1)S(1)}, u32[]{:S(2)}, u32[]{:S(2)}) %collective-permute-start.17) | collective-permute-done | bytes 24608 | tf_op jit(solution)/shard_map/ppermute | solution.py:440
  134.0 4.7 %all-to-all-done.4.a = bf16[8,384,128]{2,1,0:T(8,128)(2,1)S(1)} async-done(((bf16[8,384,128]{2,1,0:T(8,128)(2,1)}), bf16[8,384,128]{2,1,0:T(8,128)(2,1)S(1)}, u32[]{:S(2)}, u32[]{:S(2)}) %all-to-all-start.4) | async-done | bytes 786464 | tf_op jit(solution)/shard_map/all_to_all | solution.py:655
  139.5 4.8 %all-to-all-start.5 = ((bf16[8,2,96,128]{3,2,1,0:T(8,128)(2,1)}), bf16[8,2,96,128]{3,2,1,0:T(8,128)(2,1)S(1)}, u32[]{:S(2)}, u32[]{:S(2)}) async-start(bf16[8,2,96,128]{3,2,1,0:T(8,128)(2,1)} %spread.1), calls=%async_computation.5 | async-start | bytes 786432 | tf_op jit(solution)/shard_map/all_to_all | solution.py:658
  146.5 5.6 %result_rows.1 = (bf16[128,1024]{1,0:T(8,128)(2,1)}, bf16[128,1024]{1,0:T(8,128)(2,1)}) custom-call(s32[2]{0:T(128)S(1)} %copy-done.3, bf16[8,384,128]{2,1,0:T(8,128)(2,1)S(1)} %copy-done.1, bf16[8,2,32,3072]{3,2,1,0:T(8,128)(2,1)} %bitcast.33, bf16[8,2,32,3072]{3,2,1,0:T(8,128)(2,1)S(1)} %collective-permute-done.18.other, ...), custom_call_target="tpu_custom_call" | custom-call | tf_op jit(solution)/shard_map/result_rows/pallas_call | solution.py:26
  (72 shorter events, 29.8 us)
Async XLA Ops:
  7.2 54.8 %all-gather.5.cloned.1.call-start = ((), (), s32[]{:S(2)}) async-start(), calls=%async_computation.6 | async-start | bytes 1622016 | tf_op jit(solution)/shard_map/all_gather | solution.py:498
  9.0 5.0 %collective-permute-start.1 = (bf16[32,1664]{1,0:T(8,128)(2,1)}, bf16[32,1664]{1,0:T(8,128)(2,1)S(1)}, u32[]{:S(2)}, u32[]{:S(2)}) collective-permute-start(bf16[32,1664]{1,0:T(8,128)(2,1)} %get-tuple-element.54), channel_id=1, source_target_pairs={{0,132},{132,0},{4,128},{128,4},{1,133},{133,1},{5,129},{129,5},{2... | collective-permute-start | bytes 319496 | tf_op jit(solution)/shard_map/ppermute | solution.py:440
  14.8 30.7 %all-to-all-start = ((bf16[8,128,1024]{2,1,0:T(8,128)(2,1)}), bf16[8,128,1024]{2,1,0:T(8,128)(2,1)S(1)}, u32[]{:S(2)}, u32[]{:S(2)}) async-start(bf16[8,128,1024]{2,1,0:T(8,128)(2,1)} %first_norm.1), calls=%async_computation | async-start | bytes 4194304 | tf_op jit(solution)/shard_map/all_to_all | solution.py:499
  21.7 4.0 %collective-permute-start.2 = (bf16[2,32,256]{2,1,0:T(8,128)(2,1)S(1)}, bf16[2,32,256]{2,1,0:T(8,128)(2,1)S(1)}, u32[]{:S(2)}, u32[]{:S(2)}) collective-permute-start(bf16[2,32,256]{2,1,0:T(8,128)(2,1)S(1)} %get-tuple-element.103), channel_id=1, source_target_pairs={{0,16},{16,0},{32,48},{48,32},{64,80},{80,64},{96,112},{112,96},{1... | collective-permute-start | bytes 98312 | tf_op jit(solution)/shard_map/ppermute | solution.py:444
  25.8 7.9 %collective-permute-start.3 = (bf16[2,2,32,256]{3,2,1,0:T(8,128)(2,1)S(1)}, bf16[2,2,32,256]{3,2,1,0:T(8,128)(2,1)S(1)}, u32[]{:S(2)}, u32[]{:S(2)}) collective-permute-start(bf16[2,2,32,256]{3,2,1,0:T(8,128)(2,1)S(1)} %pad_maximum_fusion.2), channel_id=1, source_target_pairs={{0,32},{16,48},{32,0},{48,16},{64,96},{80,112},{96,64},{112,80},{1... | collective-permute-start | bytes 196616 | tf_op jit(solution)/shard_map/ppermute | solution.py:444
  28.2 11.8 %collective-permute-start.4 = (bf16[2,2,32,256]{3,2,1,0:T(8,128)(2,1)S(1)}, bf16[2,2,32,256]{3,2,1,0:T(8,128)(2,1)S(1)}, u32[]{:S(2)}, u32[]{:S(2)}) collective-permute-start(bf16[2,2,32,256]{3,2,1,0:T(8,128)(2,1)S(1)} %pad_maximum_fusion.2), channel_id=1, source_target_pairs={{0,64},{16,80},{32,96},{48,112},{64,0},{80,16},{96,32},{112,48},{1... | collective-permute-start | bytes 196616 | tf_op jit(solution)/shard_map/ppermute | solution.py:444
  33.6 7.8 %collective-permute-start.5 = (bf16[2,2,32,256]{3,2,1,0:T(8,128)(2,1)S(1)}, bf16[2,2,32,256]{3,2,1,0:T(8,128)(2,1)S(1)}, u32[]{:S(2)}, u32[]{:S(2)}) collective-permute-start(bf16[2,2,32,256]{3,2,1,0:T(8,128)(2,1)S(1)} %pad_maximum_fusion.2), channel_id=1, source_target_pairs={{0,96},{16,112},{32,64},{48,80},{64,32},{80,48},{96,0},{112,16},{1... | collective-permute-start | bytes 196616 | tf_op jit(solution)/shard_map/ppermute | solution.py:444
  41.4 3.6 %collective-permute-start.6 = (bf16[8,2,32,256]{3,2,1,0:T(8,128)(2,1)S(1)}, bf16[8,2,32,256]{3,2,1,0:T(8,128)(2,1)S(1)}, u32[]{:S(2)}, u32[]{:S(2)}) collective-permute-start(bf16[8,2,32,256]{3,2,1,0:T(8,128)(2,1)S(1)} %constant_dynamic-update-slice_fusion.wm), channel_id=1, source_target_pairs={{0,8},{8,0},{1,9},{9,1},{2,10},{10,2},{3,11},{11,3},{4,12},{12,4},... | collective-permute-start | bytes 786440 | tf_op jit(solution)/shard_map/ppermute | solution.py:436
  43.1 12.7 %collective-permute-start = (bf16[32,3072]{1,0:T(8,128)(2,1)}, bf16[32,3072]{1,0:T(8,128)(2,1)S(1)}, u32[]{:S(2)}, u32[]{:S(2)}) collective-permute-start(bf16[32,3072]{1,0:T(8,128)(2,1)} %pack.1), channel_id=1, source_target_pairs={{0,132},{132,0},{4,128},{128,4},{1,133},{133,1},{5,129},{129,5},{2... | collective-permute-start | bytes 589832 | tf_op jit(solution)/shard_map/ppermute | solution.py:440
  49.4 12.6 %all-to-all-start.1 = ((bf16[8,2,64,128]{3,2,1,0:T(8,128)(2,1)}), bf16[8,2,64,128]{3,2,1,0:T(8,128)(2,1)S(1)}, u32[]{:S(2)}, u32[]{:S(2)}) async-start(bf16[8,2,64,128]{3,2,1,0:T(8,128)(2,1)} %get-tuple-element.57), calls=%async_computation.1 | async-start | bytes 524288 | tf_op jit(solution)/shard_map/all_to_all | solution.py:535
  55.8 64.5 %all-gather.7.cloned.1.call-start = ((), (), s32[]{:S(2)}) async-start(), calls=%async_computation.7 | async-start | bytes 3538944 | tf_op jit(solution)/shard_map/all_gather | solution.py:539
  69.4 11.9 %all-to-all-start.2 = ((bf16[8,128,128]{2,1,0:T(8,128)(2,1)}), bf16[8,128,128]{2,1,0:T(8,128)(2,1)}, u32[]{:S(2)}, u32[]{:S(2)}) async-start(bf16[8,128,128]{2,1,0:T(8,128)(2,1)} %get-tuple-element.64), calls=%async_computation.2 | async-start | bytes 524288 | tf_op jit(solution)/shard_map/all_to_all | solution.py:572
  81.3 31.4 %all-to-all-start.3 = ((bf16[8,128,1024]{2,1,0:T(8,128)(2,1)}), bf16[8,128,1024]{2,1,0:T(8,128)(2,1)}, u32[]{:S(2)}, u32[]{:S(2)}) async-start(bf16[8,128,1024]{2,1,0:T(8,128)(2,1)} %get-tuple-element.65), calls=%async_computation.3 | async-start | bytes 4194304 | tf_op jit(solution)/shard_map/all_to_all | solution.py:575
  97.5 10.1 %collective-permute-start.10 = (bf16[2,96,128]{2,1,0:T(8,128)(2,1)}, bf16[2,96,128]{2,1,0:T(8,128)(2,1)S(1)}, u32[]{:S(2)}, u32[]{:S(2)}) collective-permute-start(bf16[2,96,128]{2,1,0:T(8,128)(2,1)} %get-tuple-element.72), channel_id=1, source_target_pairs={{0,16},{16,0},{32,48},{48,32},{64,80},{80,64},{96,112},{112,96},{1... | collective-permute-start | bytes 147464 | tf_op jit(solution)/shard_map/ppermute | solution.py:444
  99.6 12.3 %collective-permute-start.11 = (bf16[2,96,128]{2,1,0:T(8,128)(2,1)}, bf16[2,96,128]{2,1,0:T(8,128)(2,1)S(1)}, u32[]{:S(2)}, u32[]{:S(2)}) collective-permute-start(bf16[2,96,128]{2,1,0:T(8,128)(2,1)} %get-tuple-element.73), channel_id=1, source_target_pairs={{0,32},{16,48},{32,0},{48,16},{64,96},{80,112},{96,64},{112,80},{1... | collective-permute-start | bytes 147464 | tf_op jit(solution)/shard_map/ppermute | solution.py:444
  100.9 18.0 %collective-permute-start.12 = (bf16[2,96,128]{2,1,0:T(8,128)(2,1)}, bf16[2,96,128]{2,1,0:T(8,128)(2,1)S(1)}, u32[]{:S(2)}, u32[]{:S(2)}) collective-permute-start(bf16[2,96,128]{2,1,0:T(8,128)(2,1)} %get-tuple-element.80), channel_id=1, source_target_pairs={{0,48},{16,32},{32,16},{48,0},{64,112},{80,96},{96,80},{112,64},{1... | collective-permute-start | bytes 147464 | tf_op jit(solution)/shard_map/ppermute | solution.py:444
  102.1 16.9 %collective-permute-start.13 = (bf16[2,96,128]{2,1,0:T(8,128)(2,1)}, bf16[2,96,128]{2,1,0:T(8,128)(2,1)S(1)}, u32[]{:S(2)}, u32[]{:S(2)}) collective-permute-start(bf16[2,96,128]{2,1,0:T(8,128)(2,1)} %get-tuple-element.81), channel_id=1, source_target_pairs={{0,64},{16,80},{32,96},{48,112},{64,0},{80,16},{96,32},{112,48},{1... | collective-permute-start | bytes 147464 | tf_op jit(solution)/shard_map/ppermute | solution.py:444
  107.3 11.7 %collective-permute-start.14 = (bf16[2,96,128]{2,1,0:T(8,128)(2,1)}, bf16[2,96,128]{2,1,0:T(8,128)(2,1)S(1)}, u32[]{:S(2)}, u32[]{:S(2)}) collective-permute-start(bf16[2,96,128]{2,1,0:T(8,128)(2,1)} %get-tuple-element.82), channel_id=1, source_target_pairs={{0,80},{16,64},{32,112},{48,96},{64,16},{80,0},{96,48},{112,32},{1... | collective-permute-start | bytes 147464 | tf_op jit(solution)/shard_map/ppermute | solution.py:444
  107.6 11.4 %collective-permute-start.15 = (bf16[2,96,128]{2,1,0:T(8,128)(2,1)}, bf16[2,96,128]{2,1,0:T(8,128)(2,1)S(1)}, u32[]{:S(2)}, u32[]{:S(2)}) collective-permute-start(bf16[2,96,128]{2,1,0:T(8,128)(2,1)} %get-tuple-element.83), channel_id=1, source_target_pairs={{0,96},{16,112},{32,64},{48,80},{64,32},{80,48},{96,0},{112,16},{1... | collective-permute-start | bytes 147464 | tf_op jit(solution)/shard_map/ppermute | solution.py:444
  111.9 7.1 %collective-permute-start.16 = (bf16[2,96,128]{2,1,0:T(8,128)(2,1)}, bf16[2,96,128]{2,1,0:T(8,128)(2,1)S(1)}, u32[]{:S(2)}, u32[]{:S(2)}) collective-permute-start(bf16[2,96,128]{2,1,0:T(8,128)(2,1)} %get-tuple-element.84), channel_id=1, source_target_pairs={{0,112},{16,96},{32,80},{48,64},{64,48},{80,32},{96,16},{112,0},{1... | collective-permute-start | bytes 147464 | tf_op jit(solution)/shard_map/ppermute | solution.py:444
  120.3 18.3 %all-to-all-start.4 = ((bf16[8,384,128]{2,1,0:T(8,128)(2,1)}), bf16[8,384,128]{2,1,0:T(8,128)(2,1)S(1)}, u32[]{:S(2)}, u32[]{:S(2)}) async-start(bf16[8,384,128]{2,1,0:T(8,128)(2,1)} %heads.1), calls=%async_computation.4 | async-start | bytes 1572864 | tf_op jit(solution)/shard_map/all_to_all | solution.py:655
  128.3 4.0 %collective-permute-start.17 = (bf16[96,128]{1,0:T(8,128)(2,1)}, bf16[96,128]{1,0:T(8,128)(2,1)S(1)}, u32[]{:S(2)}, u32[]{:S(2)}) collective-permute-start(bf16[96,128]{1,0:T(8,128)(2,1)} %get-tuple-element.88), channel_id=1, source_target_pairs={{0,132},{132,0},{4,128},{128,4},{1,133},{133,1},{5,129},{129,5},{2... | collective-permute-start | bytes 73736 | tf_op jit(solution)/shard_map/ppermute | solution.py:440
  139.5 5.9 %collective-permute-start.18 = (bf16[8,2,32,3072]{3,2,1,0:T(8,128)(2,1)}, bf16[8,2,32,3072]{3,2,1,0:T(8,128)(2,1)S(1)}, u32[]{:S(2)}, u32[]{:S(2)}) collective-permute-start(bf16[8,2,32,3072]{3,2,1,0:T(8,128)(2,1)} %bitcast.32), channel_id=1, source_target_pairs={{0,8},{8,0},{1,9},{9,1},{2,10},{10,2},{3,11},{11,3},{4,12},{12,4},... | collective-permute-start | bytes 9437192 | tf_op jit(solution)/shard_map/ppermute | solution.py:436
  139.5 13.0 %all-to-all-start.5 = ((bf16[8,2,96,128]{3,2,1,0:T(8,128)(2,1)}), bf16[8,2,96,128]{3,2,1,0:T(8,128)(2,1)S(1)}, u32[]{:S(2)}, u32[]{:S(2)}) async-start(bf16[8,2,96,128]{3,2,1,0:T(8,128)(2,1)} %spread.1), calls=%async_computation.5 | async-start | bytes 786432 | tf_op jit(solution)/shard_map/all_to_all | solution.py:658
  (11 other events, 71.6 us)
Sparse Core Ops, SparseCore 0:
  14.9 45.6 all-gather.4
  62.9 49.6 all-gather.6
